TPU v7x, 128 devices: a whole 4x4x4 slice. The times are simulated.
128 devices in a mesh: dp: 16 (over y, z), seq: 8 (over x, core).
Axes of the slice: x: 4, y: 4, z: 4, core: 2. Of those that a mesh axis runs over, the one named last changes fastest.
Arguments:
- block_input: bfloat16 [16, 8, 256, 1408], P('dp', 'seq'), may hold values from -6 to 6
- norm_gain: float32 [1408], replicated, may hold values from 0.5 to 1.5
- qkv_weight: bfloat16 [1408, 4224], replicated, may hold values from -0.15625 to 0.15625
- frame_clip: int32 [16, 8], P('dp', 'seq'), may hold values from 0 to 2, never falling along the last dimension, each value on 1 to 4 neighbouring positions
- out_grad: bfloat16 [16, 8, 256, 1408], P('dp', 'seq'), may hold values from -6 to 6
Outputs:
- input_grad: bfloat16 [16, 8, 256, 1408], P('dp', 'seq')
- weight_grad: float32 [1408, 1408], P(('dp', 'seq'))
- gain_grad: float32 [1408], replicated
Inputs may be any that keep to these rules, and one draw needn't show every extreme that they name: `frame_clip`: in each group the frames hold clips 0 to 2 in order, each of 1 to 4 frames, one exactly 4.
All inputs are finite; a program needn't handle non-finite values.
Results may differ from a plain program's by a relative error of at most 0.018.
Values may be sent and summed in bfloat16 or wider, within the bound.
No kernel may reach another device: no remote copies, remote signals or barrier semaphores. Data moves between devices by JAX's collectives and lax.ppermute only.
A program may use at most 128 MiB of HBM per device.

v0:
```python
import jax
import jax.numpy as jnp
from jax import lax
from jax.sharding import PartitionSpec as P

HEADS = 16


epsilon = 1e-06


def attention_grad(projected, incoming, same_clip):
    frames_all, positions, triple = projected.shape
    width = triple // 3
    head_dim = width // HEADS
    blocks = projected.reshape(frames_all, positions, 3, HEADS, head_dim)
    query_part = blocks[:, :, 0]
    key_part = blocks[:, :, 1]
    value_part = blocks[:, :, 2]
    outgrad = incoming.reshape(frames_all, positions, HEADS, head_dim)
    scaling = head_dim ** (-0.5)
    scores = (
        jnp.einsum("fphd,gphd->phfg", query_part, key_part, preferred_element_type=jnp.float32)
        * scaling
    )
    largest = jnp.max(jnp.where(same_clip, scores, -jnp.inf), axis=-1, keepdims=True)
    powers = jnp.where(same_clip, jnp.exp(scores - largest), 0.0)
    softmaxed = powers / jnp.sum(powers, axis=-1, keepdims=True)
    rounded_probs = softmaxed.astype(jnp.bfloat16)
    d_value = jnp.einsum(
        "phfg,fphd->gphd", rounded_probs, outgrad, preferred_element_type=jnp.float32
    )
    d_probs = jnp.einsum("fphd,gphd->phfg", outgrad, value_part, preferred_element_type=jnp.float32)
    row_dot = jnp.sum(softmaxed * d_probs, axis=-1, keepdims=True)
    d_scores = (softmaxed * (d_probs - row_dot) * scaling).astype(jnp.bfloat16)
    d_query = jnp.einsum("phfg,gphd->fphd", d_scores, key_part, preferred_element_type=jnp.float32)
    d_key = jnp.einsum("phfg,fphd->gphd", d_scores, query_part, preferred_element_type=jnp.float32)
    stacked = jnp.stack([d_query, d_key, d_value], axis=2)
    return stacked.reshape(frames_all, positions, triple).astype(jnp.bfloat16)


def transpose_product(grad_rows, qkv_weight):
    return lax.dot_general(
        grad_rows, qkv_weight, (((1,), (1,)), ((), ())), preferred_element_type=jnp.float32
    )


def shards(block_input, norm_gain, qkv_weight, frame_clip, out_grad):
    frames_dev = block_input.shape[1]
    patches = block_input.shape[2]
    width = block_input.shape[3]
    seq_count = lax.axis_size("seq")
    group_count = lax.axis_size("dp")
    local_pos = patches // seq_count
    factor = (frames_dev * patches * seq_count * group_count) ** (-0.5)
    inputs_f = block_input[0].astype(jnp.float32)
    centered = inputs_f - jnp.mean(inputs_f, axis=-1, keepdims=True)
    inv_std = lax.rsqrt(jnp.mean(centered * centered, axis=-1, keepdims=True) + epsilon)
    normalized = centered * inv_std
    normed = (normalized * norm_gain).astype(jnp.bfloat16)
    clip_ids = lax.all_gather(frame_clip, "seq", axis=1, tiled=True)[0]
    same_clip = clip_ids[:, None] == clip_ids[None, :]
    grad_split = out_grad[0].reshape(frames_dev, seq_count, local_pos, width)
    projected = jnp.dot(normed.reshape(-1, width), qkv_weight, preferred_element_type=jnp.float32)
    projected = projected.astype(jnp.bfloat16).reshape(frames_dev, seq_count, local_pos, 3 * width)
    moved_proj = lax.all_to_all(projected, "seq", split_axis=1, concat_axis=0, tiled=True)
    incoming = lax.all_to_all(grad_split, "seq", split_axis=1, concat_axis=0, tiled=True)
    grads_frames = attention_grad(moved_proj[:, 0], incoming[:, 0], same_clip)[:, None]
    grads_qkv = lax.all_to_all(grads_frames, "seq", split_axis=0, concat_axis=1, tiled=True)
    rows_x = normed.reshape(-1, width)
    rows_g = grads_qkv.reshape(-1, 3 * width)
    d_normed = transpose_product(rows_g, qkv_weight).reshape(frames_dev, patches, width)
    value_rows = rows_g[:, 2 * width :]
    weight_sum = lax.psum_scatter(
        lax.dot_general(
            rows_x, value_rows, (((0,), (0,)), ((), ())), preferred_element_type=jnp.float32
        ),
        ("dp", "seq"),
        scatter_dimension=0,
        tiled=True,
    )
    gain_local = jnp.sum(d_normed * normalized, axis=(0, 1))
    gain_sum = lax.psum(gain_local, ("dp", "seq"))
    d_hat = d_normed * norm_gain
    first_mean = jnp.mean(d_hat, axis=-1, keepdims=True)
    second_mean = jnp.mean(d_hat * normalized, axis=-1, keepdims=True)
    input_grad = (inv_std * (d_hat - first_mean - normalized * second_mean)).astype(jnp.bfloat16)
    return (input_grad[None], weight_sum * factor, gain_sum * factor)


def solution(mesh):
    placed = (P("dp", "seq", None, None), P(), P(), P("dp", "seq"), P("dp", "seq", None, None))
    return jax.shard_map(
        shards,
        mesh=mesh,
        in_specs=placed,
        out_specs=(P("dp", "seq", None, None), P(("dp", "seq"), None), P()),
        check_vma=False,
    )
```

profile of v0, /device:TPU:1, one launch (start us, length us, event | category | flops | bytes accessed | tf_op | source)
XLA Modules:
  0.0 821.2 jit_solution(1057834231652979656)
XLA Ops:
  0.7 5.9 all-to-all-start.1
  8.3 9.4 %convolution_convert_fusion = bf16[256,4224]{1,0:T(8,128)(2,1)} fusion(bf16[1408,4224]{1,0:T(8,128)(2,1)} %param.7, bf16[1,1,256,1408]{3,2,1,0:T(8,128)(2,1)S(1)} %copy-done, f32[1408]{0:T(1024)S(1)} %copy-done.28, f32[256]{0:T(256)S(1)} %broadcast_multiply_fusion.3, f32[256]{0:T(256)S(1)} %add_rsqrt_fusion), kind=kOutput, calls=%fused_computation.2 | convolution fusion | flops 3047948288 | bytes 14786048 | tf_op jit(solution)/shard_map/dot_general | solution.py:64
  25.4 26.8 %all-reduce = s32[8]{0:T(128)S(1)} all-reduce(s32[8]{0:T(128)S(1)} %bitcast_dynamic-update-slice_fusion), channel_id=1, replica_groups=mesh['dp'=16,'seq'=8] {'seq'}, use_global_device_ids=true, to_apply=%add | all-reduce | flops 8 | bytes 64 | tf_op jit(solution)/shard_map/eq | solution.py:62
  56.2 7.0 reshape_squeeze.9
  66.9 8.0 fusion.45
  82.9 5.2 convert_element_type.63
  88.1 31.9 %all_to_all.12 = bf16[8,1,32,4224]{3,2,1,0:T(8,128)(2,1)S(1)} all-to-all(bf16[8,1,32,4224]{3,2,1,0:T(8,128)(2,1)S(1)} %bitcast.99), channel_id=1, replica_groups=mesh['dp'=16,'seq'=8] {'seq'}, dimensions={0} | all-to-all | bytes 4325376 | tf_op jit(solution)/shard_map/all_to_all | solution.py:69
  126.0 375.6 %fusion = f32[16,1408]{1,0:T(8,128)S(1)} fusion(f32[1408,1408]{1,0:T(8,128)} %fusion.38), kind=kCustom, calls=%all-reduce-scatter | all-reduce-scatter fusion | flops 2883585 | bytes 8019968
  504.1 10.3 %collective-permute-start.1 = (f32[16,1408]{1,0:T(8,128)S(1)}, f32[16,1408]{1,0:T(8,128)S(1)}, u32[]{:S(2)}, u32[]{:S(2)}) collective-permute-start(f32[16,1408]{1,0:T(8,128)S(1)} %fusion), channel_id=1, source_target_pairs={{0,2},{1,3},{2,4},{3,5},{4,6},{5,7},{6,8},{7,9},{8,10},{9,11},{10,... | collective-permute-start | bytes 270344
  514.5 6.1 collective-permute-start.10
  529.1 6.6 collective-permute-start.12
  535.7 5.1 collective-permute-start.13
  540.9 6.2 collective-permute-start.14
  553.4 6.4 collective-permute-start.17
  559.8 4.8 collective-permute-start.18
  571.4 7.6 collective-permute-start.20
  606.2 6.2 collective-permute-start.3
  612.4 7.3 fusion.24
  645.8 13.6 %collective-permute-start.4 = (f32[16,1408]{1,0:T(8,128)S(1)}, f32[16,1408]{1,0:T(8,128)S(1)}, u32[]{:S(2)}, u32[]{:S(2)}) collective-permute-start(f32[16,1408]{1,0:T(8,128)S(1)} %fusion), channel_id=1, source_target_pairs={{0,5},{1,6},{2,7},{3,8},{4,9},{5,10},{6,11},{7,12},{8,13},{9,14},{... | collective-permute-start | bytes 270344
  660.7 66.6 %psum.7 = f32[1408]{0:T(1024)S(1)} all-reduce(f32[1408]{0:T(1024)S(1)} %get-tuple-element.3), channel_id=1, replica_groups=mesh['dp'=16,'seq'=8] {'dp','seq'}, use_global_device_ids=true, to_apply=%region_9.10 | all-reduce | flops 1408 | bytes 11264 | tf_op jit(solution)/shard_map/psum | solution.py:83
  727.3 5.7 collective-permute-start.5
  733.0 10.2 %collective-permute-start.6 = (f32[16,1408]{1,0:T(8,128)S(1)}, f32[16,1408]{1,0:T(8,128)S(1)}, u32[]{:S(2)}, u32[]{:S(2)}) collective-permute-start(f32[16,1408]{1,0:T(8,128)S(1)} %fusion), channel_id=1, source_target_pairs={{0,7},{1,8},{2,9},{3,10},{4,11},{5,12},{6,13},{7,14},{8,15},{9,16}... | collective-permute-start | bytes 270344
  746.6 4.8 collective-permute-start.8
  757.3 62.3 %concatenate = f32[651,1408]{1,0:T(8,128)} concatenate(f32[11,1408]{1,0:T(8,128)S(1)} %collective-permute-done.39, f32[16,1408]{1,0:T(8,128)S(1)} %collective-permute-done.38, f32[16,1408]{1,0:T(8,128)S(1)} %collective-permute-done.37, f32[16,1408]{1,0:T(8,128)S(1)} %collective-permute-done.36, f32[16,1408]{1,0:T(8,128)S(1)} %collective-permute-done.35, ...), dimensions={0} | concatenate | bytes 7332864
  (154 shorter events, 119.5 us)
Async XLA Ops:
  19.0 37.1 %all-to-all-start = ((bf16[1,8,32,4224]{3,2,0,1:T(8,128)(2,1)}), bf16[1,8,32,4224]{3,2,0,1:T(8,128)(2,1)S(1)}, u32[]{:S(2)}, u32[]{:S(2)}) async-start(bf16[1,8,32,4224]{3,2,0,1:T(8,128)(2,1)} %bitcast.102), calls=%async_computation | async-start | bytes 4325376 | tf_op jit(solution)/shard_map/all_to_all | solution.py:66
  501.6 34.1 %collective-permute-start = (f32[16,1408]{1,0:T(8,128)S(1)}, f32[16,1408]{1,0:T(8,128)S(1)}, u32[]{:S(2)}, u32[]{:S(2)}) collective-permute-start(f32[16,1408]{1,0:T(8,128)S(1)} %fusion), channel_id=1, source_target_pairs={{0,1},{1,2},{2,3},{3,4},{4,5},{5,6},{6,7},{7,8},{8,9},{9,10},{10,1... | collective-permute-start | bytes 270344
  504.1 36.7 %collective-permute-start.1 = (f32[16,1408]{1,0:T(8,128)S(1)}, f32[16,1408]{1,0:T(8,128)S(1)}, u32[]{:S(2)}, u32[]{:S(2)}) collective-permute-start(f32[16,1408]{1,0:T(8,128)S(1)} %fusion), channel_id=1, source_target_pairs={{0,2},{1,3},{2,4},{3,5},{4,6},{5,7},{6,8},{7,9},{8,10},{9,11},{10,... | collective-permute-start | bytes 270344
  514.5 32.6 %collective-permute-start.10 = (f32[16,1408]{1,0:T(8,128)S(1)}, f32[16,1408]{1,0:T(8,128)S(1)}, u32[]{:S(2)}, u32[]{:S(2)}) collective-permute-start(f32[16,1408]{1,0:T(8,128)S(1)} %fusion), channel_id=1, source_target_pairs={{0,11},{1,12},{2,13},{3,14},{4,15},{5,16},{6,17},{7,18},{8,19},{9,... | collective-permute-start | bytes 270344
  520.6 30.5 %collective-permute-start.11 = (f32[16,1408]{1,0:T(8,128)S(1)}, f32[16,1408]{1,0:T(8,128)S(1)}, u32[]{:S(2)}, u32[]{:S(2)}) collective-permute-start(f32[16,1408]{1,0:T(8,128)S(1)} %fusion), channel_id=1, source_target_pairs={{0,12},{1,13},{2,14},{3,15},{4,16},{5,17},{6,18},{7,19},{8,20},{9,... | collective-permute-start | bytes 270344
  529.1 24.4 %collective-permute-start.12 = (f32[16,1408]{1,0:T(8,128)S(1)}, f32[16,1408]{1,0:T(8,128)S(1)}, u32[]{:S(2)}, u32[]{:S(2)}) collective-permute-start(f32[16,1408]{1,0:T(8,128)S(1)} %fusion), channel_id=1, source_target_pairs={{0,13},{1,14},{2,15},{3,16},{4,17},{5,18},{6,19},{7,20},{8,21},{9,... | collective-permute-start | bytes 270344
  535.7 24.1 %collective-permute-start.13 = (f32[16,1408]{1,0:T(8,128)S(1)}, f32[16,1408]{1,0:T(8,128)S(1)}, u32[]{:S(2)}, u32[]{:S(2)}) collective-permute-start(f32[16,1408]{1,0:T(8,128)S(1)} %fusion), channel_id=1, source_target_pairs={{0,14},{1,15},{2,16},{3,17},{4,18},{5,19},{6,20},{7,21},{8,22},{9,... | collective-permute-start | bytes 270344
  540.9 23.8 %collective-permute-start.14 = (f32[16,1408]{1,0:T(8,128)S(1)}, f32[16,1408]{1,0:T(8,128)S(1)}, u32[]{:S(2)}, u32[]{:S(2)}) collective-permute-start(f32[16,1408]{1,0:T(8,128)S(1)} %fusion), channel_id=1, source_target_pairs={{0,15},{1,16},{2,17},{3,18},{4,19},{5,20},{6,21},{7,22},{8,23},{9,... | collective-permute-start | bytes 270344
  553.4 25.5 %collective-permute-start.17 = (f32[16,1408]{1,0:T(8,128)S(1)}, f32[16,1408]{1,0:T(8,128)S(1)}, u32[]{:S(2)}, u32[]{:S(2)}) collective-permute-start(f32[16,1408]{1,0:T(8,128)S(1)} %fusion), channel_id=1, source_target_pairs={{0,18},{1,19},{2,20},{3,21},{4,22},{5,23},{6,24},{7,25},{8,26},{9,... | collective-permute-start | bytes 270344
  559.8 23.0 %collective-permute-start.18 = (f32[16,1408]{1,0:T(8,128)S(1)}, f32[16,1408]{1,0:T(8,128)S(1)}, u32[]{:S(2)}, u32[]{:S(2)}) collective-permute-start(f32[16,1408]{1,0:T(8,128)S(1)} %fusion), channel_id=1, source_target_pairs={{0,19},{1,20},{2,21},{3,22},{4,23},{5,24},{6,25},{7,26},{8,27},{9,... | collective-permute-start | bytes 270344
  564.7 22.5 %collective-permute-start.19 = (f32[16,1408]{1,0:T(8,128)S(1)}, f32[16,1408]{1,0:T(8,128)S(1)}, u32[]{:S(2)}, u32[]{:S(2)}) collective-permute-start(f32[16,1408]{1,0:T(8,128)S(1)} %fusion), channel_id=1, source_target_pairs={{0,20},{1,21},{2,22},{3,23},{4,24},{5,25},{6,26},{7,27},{8,28},{9,... | collective-permute-start | bytes 270344
  567.8 23.9 %collective-permute-start.2 = (f32[16,1408]{1,0:T(8,128)S(1)}, f32[16,1408]{1,0:T(8,128)S(1)}, u32[]{:S(2)}, u32[]{:S(2)}) collective-permute-start(f32[16,1408]{1,0:T(8,128)S(1)} %fusion), channel_id=1, source_target_pairs={{0,3},{1,4},{2,5},{3,6},{4,7},{5,8},{6,9},{7,10},{8,11},{9,12},{10... | collective-permute-start | bytes 270344
  571.4 23.3 %collective-permute-start.20 = (f32[16,1408]{1,0:T(8,128)S(1)}, f32[16,1408]{1,0:T(8,128)S(1)}, u32[]{:S(2)}, u32[]{:S(2)}) collective-permute-start(f32[16,1408]{1,0:T(8,128)S(1)} %fusion), channel_id=1, source_target_pairs={{0,21},{1,22},{2,23},{3,24},{4,25},{5,26},{6,27},{7,28},{8,29},{9,... | collective-permute-start | bytes 270344
  599.8 23.7 %collective-permute-start.27 = (f32[16,1408]{1,0:T(8,128)S(1)}, f32[16,1408]{1,0:T(8,128)S(1)}, u32[]{:S(2)}, u32[]{:S(2)}) collective-permute-start(f32[16,1408]{1,0:T(8,128)S(1)} %fusion), channel_id=1, source_target_pairs={{0,28},{1,29},{2,30},{3,31},{4,32},{5,33},{6,34},{7,35},{8,36},{9,... | collective-permute-start | bytes 270344
  603.0 23.7 %collective-permute-start.28 = (f32[16,1408]{1,0:T(8,128)S(1)}, f32[16,1408]{1,0:T(8,128)S(1)}, u32[]{:S(2)}, u32[]{:S(2)}) collective-permute-start(f32[16,1408]{1,0:T(8,128)S(1)} %fusion), channel_id=1, source_target_pairs={{0,29},{1,30},{2,31},{3,32},{4,33},{5,34},{6,35},{7,36},{8,37},{9,... | collective-permute-start | bytes 270344
  604.6 26.2 %collective-permute-start.29 = (f32[16,1408]{1,0:T(8,128)S(1)}, f32[16,1408]{1,0:T(8,128)S(1)}, u32[]{:S(2)}, u32[]{:S(2)}) collective-permute-start(f32[16,1408]{1,0:T(8,128)S(1)} %fusion), channel_id=1, source_target_pairs={{0,30},{1,31},{2,32},{3,33},{4,34},{5,35},{6,36},{7,37},{8,38},{9,... | collective-permute-start | bytes 270344
  606.2 27.1 %collective-permute-start.3 = (f32[16,1408]{1,0:T(8,128)S(1)}, f32[16,1408]{1,0:T(8,128)S(1)}, u32[]{:S(2)}, u32[]{:S(2)}) collective-permute-start(f32[16,1408]{1,0:T(8,128)S(1)} %fusion), channel_id=1, source_target_pairs={{0,4},{1,5},{2,6},{3,7},{4,8},{5,9},{6,10},{7,11},{8,12},{9,13},{1... | collective-permute-start | bytes 270344
  637.1 90.2 %collective-permute-start.35 = (f32[16,1408]{1,0:T(8,128)S(1)}, f32[16,1408]{1,0:T(8,128)S(1)}, u32[]{:S(2)}, u32[]{:S(2)}) collective-permute-start(f32[16,1408]{1,0:T(8,128)S(1)} %fusion), channel_id=1, source_target_pairs={{0,36},{1,37},{2,38},{3,39},{4,40},{5,41},{6,42},{7,43},{8,44},{9,... | collective-permute-start | bytes 270344
  640.9 92.1 %collective-permute-start.36 = (f32[16,1408]{1,0:T(8,128)S(1)}, f32[16,1408]{1,0:T(8,128)S(1)}, u32[]{:S(2)}, u32[]{:S(2)}) collective-permute-start(f32[16,1408]{1,0:T(8,128)S(1)} %fusion), channel_id=1, source_target_pairs={{0,37},{1,38},{2,39},{3,40},{4,41},{5,42},{6,43},{7,44},{8,45},{9,... | collective-permute-start | bytes 270344
  642.8 100.4 %collective-permute-start.37 = (f32[16,1408]{1,0:T(8,128)S(1)}, f32[16,1408]{1,0:T(8,128)S(1)}, u32[]{:S(2)}, u32[]{:S(2)}) collective-permute-start(f32[16,1408]{1,0:T(8,128)S(1)} %fusion), channel_id=1, source_target_pairs={{0,38},{1,39},{2,40},{3,41},{4,42},{5,43},{6,44},{7,45},{8,46},{9,... | collective-permute-start | bytes 270344
  644.4 102.2 %collective-permute-start.38 = (f32[16,1408]{1,0:T(8,128)S(1)}, f32[16,1408]{1,0:T(8,128)S(1)}, u32[]{:S(2)}, u32[]{:S(2)}) collective-permute-start(f32[16,1408]{1,0:T(8,128)S(1)} %fusion), channel_id=1, source_target_pairs={{0,39},{1,40},{2,41},{3,42},{4,43},{5,44},{6,45},{7,46},{8,47},{9,... | collective-permute-start | bytes 270344
  645.8 105.7 %collective-permute-start.4 = (f32[16,1408]{1,0:T(8,128)S(1)}, f32[16,1408]{1,0:T(8,128)S(1)}, u32[]{:S(2)}, u32[]{:S(2)}) collective-permute-start(f32[16,1408]{1,0:T(8,128)S(1)} %fusion), channel_id=1, source_target_pairs={{0,5},{1,6},{2,7},{3,8},{4,9},{5,10},{6,11},{7,12},{8,13},{9,14},{... | collective-permute-start | bytes 270344
  727.3 28.8 %collective-permute-start.5 = (f32[16,1408]{1,0:T(8,128)S(1)}, f32[16,1408]{1,0:T(8,128)S(1)}, u32[]{:S(2)}, u32[]{:S(2)}) collective-permute-start(f32[16,1408]{1,0:T(8,128)S(1)} %fusion), channel_id=1, source_target_pairs={{0,6},{1,7},{2,8},{3,9},{4,10},{5,11},{6,12},{7,13},{8,14},{9,15},... | collective-permute-start | bytes 270344
  733.0 23.1 %collective-permute-start.6 = (f32[16,1408]{1,0:T(8,128)S(1)}, f32[16,1408]{1,0:T(8,128)S(1)}, u32[]{:S(2)}, u32[]{:S(2)}) collective-permute-start(f32[16,1408]{1,0:T(8,128)S(1)} %fusion), channel_id=1, source_target_pairs={{0,7},{1,8},{2,9},{3,10},{4,11},{5,12},{6,13},{7,14},{8,15},{9,16}... | collective-permute-start | bytes 270344
  (48 other events, 2366.2 us)
where the time goes:
time: 829 us; the launch traced here: 821 us
  blocking collectives  501 us (60%)
  starting transfers between devices  186 us (22%)
  local copies, waits for them, and re-layouts  86.7 us (10%)
  matrix products  26.6 us (3%)
  other arithmetic  15 us (2%)
    unnamed x1, blocking collectives  376 us
    unnamed x40, starting transfers between devices  176 us
    psum x1, blocking collectives, shards(): gain_sum = lax.psum(gain_local, ('dp', 'seq'))  66.6 us
    unnamed x65, local copies, waits for them, and re-layouts  66 us
    all_to_all x1, blocking collectives, shards(): lax.all_to_all(grads_frames, 'seq', split_axis=0, concat_axis=1, tiled=True)  31.9 us
    eq x1, blocking collectives, shards(): same_clip = clip_ids[:, None] == clip_ids[None, :]  26.8 us
  transfers between devices with their start and end apart: 42, of which 3 were waited for; matrix products, arithmetic and copies ran while one was open for 3% of the time, Pallas kernels for 0%

commit v1 on v0

v1 whole, which is shorter than its diff:
```python
import jax
import jax.numpy as jnp
from jax import lax
from jax.experimental import pallas as pl
from jax.experimental.pallas import tpu as pltpu
from jax.sharding import PartitionSpec as P

HEADS = 16
HEAD_DIM = 88
D = 1408
TRIPLE = 3 * D
WIN = 256
PADDED = TRIPLE + 128
WIDE = D + 128
ROWS = 256
CHUNK = 32
SLOTS = 8
TILE = 256
BLOCK = 88
HALF = 768
EPSILON = 1e-06
SCALING = HEAD_DIM ** (-0.5)
MASKED = -1e30

BF = jnp.bfloat16
F32 = jnp.float32


def shape(dims, dtype):
    return jax.ShapeDtypeStruct(dims, dtype)


def call(body, outs, scratch=(), in_specs=None, mib=16, flops=0, data=0, name=None):
    extra = {} if in_specs is None else {"in_specs": in_specs}
    return pl.pallas_call(
        body,
        out_shape=outs,
        scratch_shapes=list(scratch),
        compiler_params=pltpu.CompilerParams(vmem_limit_bytes=mib << 20),
        cost_estimate=pl.CostEstimate(flops=flops, bytes_accessed=data, transcendentals=0),
        name=name,
        **extra,
    )


VMEM = pl.BlockSpec(memory_space=pltpu.VMEM)
SMEM = pl.BlockSpec(memory_space=pltpu.SMEM)
HBM = pl.BlockSpec(memory_space=pl.ANY)


def head_window(head):
    first = (head * HEAD_DIM) // 128 * 128
    offset = head * HEAD_DIM - first
    lane = lax.broadcasted_iota(jnp.int32, (1, WIN), 1)
    return first, (lane >= offset) & (lane < offset + HEAD_DIM)


def keep(lanes, values):
    return jnp.where(lanes, values, jnp.zeros_like(values))


def normalize(rows):
    values = rows.astype(F32)
    centered = values - jnp.mean(values, axis=-1, keepdims=True)
    inv_std = lax.rsqrt(jnp.mean(centered * centered, axis=-1, keepdims=True) + EPSILON)
    return centered * inv_std, inv_std


def pack_body(clip_ref, rows_ref, out_ref):
    out_ref[:, pl.ds(0, D)] = rows_ref[...]
    clip = jnp.full((ROWS, 128), clip_ref[0, 0], jnp.int32)
    out_ref[:, pl.ds(D, 128)] = clip.astype(F32).astype(BF)


def split_body(after_ref, rows_ref, *out_refs):
    me = lax.axis_index("seq")
    for k in range(SLOTS):
        start = pl.multiple_of((me ^ k) * CHUNK, CHUNK)
        out_refs[k][...] = rows_ref[pl.ds(start, CHUNK), :]


def join_body(*refs):
    out_ref = refs[SLOTS]
    me = lax.axis_index("seq")
    for k in range(SLOTS):
        start = pl.multiple_of((me ^ k) * CHUNK, CHUNK)
        out_ref[pl.ds(start, CHUNK), :] = refs[k][...]


def norm_body(x_ref, gain_ref, normed_ref):
    normalized, _ = normalize(x_ref[:, pl.ds(0, D)])
    normed_ref[...] = (normalized * gain_ref[...]).astype(BF)


def turn_body(normed_ref, mine_ref, theirs_ref, wide_ref, other_ref):
    core = lax.axis_index("seq") % 2
    for b in range(16):
        block = normed_ref[:, pl.ds(b * BLOCK // 128 * 128, 256 if b < 15 else 128)]
        offset = b * BLOCK % 128
        turned = jnp.transpose(block.astype(F32))[offset : offset + BLOCK]
        slot = lax.axis_index("dp") ^ b
        by_y = slot // 4 * 4 + b % 4
        by_z = slot % 4 * 4 + b // 4
        slot = jnp.where(core == 0, by_y, by_z)
        wide_ref[pl.ds(pl.multiple_of(slot * BLOCK, 8), BLOCK), :] = turned
        slot = jnp.where(core == 0, by_z, by_y)
        other_ref[pl.ds(pl.multiple_of(slot * BLOCK, 8), BLOCK), :] = turned
    mine_ref[...] = wide_ref[...].astype(BF)
    theirs_ref[...] = other_ref[...].astype(BF)


def project_body(x_ref, normed_ref, w_hbm, qkv_ref, soft_ref, prob_ref, wbuf, bias_ref, sems):
    first = [(0, 512), (512, 1152), (1664, 1152)]
    rest = [(2816, 384), (3200, 384), (3584, 384), (3968, 256)]

    def fetch(i, start, count):
        cols = pl.ds(start, count)
        return pltpu.make_async_copy(w_hbm.at[:, cols], wbuf.at[:, cols], sems.at[i])

    def project(i, start, count):
        cols = pl.ds(start, count)
        fetch(i, start, count).wait()
        out = jnp.dot(normed_ref[...], wbuf[:, cols], preferred_element_type=F32)
        qkv_ref[:, cols] = out.astype(BF)

    for i, (start, count) in enumerate(first + rest):
        fetch(i, start, count).start()

    row = lax.broadcasted_iota(jnp.int32, (ROWS, ROWS), 0)
    col = lax.broadcasted_iota(jnp.int32, (ROWS, ROWS), 1)
    clip = x_ref[:, pl.ds(D, 128)].astype(F32)
    clip = jnp.concatenate([clip, clip], axis=1)
    kept = (clip == jnp.transpose(clip)) & (row % CHUNK == col % CHUNK)
    bias_ref[...] = jnp.where(kept, 0.0, MASKED).astype(F32)
    qkv_ref[:, pl.ds(TRIPLE, 128)] = jnp.zeros((ROWS, 128), BF)

    for i, (start, count) in enumerate(first):
        project(i, start, count)

    def attend(head):
        start, lanes = head_window(head)
        query = qkv_ref[:, pl.ds(start, WIN)]
        key = keep(lanes, qkv_ref[:, pl.ds(D + start, WIN)])
        scores = lax.dot_general(key, query, (((1,), (1,)), ((), ())), preferred_element_type=F32)
        scores = scores * SCALING + bias_ref[...]
        powers = jnp.exp(scores - jnp.max(scores, axis=0, keepdims=True))
        softmaxed = powers / jnp.sum(powers, axis=0, keepdims=True)
        soft_ref[head] = softmaxed
        prob_ref[head] = softmaxed.astype(BF)

    qkv_ref[:, pl.ds(2 * D, 128)] = jnp.zeros((ROWS, 128), BF)
    for head in range(HEADS):
        attend(head)
        if head % 4 == 3:
            project(len(first) + head // 4, *rest[head // 4])


def value_body(prob_ref, *refs):
    chunks = refs[:SLOTS]
    dv_ref, mine_ref, theirs_ref, grad_ref, acc_ref = refs[SLOTS:]
    me = lax.axis_index("seq")
    for k in range(SLOTS):
        start = pl.multiple_of((me ^ k) * CHUNK, CHUNK)
        grad_ref[pl.ds(start, CHUNK), pl.ds(0, D)] = chunks[k][...]
    grad_ref[:, pl.ds(D, 128)] = jnp.zeros((ROWS, 128), BF)
    acc_ref[...] = jnp.zeros_like(acc_ref)

    def one(head):
        first, lanes = head_window(head)
        grad = keep(lanes, grad_ref[:, pl.ds(first, WIN)])
        acc_ref[:, pl.ds(first, WIN)] += jnp.dot(prob_ref[head], grad, preferred_element_type=F32)

    for head in range(HEADS):
        one(head)
    dv_ref[...] = acc_ref[:, pl.ds(0, D)].astype(BF)
    core = lax.axis_index("seq") % 2
    lead = D - HALF
    mine_ref[...] = dv_ref[:, pl.ds(pl.multiple_of(core * lead, 128), HALF)]
    theirs_ref[...] = dv_ref[:, pl.ds(pl.multiple_of((1 - core) * lead, 128), HALF)]


def weight_body(nt_ref, nt_other_ref, dv_ref, dv_other_ref, *out_refs):
    for tile in range(HALF // TILE):
        cols = pl.ds(tile * TILE, TILE)
        term = jnp.dot(nt_ref[...], dv_ref[:, cols], preferred_element_type=F32)
        term += jnp.dot(nt_other_ref[...], dv_other_ref[:, cols], preferred_element_type=F32)
        for j in range(4):
            out = out_refs[j]
            out[:, cols] = term[j * 4 * BLOCK : (j + 1) * 4 * BLOCK].astype(out.dtype)


def second_body(*refs):
    parts, gains, out_ref = refs[:4], refs[4:8], refs[8]
    gain = gains[0][...]
    for g in gains[1:]:
        gain = gain + g[...]
    gain = jnp.concatenate([gain, jnp.zeros((1, 2 * HALF - D), F32)], axis=1)
    rest = jnp.concatenate([gain[:, :HALF], gain[:, HALF:]], axis=0)
    total = parts[0][...]
    for part in parts[1:]:
        total = total + part[...].astype(F32)
    for i in range(16):
        rows = jnp.concatenate([total[i * 22 : i * 22 + 22], rest], axis=0)
        out_ref[i] = rows.astype(BF)


def third_body(parts_ref, mine_ref, theirs_ref):
    total = parts_ref[0].astype(F32)
    for i in range(1, 16):
        total = total + parts_ref[i].astype(F32)
    rest = jnp.concatenate([total[22:24], jnp.zeros((3, HALF), F32)], axis=0)
    low = jnp.concatenate([total[:11], rest], axis=0)
    high = jnp.concatenate([total[11:22], rest], axis=0)
    core = lax.axis_index("seq") % 2
    mine_ref[...] = jnp.where(core == 0, low, high)
    theirs_ref[...] = jnp.where(core == 0, high, low)


def last_body(factor):
    def body(mine_ref, other_ref, out_ref, gain_ref):
        core = lax.axis_index("seq") % 2
        mine, other = mine_ref[...] * factor, other_ref[...] * factor
        first = jnp.where(core == 0, mine, other)
        second = jnp.where(core == 0, other, mine)
        gain = (first + second)[11:13]
        out_ref[:, pl.ds(0, HALF)] = first[:11]
        out_ref[:, pl.ds(HALF, D - HALF)] = second[:11, 2 * HALF - D :]
        gain_ref[:, pl.ds(0, HALF)] = gain[0:1]
        gain_ref[:, pl.ds(HALF, D - HALF)] = gain[1:2, : D - HALF]

    return body


def input_body(*refs):
    x_ref, qkv_ref, soft_ref, grad_ref, dv_ref, gain_ref, w_hbm = refs[:7]
    outs, gain_out = refs[7 : 7 + SLOTS], refs[7 + SLOTS]
    wbuf, dq_ref, dk_ref, g_ref, dn_ref, sems = refs[8 + SLOTS :]
    tiles = [(0, 512), (512, 512), (1024, 384)]
    parts = [pl.ds(2 * D, D), pl.ds(0, 2 * D)]

    def fetch(part, i):
        at = pl.ds(*tiles[i]), parts[part]
        return pltpu.make_async_copy(w_hbm.at[at], wbuf.at[at], sems.at[part, i])

    for part in range(2):
        for i in range(len(tiles)):
            fetch(part, i).start()
    dq_ref[...] = jnp.zeros_like(dq_ref)
    dk_ref[...] = jnp.zeros_like(dk_ref)
    across = (((1,), (1,)), ((), ()))

    def one(head):
        first, lanes = head_window(head)
        query = keep(lanes, qkv_ref[:, pl.ds(first, WIN)])
        key = keep(lanes, qkv_ref[:, pl.ds(D + first, WIN)])
        value = keep(lanes, qkv_ref[:, pl.ds(2 * D + first, WIN)])
        grad = grad_ref[:, pl.ds(first, WIN)]
        d_probs = lax.dot_general(value, grad, across, preferred_element_type=F32)
        softmaxed = soft_ref[head]
        row_dot = jnp.sum(softmaxed * d_probs, axis=0, keepdims=True)
        d_scores = (softmaxed * (d_probs - row_dot) * SCALING).astype(BF)
        dk_ref[:, pl.ds(first, WIN)] += jnp.dot(d_scores, query, preferred_element_type=F32)
        dq_ref[:, pl.ds(first, WIN)] += lax.dot_general(
            d_scores, key, (((0,), (0,)), ((), ())), preferred_element_type=F32
        )

    for head in range(HEADS):
        one(head)
        if head % 4 == 3 and head < 15:
            i = head // 4
            fetch(0, i).wait()
            rows = pl.ds(*tiles[i])
            dn_ref[:, rows] = lax.dot_general(
                dv_ref[...], wbuf[rows, parts[0]], across, preferred_element_type=F32
            )
    g_ref[:, pl.ds(0, D)] = dq_ref[:, pl.ds(0, D)].astype(BF)
    g_ref[:, pl.ds(D, D)] = dk_ref[:, pl.ds(0, D)].astype(BF)
    for i in range(len(tiles)):
        fetch(1, i).wait()
        rows = pl.ds(*tiles[i])
        dn_ref[:, rows] += lax.dot_general(
            g_ref[...], wbuf[rows, parts[1]], across, preferred_element_type=F32
        )
    gain = gain_ref[...]
    gain_sum = jnp.zeros((1, D), F32)
    me = lax.axis_index("seq")
    for k in range(SLOTS):
        rows = pl.ds(pl.multiple_of((me ^ k) * CHUNK, CHUNK), CHUNK)
        normalized, inv_std = normalize(x_ref[rows, pl.ds(0, D)])
        d_normed = dn_ref[rows, :]
        gain_sum = gain_sum + jnp.sum(d_normed * normalized, axis=0, keepdims=True)
        d_hat = d_normed * gain
        first_mean = jnp.mean(d_hat, axis=-1, keepdims=True)
        second_mean = jnp.mean(d_hat * normalized, axis=-1, keepdims=True)
        out = inv_std * (d_hat - first_mean - normalized * second_mean)
        outs[k][...] = out.astype(BF)
    gain_out[...] = gain_sum


def swap_seq(value, k):
    return lax.ppermute(value, "seq", [(i, i ^ k) for i in range(SLOTS)])


def swap_plane(value, j):
    pairs = []
    for dp in range(16):
        for seq in range(SLOTS):
            pairs.append((dp * SLOTS + seq, (dp ^ (4 * j if seq % 2 == 0 else j)) * SLOTS + seq))
    return lax.ppermute(value, ("dp", "seq"), pairs)


def exchange_plane(blocks):
    groups = []
    for core in range(2):
        for i in range(4):
            plane = [4 * i + j if core == 0 else 4 * j + i for j in range(4)]
            groups.append([dp * SLOTS + 2 * x + core for dp in plane for x in range(4)])
    return lax.all_to_all(
        blocks, ("dp", "seq"), split_axis=0, concat_axis=0, tiled=True, axis_index_groups=groups
    )


def exchange(rows):
    blocks = rows.reshape(SLOTS, CHUNK, -1)
    moved = lax.all_to_all(blocks, "seq", split_axis=0, concat_axis=0, tiled=True)
    return moved.reshape(rows.shape)


def four(rank, dims):
    return [shape(dims, F32)] + [shape(dims, BF)] * (rank - 1)


def shards(block_input, norm_gain, qkv_weight, frame_clip, out_grad):
    factor = 32768 ** (-0.5)
    gain = norm_gain.reshape(1, D)

    packed = call(
        pack_body,
        shape((ROWS, WIDE), BF),
        in_specs=[SMEM, VMEM],
        mib=8,
        data=10**6,
        name="pack",
    )(frame_clip, block_input.reshape(ROWS, D))
    x = exchange(packed)
    chunks = [shape((CHUNK, D), BF)] * SLOTS
    sent = call(
        split_body, chunks, in_specs=[pl.BlockSpec(memory_space=pl.ANY), VMEM], mib=8, data=10**6, name="split"
    )(x, out_grad.reshape(ROWS, D))
    grads = [sent[0]] + [swap_seq(sent[k], k) for k in range(1, SLOTS)]

    normed = call(norm_body, shape((ROWS, D), BF), mib=8, data=10**6, name="norm")(x, gain)
    nt, nt_sent = call(
        turn_body,
        [shape((D, ROWS), BF)] * 2,
        scratch=[pltpu.VMEM((D, ROWS), F32)] * 2,
        mib=8,
        data=4 * 10**6,
        name="turn",
    )(normed)
    nt_other = swap_seq(nt_sent, 1)
    qkv, soft, probs = call(
        project_body,
        [
            shape((ROWS, PADDED), BF),
            shape((HEADS, ROWS, ROWS), F32),
            shape((HEADS, ROWS, ROWS), BF),
        ],
        scratch=[
            pltpu.VMEM((D, TRIPLE), BF),
            pltpu.VMEM((ROWS, ROWS), F32),
            pltpu.SemaphoreType.DMA((7,)),
        ],
        in_specs=[VMEM, VMEM, HBM],
        mib=40,
        flops=5 * 10**9,
        data=40 * 10**6,
        name="project",
    )(x, normed, qkv_weight)

    d_value, mine, theirs, grad_wide = call(
        value_body,
        [
            shape((ROWS, D), BF),
            shape((ROWS, HALF), BF),
            shape((ROWS, HALF), BF),
            shape((ROWS, WIDE), BF),
        ],
        scratch=[pltpu.VMEM((ROWS, WIDE), F32)],
        mib=16,
        flops=10**9,
        data=5 * 10**6,
        name="value",
    )(probs, *grads)
    other = swap_seq(theirs, 1)
    terms = call(
        weight_body,
        four(4, (4 * BLOCK, HALF)),
        mib=16,
        flops=11 * 10**8,
        data=6 * 10**6,
        name="weight",
    )(nt, nt_other, mine, other)
    terms = [terms[0]] + [swap_plane(terms[j], j) for j in range(1, 4)]

    results = call(
        input_body,
        chunks + [shape((1, D), F32)],
        scratch=[
            pltpu.VMEM((D, TRIPLE), BF),
            pltpu.VMEM((ROWS, WIDE), F32),
            pltpu.VMEM((ROWS, WIDE), F32),
            pltpu.VMEM((ROWS, 2 * D), BF),
            pltpu.VMEM((ROWS, D), F32),
            pltpu.SemaphoreType.DMA((2, 3)),
        ],
        in_specs=[VMEM] * 6 + [HBM],
        mib=40,
        flops=6 * 10**9,
        data=20 * 10**6,
        name="input",
    )(x, qkv, soft, grad_wide, d_value, gain, qkv_weight)
    returned = [results[0]] + [swap_seq(results[k], k) for k in range(1, SLOTS)]
    gain_term = results[SLOTS]
    gains = [gain_term] + [swap_plane(gain_term, j) for j in range(1, 4)]

    sums = call(second_body, shape((16, 24, HALF), BF), mib=16, data=5 * 10**6, name="second")(
        *terms, *gains
    )
    sums = exchange_plane(sums)
    mine, theirs = call(third_body, [shape((16, HALF), F32)] * 2, mib=8, data=10**6, name="third")(
        sums
    )
    weight_grad, gain_grad = call(
        last_body(factor),
        [shape((11, D), F32), shape((1, D), F32)],
        mib=8,
        data=10**5,
        name="last",
    )(mine, swap_seq(theirs, 1))
    input_grad = call(join_body, shape((ROWS, D), BF), mib=8, data=10**6, name="join")(*returned)
    return input_grad.reshape(block_input.shape), weight_grad, gain_grad.reshape(D)


def solution(mesh):
    placed = (P("dp", "seq", None, None), P(), P(), P("dp", "seq"), P("dp", "seq", None, None))
    return jax.shard_map(
        shards,
        mesh=mesh,
        in_specs=placed,
        out_specs=(P("dp", "seq", None, None), P(("dp", "seq"), None), P()),
        check_vma=False,
    )
```

time: 829 us -> 96.1 us (0.12)
  blocking collectives: 501 us -> 17.9 us
  starting transfers between devices: 186 us -> 41.8 us
  local copies, waits for them, and re-layouts: 86.7 us -> 1.12 us
  matrix products: 26.6 us -> 0 us
  Pallas kernels: 0 us -> 25.3 us
  other arithmetic: 15 us -> 0.62 us
    unnamed x1 -> x0, blocking collectives: 376 us -> none
    unnamed x40 -> x0, starting transfers between devices: 176 us -> none
    psum x1 -> x0, blocking collectives: 66.6 us -> none  [shards(): gain_sum = lax.psum(gain_local, ('dp', 'seq'))]
    unnamed x65 -> x6, local copies, waits for them, and re-layouts: 66 us -> 1.11 us
    ppermute x0 -> x23, starting transfers between devices: none -> 36.9 us  [the longest x17 26.3 us: swap_seq(): return lax.ppermute(value, 'seq', [(i, i ^ k) for i in range(SLOTS)])]
    eq x1 -> x0, blocking collectives: 26.8 us -> none  [shards(): same_clip = clip_ids[:, None] == clip_ids[None, :]]
    dot_general x8 -> x0, matrix products: 26.6 us -> none  [the longest x1 9.44 us: shards(): jnp.dot(normed.reshape(-1, width), qkv_weight, preferred_element_type=jnp...]
    pallas_call x0 -> x12, Pallas kernels: none -> 25.3 us  [the longest x1 10.3 us: shards(): call(input_body, chunks + [shape((1, D), F32)], scratch=[pltpu.VMEM((D, T...]
  transfers between devices with their start and end apart: 42 -> 24, of which waited for: 3 -> 4; matrix products, arithmetic and copies ran while one was open for 3% -> 0% of each run, Pallas kernels for 0% -> 23%
where the time goes in v1:
time: 96.1 us; the launch traced here: 95.8 us
  starting transfers between devices  41.8 us (43%)
  Pallas kernels  25.3 us (26%)
  blocking collectives  17.9 us (19%)
  waiting for transfers between devices  7.61 us (8%)
  between operations  1.43 us (1%)
  local copies, waits for them, and re-layouts  1.12 us (1%)
    ppermute x17, starting transfers between devices, swap_seq(): return lax.ppermute(value, 'seq', [(i, i ^ k) for i in range(SLOTS)])  26.3 us
    all_to_all x1, blocking collectives, exchange(): lax.all_to_all(blocks, 'seq', split_axis=0, concat_axis=0, tiled=True)  17.9 us
    ppermute x6, starting transfers between devices, swap_plane(): return lax.ppermute(value, ('dp', 'seq'), pairs)  10.5 us
    pallas_call x1, Pallas kernels, shards(): call(input_body, chunks + [shape((1, D), F32)], scratch=[pltpu.VMEM((D, T...  10.3 us
    pallas_call x1, Pallas kernels, shards(): call(project_body, [shape((ROWS, PADDED), BF), shape((HEADS, ROWS, ROWS),...  8.85 us
    ppermute x17, waiting for transfers between devices, swap_seq(): return lax.ppermute(value, 'seq', [(i, i ^ k) for i in range(SLOTS)])  5.5 us
    all_to_all x1, starting transfers between devices, exchange_plane(): lax.all_to_all(blocks, ('dp', 'seq'), split_axis=0, concat_axis=0, tiled=...  4.89 us
    ppermute x6, waiting for transfers between devices, swap_plane(): return lax.ppermute(value, ('dp', 'seq'), pairs)  2.11 us
  transfers between devices with their start and end apart: 24, of which 4 were waited for; matrix products, arithmetic and copies ran while one was open for 0% of the time, Pallas kernels for 23%

profile of v1, /device:TPU:1, one launch (start us, length us, event | category | flops | bytes accessed | tf_op | source)
XLA Modules:
  0.0 95.8 jit_solution(4970564193292524754)
XLA Ops:
  1.3 1.1 %copy-done = bf16[1,1,256,1408]{3,2,1,0:T(8,128)(2,1)S(1)} copy-done((bf16[1,1,256,1408]{3,2,1,0:T(8,128)(2,1)S(1)}, bf16[1,1,256,1408]{3,2,1,0:T(8,128)(2,1)}, u32[]{:S(2)}) %copy-start) | copy-done | bytes 720920
  2.5 17.9 %all_to_all.10 = bf16[8,32,1536]{2,1,0:T(8,128)(2,1)S(1)} all-to-all(bf16[8,32,1536]{2,1,0:T(8,128)(2,1)S(1)} %bitcast.9), channel_id=1, replica_groups=mesh['dp'=16,'seq'=8] {'seq'}, dimensions={0} | all-to-all | bytes 1572864 | tf_op jit(solution)/shard_map/all_to_all | solution.py:325
  20.5 1.1 %collective-permute-start = (bf16[32,1408]{1,0:T(8,128)(2,1)S(1)}, bf16[32,1408]{1,0:T(8,128)(2,1)S(1)}, u32[]{:S(2)}, u32[]{:S(2)}) collective-permute-start(bf16[32,1408]{1,0:T(8,128)(2,1)S(1)} %get-tuple-element.41), channel_id=1, source_target_pairs={{0,1},{1,0},{2,3},{3,2},{4,5},{5,4},{6,7},{7,6},{8,9},{9,8},{10,11... | collective-permute-start | bytes 270344 | tf_op jit(solution)/shard_map/ppermute | solution.py:301
  21.9 1.4 %collective-permute-start.2 = (bf16[32,1408]{1,0:T(8,128)(2,1)S(1)}, bf16[32,1408]{1,0:T(8,128)(2,1)S(1)}, u32[]{:S(2)}, u32[]{:S(2)}) collective-permute-start(bf16[32,1408]{1,0:T(8,128)(2,1)S(1)} %get-tuple-element.43), channel_id=1, source_target_pairs={{0,3},{1,2},{2,1},{3,0},{4,7},{5,6},{6,5},{7,4},{8,11},{9,10},{10,... | collective-permute-start | bytes 270344 | tf_op jit(solution)/shard_map/ppermute | solution.py:301
  24.3 2.9 %collective-permute-start.4 = (bf16[32,1408]{1,0:T(8,128)(2,1)S(1)}, bf16[32,1408]{1,0:T(8,128)(2,1)S(1)}, u32[]{:S(2)}, u32[]{:S(2)}) collective-permute-start(bf16[32,1408]{1,0:T(8,128)(2,1)S(1)} %get-tuple-element.45), channel_id=1, source_target_pairs={{0,5},{1,4},{2,7},{3,6},{4,1},{5,0},{6,3},{7,2},{8,13},{9,12},{10,... | collective-permute-start | bytes 270344 | tf_op jit(solution)/shard_map/ppermute | solution.py:301
  28.8 2.0 %collective-permute-start.6 = (bf16[32,1408]{1,0:T(8,128)(2,1)S(1)}, bf16[32,1408]{1,0:T(8,128)(2,1)S(1)}, u32[]{:S(2)}, u32[]{:S(2)}) collective-permute-start(bf16[32,1408]{1,0:T(8,128)(2,1)S(1)} %get-tuple-element.47), channel_id=1, source_target_pairs={{0,7},{1,6},{2,5},{3,4},{4,3},{5,2},{6,1},{7,0},{8,15},{9,14},{10,... | collective-permute-start | bytes 270344 | tf_op jit(solution)/shard_map/ppermute | solution.py:301
  31.0 8.8 %project.1 = (bf16[256,4352]{1,0:T(8,128)(2,1)S(1)}, f32[16,256,256]{2,1,0:T(8,128)S(1)}, bf16[16,256,256]{2,1,0:T(8,128)(2,1)S(1)}) custom-call(bf16[256,1536]{1,0:T(8,128)(2,1)S(1)} %bitcast.7, bf16[256,1408]{1,0:T(8,128)(2,1)S(1)} %norm.1.normed_ref, bf16[1408,4224]{1,0:T(8,128)(2,1)} %refs_6_.1), custom_call_target="tpu_custom_call" | custom-call | flops 5000000000 | bytes 40000000 | tf_op jit(solution)/shard_map/project/pallas_call | solution.py:362
  41.4 1.4 %collective-permute-done.15.dv_other_ref = bf16[256,768]{1,0:T(8,128)(2,1)S(1)} collective-permute-done((bf16[256,768]{1,0:T(8,128)(2,1)S(1)}, bf16[256,768]{1,0:T(8,128)(2,1)S(1)}, u32[]{:S(2)}, u32[]{:S(2)}) %collective-permute-start.15) | collective-permute-done | bytes 393248 | tf_op jit(solution)/shard_map/ppermute | solution.py:301
  42.8 1.3 %weight.1 = (f32[352,768]{1,0:T(8,128)S(1)}, bf16[352,768]{1,0:T(8,128)(2,1)S(1)}, bf16[352,768]{1,0:T(8,128)(2,1)S(1)}, bf16[352,768]{1,0:T(8,128)(2,1)S(1)}) custom-call(bf16[1408,256]{1,0:T(8,128)(2,1)S(1)} %get-tuple-element.58.nt_ref, bf16[1408,256]{1,0:T(8,128)(2,1)S(1)} %collective-permute-done.14.nt_other_ref, ...), custom_call_target="tpu_custom_call" | custom-call | flops 1100000000 | bytes 6000000 | tf_op jit(solution)/shard_map/weight/pallas_call | solution.py:396
  44.1 1.7 %collective-permute-start.16 = (bf16[352,768]{1,0:T(8,128)(2,1)S(1)}, bf16[352,768]{1,0:T(8,128)(2,1)S(1)}, u32[]{:S(2)}, u32[]{:S(2)}) collective-permute-start(bf16[352,768]{1,0:T(8,128)(2,1)S(1)} %get-tuple-element.63), channel_id=1, source_target_pairs={{0,32},{1,9},{2,34},{3,11},{4,36},{5,13},{6,38},{7,15},{8,40},{9,1... | collective-permute-start | bytes 1622024 | tf_op jit(solution)/shard_map/ppermute | solution.py:309
  45.8 3.3 %collective-permute-start.17 = (bf16[352,768]{1,0:T(8,128)(2,1)S(1)}, bf16[352,768]{1,0:T(8,128)(2,1)S(1)}, u32[]{:S(2)}, u32[]{:S(2)}) collective-permute-start(bf16[352,768]{1,0:T(8,128)(2,1)S(1)} %get-tuple-element.64), channel_id=1, source_target_pairs={{0,64},{1,17},{2,66},{3,19},{4,68},{5,21},{6,70},{7,23},{8,72},{9,... | collective-permute-start | bytes 1622024 | tf_op jit(solution)/shard_map/ppermute | solution.py:309
  49.1 10.3 %input.1 = (bf16[32,1408]{1,0:T(8,128)(2,1)S(1)}, bf16[32,1408]{1,0:T(8,128)(2,1)S(1)}, bf16[32,1408]{1,0:T(8,128)(2,1)S(1)}, bf16[32,1408]{1,0:T(8,128)(2,1)S(1...) custom-call(bf16[256,1536]{1,0:T(8,128)(2,1)S(1)} %bitcast.8, ...), custom_call_target="tpu_custom_call" | custom-call | flops 6000000000 | bytes 20000000 | tf_op jit(solution)/shard_map/input/pallas_call | solution.py:406
  59.5 3.9 %collective-permute-start.20 = (f32[1,1408]{1,0:T(1,128)S(1)}, f32[1,1408]{1,0:T(1,128)S(1)}, u32[]{:S(2)}, u32[]{:S(2)}) collective-permute-start(f32[1,1408]{1,0:T(1,128)S(1)} %get-tuple-element.66.refs_4_), channel_id=1, source_target_pairs={{0,64},{1,17},{2,66},{3,19},{4,68},{5,21},{6,70},{7,23},{8,72},{9,... | collective-permute-start | bytes 16904 | tf_op jit(solution)/shard_map/ppermute | solution.py:309
  63.3 1.6 %collective-permute-start.21 = (f32[1,1408]{1,0:T(1,128)S(1)}, f32[1,1408]{1,0:T(1,128)S(1)}, u32[]{:S(2)}, u32[]{:S(2)}) collective-permute-start(f32[1,1408]{1,0:T(1,128)S(1)} %get-tuple-element.66.refs_4_), channel_id=1, source_target_pairs={{0,96},{1,25},{2,98},{3,27},{4,100},{5,29},{6,102},{7,31},{8,104},... | collective-permute-start | bytes 16904 | tf_op jit(solution)/shard_map/ppermute | solution.py:309
  64.9 2.1 %collective-permute-done.21.refs_7_ = f32[1,1408]{1,0:T(1,128)S(1)} collective-permute-done((f32[1,1408]{1,0:T(1,128)S(1)}, f32[1,1408]{1,0:T(1,128)S(1)}, u32[]{:S(2)}, u32[]{:S(2)}) %collective-permute-start.21) | collective-permute-done | bytes 5664 | tf_op jit(solution)/shard_map/ppermute | solution.py:309
  67.0 1.1 %second.1 = bf16[16,24,768]{2,1,0:T(8,128)(2,1)} custom-call(f32[352,768]{1,0:T(8,128)S(1)} %get-tuple-element.62.refs_0_, bf16[352,768]{1,0:T(8,128)(2,1)S(1)} %collective-permute-done.16.refs_1_, bf16[352,768]{1,0:T(8,128)(2,1)S(1)} %collective-permute-done.17.refs_2_, bf16[352,768]{1,0:T(8,128)(2,1)S(1)} %collective-permute-done.18.refs_3_, ...), custom_call_target="tpu_custom_call" | custom-call | bytes 5000000 | tf_op jit(solution)/shard_map/second/pallas_call | solution.py:427
  68.2 4.9 %all-to-all-start.1 = ((bf16[16,24,768]{2,1,0:T(8,128)(2,1)}), bf16[16,24,768]{2,1,0:T(8,128)(2,1)S(1)}, u32[]{:S(2)}, u32[]{:S(2)}) async-start(bf16[16,24,768]{2,1,0:T(8,128)(2,1)} %second.1), calls=%async_computation.1 | async-start | bytes 1179648 | tf_op jit(solution)/shard_map/all_to_all | solution.py:318
  73.1 3.1 %collective-permute-start.7 = (bf16[32,1408]{1,0:T(8,128)(2,1)S(1)}, bf16[32,1408]{1,0:T(8,128)(2,1)S(1)}, u32[]{:S(2)}, u32[]{:S(2)}) collective-permute-start(bf16[32,1408]{1,0:T(8,128)(2,1)S(1)} %get-tuple-element.51), channel_id=1, source_target_pairs={{0,1},{1,0},{2,3},{3,2},{4,5},{5,4},{6,7},{7,6},{8,9},{9,8},{10,11... | collective-permute-start | bytes 270344 | tf_op jit(solution)/shard_map/ppermute | solution.py:301
  76.2 1.6 %collective-permute-start.8 = (bf16[32,1408]{1,0:T(8,128)(2,1)S(1)}, bf16[32,1408]{1,0:T(8,128)(2,1)S(1)}, u32[]{:S(2)}, u32[]{:S(2)}) collective-permute-start(bf16[32,1408]{1,0:T(8,128)(2,1)S(1)} %get-tuple-element.52), channel_id=1, source_target_pairs={{0,2},{1,3},{2,0},{3,1},{4,6},{5,7},{6,4},{7,5},{8,10},{9,11},{10,... | collective-permute-start | bytes 270344 | tf_op jit(solution)/shard_map/ppermute | solution.py:301
  77.9 3.1 %collective-permute-start.10 = (bf16[32,1408]{1,0:T(8,128)(2,1)S(1)}, bf16[32,1408]{1,0:T(8,128)(2,1)S(1)}, u32[]{:S(2)}, u32[]{:S(2)}) collective-permute-start(bf16[32,1408]{1,0:T(8,128)(2,1)S(1)} %get-tuple-element.54), channel_id=1, source_target_pairs={{0,4},{1,5},{2,6},{3,7},{4,0},{5,1},{6,2},{7,3},{8,12},{9,13},{10,... | collective-permute-start | bytes 270344 | tf_op jit(solution)/shard_map/ppermute | solution.py:301
  81.3 2.7 %collective-permute-start.12 = (bf16[32,1408]{1,0:T(8,128)(2,1)S(1)}, bf16[32,1408]{1,0:T(8,128)(2,1)S(1)}, u32[]{:S(2)}, u32[]{:S(2)}) collective-permute-start(bf16[32,1408]{1,0:T(8,128)(2,1)S(1)} %get-tuple-element.56), channel_id=1, source_target_pairs={{0,6},{1,7},{2,4},{3,5},{4,2},{5,3},{6,0},{7,1},{8,14},{9,15},{10,... | collective-permute-start | bytes 270344 | tf_op jit(solution)/shard_map/ppermute | solution.py:301
  84.0 5.3 %collective-permute-start.13 = (bf16[32,1408]{1,0:T(8,128)(2,1)S(1)}, bf16[32,1408]{1,0:T(8,128)(2,1)S(1)}, u32[]{:S(2)}, u32[]{:S(2)}) collective-permute-start(bf16[32,1408]{1,0:T(8,128)(2,1)S(1)} %get-tuple-element.57), channel_id=1, source_target_pairs={{0,7},{1,6},{2,5},{3,4},{4,3},{5,2},{6,1},{7,0},{8,15},{9,14},{10,... | collective-permute-start | bytes 270344 | tf_op jit(solution)/shard_map/ppermute | solution.py:301
  89.5 2.0 %collective-permute-done.11.refs_5_ = bf16[32,1408]{1,0:T(8,128)(2,1)S(1)} collective-permute-done((bf16[32,1408]{1,0:T(8,128)(2,1)S(1)}, bf16[32,1408]{1,0:T(8,128)(2,1)S(1)}, u32[]{:S(2)}, u32[]{:S(2)}) %collective-permute-start.11) | collective-permute-done | bytes 90144 | tf_op jit(solution)/shard_map/ppermute | solution.py:301
  91.5 2.1 %collective-permute-done.13.refs_7_ = bf16[32,1408]{1,0:T(8,128)(2,1)S(1)} collective-permute-done((bf16[32,1408]{1,0:T(8,128)(2,1)S(1)}, bf16[32,1408]{1,0:T(8,128)(2,1)S(1)}, u32[]{:S(2)}, u32[]{:S(2)}) %collective-permute-start.13) | collective-permute-done | bytes 90144 | tf_op jit(solution)/shard_map/ppermute | solution.py:301
  (45 shorter events, 7.8 us)
Async XLA Ops:
  20.5 7.4 %collective-permute-start = (bf16[32,1408]{1,0:T(8,128)(2,1)S(1)}, bf16[32,1408]{1,0:T(8,128)(2,1)S(1)}, u32[]{:S(2)}, u32[]{:S(2)}) collective-permute-start(bf16[32,1408]{1,0:T(8,128)(2,1)S(1)} %get-tuple-element.41), channel_id=1, source_target_pairs={{0,1},{1,0},{2,3},{3,2},{4,5},{5,4},{6,7},{7,6},{8,9},{9,8},{10,11... | collective-permute-start | bytes 270344 | tf_op jit(solution)/shard_map/ppermute | solution.py:301
  21.6 7.2 %collective-permute-start.1 = (bf16[32,1408]{1,0:T(8,128)(2,1)S(1)}, bf16[32,1408]{1,0:T(8,128)(2,1)S(1)}, u32[]{:S(2)}, u32[]{:S(2)}) collective-permute-start(bf16[32,1408]{1,0:T(8,128)(2,1)S(1)} %get-tuple-element.42), channel_id=1, source_target_pairs={{0,2},{1,3},{2,0},{3,1},{4,6},{5,7},{6,4},{7,5},{8,10},{9,11},{10,... | collective-permute-start | bytes 270344 | tf_op jit(solution)/shard_map/ppermute | solution.py:301
  21.9 9.0 %collective-permute-start.2 = (bf16[32,1408]{1,0:T(8,128)(2,1)S(1)}, bf16[32,1408]{1,0:T(8,128)(2,1)S(1)}, u32[]{:S(2)}, u32[]{:S(2)}) collective-permute-start(bf16[32,1408]{1,0:T(8,128)(2,1)S(1)} %get-tuple-element.43), channel_id=1, source_target_pairs={{0,3},{1,2},{2,1},{3,0},{4,7},{5,6},{6,5},{7,4},{8,11},{9,10},{10,... | collective-permute-start | bytes 270344 | tf_op jit(solution)/shard_map/ppermute | solution.py:301
  23.8 16.1 %collective-permute-start.3 = (bf16[32,1408]{1,0:T(8,128)(2,1)S(1)}, bf16[32,1408]{1,0:T(8,128)(2,1)S(1)}, u32[]{:S(2)}, u32[]{:S(2)}) collective-permute-start(bf16[32,1408]{1,0:T(8,128)(2,1)S(1)} %get-tuple-element.44), channel_id=1, source_target_pairs={{0,4},{1,5},{2,6},{3,7},{4,0},{5,1},{6,2},{7,3},{8,12},{9,13},{10,... | collective-permute-start | bytes 270344 | tf_op jit(solution)/shard_map/ppermute | solution.py:301
  24.3 15.6 %collective-permute-start.4 = (bf16[32,1408]{1,0:T(8,128)(2,1)S(1)}, bf16[32,1408]{1,0:T(8,128)(2,1)S(1)}, u32[]{:S(2)}, u32[]{:S(2)}) collective-permute-start(bf16[32,1408]{1,0:T(8,128)(2,1)S(1)} %get-tuple-element.45), channel_id=1, source_target_pairs={{0,5},{1,4},{2,7},{3,6},{4,1},{5,0},{6,3},{7,2},{8,13},{9,12},{10,... | collective-permute-start | bytes 270344 | tf_op jit(solution)/shard_map/ppermute | solution.py:301
  27.8 12.0 %collective-permute-start.5 = (bf16[32,1408]{1,0:T(8,128)(2,1)S(1)}, bf16[32,1408]{1,0:T(8,128)(2,1)S(1)}, u32[]{:S(2)}, u32[]{:S(2)}) collective-permute-start(bf16[32,1408]{1,0:T(8,128)(2,1)S(1)} %get-tuple-element.46), channel_id=1, source_target_pairs={{0,6},{1,7},{2,4},{3,5},{4,2},{5,3},{6,0},{7,1},{8,14},{9,15},{10,... | collective-permute-start | bytes 270344 | tf_op jit(solution)/shard_map/ppermute | solution.py:301
  28.8 11.1 %collective-permute-start.6 = (bf16[32,1408]{1,0:T(8,128)(2,1)S(1)}, bf16[32,1408]{1,0:T(8,128)(2,1)S(1)}, u32[]{:S(2)}, u32[]{:S(2)}) collective-permute-start(bf16[32,1408]{1,0:T(8,128)(2,1)S(1)} %get-tuple-element.47), channel_id=1, source_target_pairs={{0,7},{1,6},{2,5},{3,4},{4,3},{5,2},{6,1},{7,0},{8,15},{9,14},{10,... | collective-permute-start | bytes 270344 | tf_op jit(solution)/shard_map/ppermute | solution.py:301
  30.8 11.9 %collective-permute-start.14 = (bf16[1408,256]{1,0:T(8,128)(2,1)S(1)}, bf16[1408,256]{1,0:T(8,128)(2,1)S(1)}, u32[]{:S(2)}, u32[]{:S(2)}) collective-permute-start(bf16[1408,256]{1,0:T(8,128)(2,1)S(1)} %get-tuple-element.59), channel_id=1, source_target_pairs={{0,1},{1,0},{2,3},{3,2},{4,5},{5,4},{6,7},{7,6},{8,9},{9,8},{10,11... | collective-permute-start | bytes 2162696 | tf_op jit(solution)/shard_map/ppermute | solution.py:301
  40.8 2.0 %collective-permute-start.15 = (bf16[256,768]{1,0:T(8,128)(2,1)S(1)}, bf16[256,768]{1,0:T(8,128)(2,1)S(1)}, u32[]{:S(2)}, u32[]{:S(2)}) collective-permute-start(bf16[256,768]{1,0:T(8,128)(2,1)S(1)} %get-tuple-element.61), channel_id=1, source_target_pairs={{0,1},{1,0},{2,3},{3,2},{4,5},{5,4},{6,7},{7,6},{8,9},{9,8},{10,11... | collective-permute-start | bytes 1179656 | tf_op jit(solution)/shard_map/ppermute | solution.py:301
  44.1 23.0 %collective-permute-start.16 = (bf16[352,768]{1,0:T(8,128)(2,1)S(1)}, bf16[352,768]{1,0:T(8,128)(2,1)S(1)}, u32[]{:S(2)}, u32[]{:S(2)}) collective-permute-start(bf16[352,768]{1,0:T(8,128)(2,1)S(1)} %get-tuple-element.63), channel_id=1, source_target_pairs={{0,32},{1,9},{2,34},{3,11},{4,36},{5,13},{6,38},{7,15},{8,40},{9,1... | collective-permute-start | bytes 1622024 | tf_op jit(solution)/shard_map/ppermute | solution.py:309
  45.8 21.2 %collective-permute-start.17 = (bf16[352,768]{1,0:T(8,128)(2,1)S(1)}, bf16[352,768]{1,0:T(8,128)(2,1)S(1)}, u32[]{:S(2)}, u32[]{:S(2)}) collective-permute-start(bf16[352,768]{1,0:T(8,128)(2,1)S(1)} %get-tuple-element.64), channel_id=1, source_target_pairs={{0,64},{1,17},{2,66},{3,19},{4,68},{5,21},{6,70},{7,23},{8,72},{9,... | collective-permute-start | bytes 1622024 | tf_op jit(solution)/shard_map/ppermute | solution.py:309
  49.1 17.9 %collective-permute-start.18 = (bf16[352,768]{1,0:T(8,128)(2,1)S(1)}, bf16[352,768]{1,0:T(8,128)(2,1)S(1)}, u32[]{:S(2)}, u32[]{:S(2)}) collective-permute-start(bf16[352,768]{1,0:T(8,128)(2,1)S(1)} %get-tuple-element.65), channel_id=1, source_target_pairs={{0,96},{1,25},{2,98},{3,27},{4,100},{5,29},{6,102},{7,31},{8,104},... | collective-permute-start | bytes 1622024 | tf_op jit(solution)/shard_map/ppermute | solution.py:309
  59.4 3.9 %collective-permute-start.19 = (f32[1,1408]{1,0:T(1,128)S(1)}, f32[1,1408]{1,0:T(1,128)S(1)}, u32[]{:S(2)}, u32[]{:S(2)}) collective-permute-start(f32[1,1408]{1,0:T(1,128)S(1)} %get-tuple-element.66.refs_4_), channel_id=1, source_target_pairs={{0,32},{1,9},{2,34},{3,11},{4,36},{5,13},{6,38},{7,15},{8,40},{9,1... | collective-permute-start | bytes 16904 | tf_op jit(solution)/shard_map/ppermute | solution.py:309
  59.5 5.4 %collective-permute-start.20 = (f32[1,1408]{1,0:T(1,128)S(1)}, f32[1,1408]{1,0:T(1,128)S(1)}, u32[]{:S(2)}, u32[]{:S(2)}) collective-permute-start(f32[1,1408]{1,0:T(1,128)S(1)} %get-tuple-element.66.refs_4_), channel_id=1, source_target_pairs={{0,64},{1,17},{2,66},{3,19},{4,68},{5,21},{6,70},{7,23},{8,72},{9,... | collective-permute-start | bytes 16904 | tf_op jit(solution)/shard_map/ppermute | solution.py:309
  63.3 3.7 %collective-permute-start.21 = (f32[1,1408]{1,0:T(1,128)S(1)}, f32[1,1408]{1,0:T(1,128)S(1)}, u32[]{:S(2)}, u32[]{:S(2)}) collective-permute-start(f32[1,1408]{1,0:T(1,128)S(1)} %get-tuple-element.66.refs_4_), channel_id=1, source_target_pairs={{0,96},{1,25},{2,98},{3,27},{4,100},{5,29},{6,102},{7,31},{8,104},... | collective-permute-start | bytes 16904 | tf_op jit(solution)/shard_map/ppermute | solution.py:309
  68.2 21.1 %all-to-all-start.1 = ((bf16[16,24,768]{2,1,0:T(8,128)(2,1)}), bf16[16,24,768]{2,1,0:T(8,128)(2,1)S(1)}, u32[]{:S(2)}, u32[]{:S(2)}) async-start(bf16[16,24,768]{2,1,0:T(8,128)(2,1)} %second.1), calls=%async_computation.1 | async-start | bytes 1179648 | tf_op jit(solution)/shard_map/all_to_all | solution.py:318
  73.1 8.2 %collective-permute-start.7 = (bf16[32,1408]{1,0:T(8,128)(2,1)S(1)}, bf16[32,1408]{1,0:T(8,128)(2,1)S(1)}, u32[]{:S(2)}, u32[]{:S(2)}) collective-permute-start(bf16[32,1408]{1,0:T(8,128)(2,1)S(1)} %get-tuple-element.51), channel_id=1, source_target_pairs={{0,1},{1,0},{2,3},{3,2},{4,5},{5,4},{6,7},{7,6},{8,9},{9,8},{10,11... | collective-permute-start | bytes 270344 | tf_op jit(solution)/shard_map/ppermute | solution.py:301
  76.2 7.8 %collective-permute-start.8 = (bf16[32,1408]{1,0:T(8,128)(2,1)S(1)}, bf16[32,1408]{1,0:T(8,128)(2,1)S(1)}, u32[]{:S(2)}, u32[]{:S(2)}) collective-permute-start(bf16[32,1408]{1,0:T(8,128)(2,1)S(1)} %get-tuple-element.52), channel_id=1, source_target_pairs={{0,2},{1,3},{2,0},{3,1},{4,6},{5,7},{6,4},{7,5},{8,10},{9,11},{10,... | collective-permute-start | bytes 270344 | tf_op jit(solution)/shard_map/ppermute | solution.py:301
  77.7 11.6 %collective-permute-start.9 = (bf16[32,1408]{1,0:T(8,128)(2,1)S(1)}, bf16[32,1408]{1,0:T(8,128)(2,1)S(1)}, u32[]{:S(2)}, u32[]{:S(2)}) collective-permute-start(bf16[32,1408]{1,0:T(8,128)(2,1)S(1)} %get-tuple-element.53), channel_id=1, source_target_pairs={{0,3},{1,2},{2,1},{3,0},{4,7},{5,6},{6,5},{7,4},{8,11},{9,10},{10,... | collective-permute-start | bytes 270344 | tf_op jit(solution)/shard_map/ppermute | solution.py:301
  77.9 11.6 %collective-permute-start.10 = (bf16[32,1408]{1,0:T(8,128)(2,1)S(1)}, bf16[32,1408]{1,0:T(8,128)(2,1)S(1)}, u32[]{:S(2)}, u32[]{:S(2)}) collective-permute-start(bf16[32,1408]{1,0:T(8,128)(2,1)S(1)} %get-tuple-element.54), channel_id=1, source_target_pairs={{0,4},{1,5},{2,6},{3,7},{4,0},{5,1},{6,2},{7,3},{8,12},{9,13},{10,... | collective-permute-start | bytes 270344 | tf_op jit(solution)/shard_map/ppermute | solution.py:301
  80.9 10.6 %collective-permute-start.11 = (bf16[32,1408]{1,0:T(8,128)(2,1)S(1)}, bf16[32,1408]{1,0:T(8,128)(2,1)S(1)}, u32[]{:S(2)}, u32[]{:S(2)}) collective-permute-start(bf16[32,1408]{1,0:T(8,128)(2,1)S(1)} %get-tuple-element.55), channel_id=1, source_target_pairs={{0,5},{1,4},{2,7},{3,6},{4,1},{5,0},{6,3},{7,2},{8,13},{9,12},{10,... | collective-permute-start | bytes 270344 | tf_op jit(solution)/shard_map/ppermute | solution.py:301
  81.3 10.2 %collective-permute-start.12 = (bf16[32,1408]{1,0:T(8,128)(2,1)S(1)}, bf16[32,1408]{1,0:T(8,128)(2,1)S(1)}, u32[]{:S(2)}, u32[]{:S(2)}) collective-permute-start(bf16[32,1408]{1,0:T(8,128)(2,1)S(1)} %get-tuple-element.56), channel_id=1, source_target_pairs={{0,6},{1,7},{2,4},{3,5},{4,2},{5,3},{6,0},{7,1},{8,14},{9,15},{10,... | collective-permute-start | bytes 270344 | tf_op jit(solution)/shard_map/ppermute | solution.py:301
  84.0 9.7 %collective-permute-start.13 = (bf16[32,1408]{1,0:T(8,128)(2,1)S(1)}, bf16[32,1408]{1,0:T(8,128)(2,1)S(1)}, u32[]{:S(2)}, u32[]{:S(2)}) collective-permute-start(bf16[32,1408]{1,0:T(8,128)(2,1)S(1)} %get-tuple-element.57), channel_id=1, source_target_pairs={{0,7},{1,6},{2,5},{3,4},{4,3},{5,2},{6,1},{7,0},{8,15},{9,14},{10,... | collective-permute-start | bytes 270344 | tf_op jit(solution)/shard_map/ppermute | solution.py:301
  89.3 5.2 %collective-permute-start.22 = (f32[16,768]{1,0:T(8,128)S(1)}, f32[16,768]{1,0:T(8,128)S(1)}, u32[]{:S(2)}, u32[]{:S(2)}) collective-permute-start(f32[16,768]{1,0:T(8,128)S(1)} %get-tuple-element.68), channel_id=1, source_target_pairs={{0,1},{1,0},{2,3},{3,2},{4,5},{5,4},{6,7},{7,6},{8,9},{9,8},{10,11... | collective-permute-start | bytes 147464 | tf_op jit(solution)/shard_map/ppermute | solution.py:301
  (3 other events, 40.0 us)

commit v2 on v1

--- a/solution.py
+++ b/solution.py
@@ -15,6 +15,8 @@
 ROWS = 256
 CHUNK = 32
 SLOTS = 8
+CHIPS = 4
+PAIR = 2 * CHUNK
 TILE = 256
 BLOCK = 88
 HALF = 768
@@ -66,30 +68,57 @@
     return centered * inv_std, inv_std
 
 
-def pack_body(clip_ref, rows_ref, out_ref):
-    out_ref[:, pl.ds(0, D)] = rows_ref[...]
-    clip = jnp.full((ROWS, 128), clip_ref[0, 0], jnp.int32)
-    out_ref[:, pl.ds(D, 128)] = clip.astype(F32).astype(BF)
-
-
-def split_body(after_ref, rows_ref, *out_refs):
+def place():
     me = lax.axis_index("seq")
-    for k in range(SLOTS):
-        start = pl.multiple_of((me ^ k) * CHUNK, CHUNK)
-        out_refs[k][...] = rows_ref[pl.ds(start, CHUNK), :]
-
-
-def join_body(*refs):
-    out_ref = refs[SLOTS]
-    me = lax.axis_index("seq")
-    for k in range(SLOTS):
-        start = pl.multiple_of((me ^ k) * CHUNK, CHUNK)
-        out_ref[pl.ds(start, CHUNK), :] = refs[k][...]
-
-
-def norm_body(x_ref, gain_ref, normed_ref):
-    normalized, _ = normalize(x_ref[:, pl.ds(0, D)])
-    normed_ref[...] = (normalized * gain_ref[...]).astype(BF)
+    return me // 2, me % 2
+
+
+def part_rows(chip, core):
+    return pl.ds(pl.multiple_of((2 * chip + core) * CHUNK, CHUNK), CHUNK)
+
+
+def split_body(rows_ref, *refs):
+    clip_ref, (mine_ref, theirs_ref) = refs[:-2], refs[-2:]
+    chip, core = place()
+    for j in range(CHIPS):
+        mine_ref[j, :, pl.ds(0, D)] = rows_ref[part_rows(chip ^ j, core), :]
+        theirs_ref[j, :, pl.ds(0, D)] = rows_ref[part_rows(chip ^ j, 1 - core), :]
+    if clip_ref:
+        clip = jnp.full((CHIPS, CHUNK, 128), clip_ref[0][0, 0], jnp.int32).astype(F32).astype(BF)
+        mine_ref[:, :, pl.ds(D, 128)] = clip
+        theirs_ref[:, :, pl.ds(D, 128)] = clip
+
+
+def merge_body(mine_ref, other_ref, *refs):
+    out_refs = refs[-CHIPS:]
+    _, core = place()
+    for j in range(CHIPS):
+        out_refs[j][pl.ds(pl.multiple_of(core * CHUNK, CHUNK), CHUNK), :] = mine_ref[j]
+        out_refs[j][pl.ds(pl.multiple_of((1 - core) * CHUNK, CHUNK), CHUNK), :] = other_ref[j]
+
+
+def part_body(*refs):
+    mine_ref, theirs_ref = refs[CHIPS:]
+    _, core = place()
+    for j in range(CHIPS):
+        mine_ref[j] = refs[j][pl.ds(pl.multiple_of(core * CHUNK, CHUNK), CHUNK), :]
+        theirs_ref[j] = refs[j][pl.ds(pl.multiple_of((1 - core) * CHUNK, CHUNK), CHUNK), :]
+
+
+def join_body(mine_ref, other_ref, out_ref):
+    chip, core = place()
+    for j in range(CHIPS):
+        out_ref[part_rows(chip ^ j, core), :] = mine_ref[j]
+        out_ref[part_rows(chip ^ j, 1 - core), :] = other_ref[j]
+
+
+def norm_body(*refs):
+    xs, (gain_ref, normed_ref, clip_ref) = refs[:CHIPS], refs[CHIPS:]
+    for j in range(CHIPS):
+        rows = pl.ds(j * PAIR, PAIR)
+        normalized, _ = normalize(xs[j][:, pl.ds(0, D)])
+        normed_ref[rows, :] = (normalized * gain_ref[...]).astype(BF)
+        clip_ref[rows, :] = xs[j][:, pl.ds(D, 128)].astype(F32)
 
 
 def turn_body(normed_ref, mine_ref, theirs_ref, wide_ref, other_ref):
@@ -109,7 +138,7 @@
     theirs_ref[...] = other_ref[...].astype(BF)
 
 
-def project_body(x_ref, normed_ref, w_hbm, qkv_ref, soft_ref, prob_ref, wbuf, bias_ref, sems):
+def project_body(clip_ref, normed_ref, w_hbm, qkv_ref, soft_ref, prob_ref, wbuf, bias_ref, sems):
     first = [(0, 512), (512, 1152), (1664, 1152)]
     rest = [(2816, 384), (3200, 384), (3584, 384), (3968, 256)]
 
@@ -128,7 +157,7 @@
 
     row = lax.broadcasted_iota(jnp.int32, (ROWS, ROWS), 0)
     col = lax.broadcasted_iota(jnp.int32, (ROWS, ROWS), 1)
-    clip = x_ref[:, pl.ds(D, 128)].astype(F32)
+    clip = clip_ref[...]
     clip = jnp.concatenate([clip, clip], axis=1)
     kept = (clip == jnp.transpose(clip)) & (row % CHUNK == col % CHUNK)
     bias_ref[...] = jnp.where(kept, 0.0, MASKED).astype(F32)
@@ -156,12 +185,10 @@
 
 
 def value_body(prob_ref, *refs):
-    chunks = refs[:SLOTS]
-    dv_ref, mine_ref, theirs_ref, grad_ref, acc_ref = refs[SLOTS:]
-    me = lax.axis_index("seq")
-    for k in range(SLOTS):
-        start = pl.multiple_of((me ^ k) * CHUNK, CHUNK)
-        grad_ref[pl.ds(start, CHUNK), pl.ds(0, D)] = chunks[k][...]
+    chunks = refs[:CHIPS]
+    dv_ref, mine_ref, theirs_ref, grad_ref, acc_ref = refs[CHIPS:]
+    for j in range(CHIPS):
+        grad_ref[pl.ds(j * PAIR, PAIR), pl.ds(0, D)] = chunks[j][...]
     grad_ref[:, pl.ds(D, 128)] = jnp.zeros((ROWS, 128), BF)
     acc_ref[...] = jnp.zeros_like(acc_ref)
 
@@ -232,9 +259,10 @@
 
 
 def input_body(*refs):
-    x_ref, qkv_ref, soft_ref, grad_ref, dv_ref, gain_ref, w_hbm = refs[:7]
-    outs, gain_out = refs[7 : 7 + SLOTS], refs[7 + SLOTS]
-    wbuf, dq_ref, dk_ref, g_ref, dn_ref, sems = refs[8 + SLOTS :]
+    xs, refs = refs[:CHIPS], refs[CHIPS:]
+    qkv_ref, soft_ref, grad_ref, dv_ref, gain_ref, w_hbm = refs[:6]
+    outs, gain_out = refs[6 : 6 + CHIPS], refs[6 + CHIPS]
+    wbuf, dq_ref, dk_ref, g_ref, dn_ref, sems = refs[7 + CHIPS :]
     tiles = [(0, 512), (512, 512), (1024, 384)]
     parts = [pl.ds(2 * D, D), pl.ds(0, 2 * D)]
 
@@ -283,17 +311,16 @@
         )
     gain = gain_ref[...]
     gain_sum = jnp.zeros((1, D), F32)
-    me = lax.axis_index("seq")
     for k in range(SLOTS):
-        rows = pl.ds(pl.multiple_of((me ^ k) * CHUNK, CHUNK), CHUNK)
-        normalized, inv_std = normalize(x_ref[rows, pl.ds(0, D)])
-        d_normed = dn_ref[rows, :]
+        rows = pl.ds(k % 2 * CHUNK, CHUNK)
+        normalized, inv_std = normalize(xs[k // 2][rows, pl.ds(0, D)])
+        d_normed = dn_ref[pl.ds(k * CHUNK, CHUNK), :]
         gain_sum = gain_sum + jnp.sum(d_normed * normalized, axis=0, keepdims=True)
         d_hat = d_normed * gain
         first_mean = jnp.mean(d_hat, axis=-1, keepdims=True)
         second_mean = jnp.mean(d_hat * normalized, axis=-1, keepdims=True)
         out = inv_std * (d_hat - first_mean - normalized * second_mean)
-        outs[k][...] = out.astype(BF)
+        outs[k // 2][rows, :] = out.astype(BF)
     gain_out[...] = gain_sum
 
 
@@ -320,10 +347,43 @@
     )
 
 
-def exchange(rows):
-    blocks = rows.reshape(SLOTS, CHUNK, -1)
-    moved = lax.all_to_all(blocks, "seq", split_axis=0, concat_axis=0, tiled=True)
-    return moved.reshape(rows.shape)
+def swap_chips(chunks):
+    return [chunks[0]] + [swap_seq(chunks[j], 2 * j) for j in range(1, CHIPS)]
+
+
+def spread(rows, *clip, after=()):
+    width = D + 128 * len(clip)
+    mine, theirs = call(
+        split_body,
+        [shape((CHIPS, CHUNK, width), BF)] * 2,
+        in_specs=[VMEM] + [SMEM] * len(clip),
+        mib=8,
+        data=10**6,
+        name="split",
+    )(rows, *clip)
+    chunks = call(
+        merge_body,
+        [shape((PAIR, width), BF)] * CHIPS,
+        in_specs=[VMEM, VMEM] + [pl.BlockSpec(memory_space=pl.ANY)] * len(after),
+        mib=8,
+        data=10**6,
+        name="merge",
+    )(mine, swap_seq(theirs, 1), *after)
+    return swap_chips(chunks)
+
+
+def gather(chunks):
+    mine, theirs = call(
+        part_body,
+        [shape((CHIPS, CHUNK, D), BF)] * 2,
+        mib=8,
+        flops=2 * 10**10,
+        data=10**6,
+        name="part",
+    )(*swap_chips(chunks))
+    return call(join_body, shape((ROWS, D), BF), mib=8, data=10**6, name="join")(
+        mine, swap_seq(theirs, 1)
+    )
 
 
 def four(rank, dims):
@@ -334,22 +394,12 @@
     factor = 32768 ** (-0.5)
     gain = norm_gain.reshape(1, D)
 
-    packed = call(
-        pack_body,
-        shape((ROWS, WIDE), BF),
-        in_specs=[SMEM, VMEM],
-        mib=8,
-        data=10**6,
-        name="pack",
-    )(frame_clip, block_input.reshape(ROWS, D))
-    x = exchange(packed)
-    chunks = [shape((CHUNK, D), BF)] * SLOTS
-    sent = call(
-        split_body, chunks, in_specs=[pl.BlockSpec(memory_space=pl.ANY), VMEM], mib=8, data=10**6, name="split"
-    )(x, out_grad.reshape(ROWS, D))
-    grads = [sent[0]] + [swap_seq(sent[k], k) for k in range(1, SLOTS)]
-
-    normed = call(norm_body, shape((ROWS, D), BF), mib=8, data=10**6, name="norm")(x, gain)
+    x = spread(block_input.reshape(ROWS, D), frame_clip)
+    grads = spread(out_grad.reshape(ROWS, D), after=x[1:2])
+
+    normed, clips = call(
+        norm_body, [shape((ROWS, D), BF), shape((ROWS, 128), F32)], mib=8, data=10**6, name="norm"
+    )(*x, gain)
     nt, nt_sent = call(
         turn_body,
         [shape((D, ROWS), BF)] * 2,
@@ -376,7 +426,7 @@
         flops=5 * 10**9,
         data=40 * 10**6,
         name="project",
-    )(x, normed, qkv_weight)
+    )(clips, normed, qkv_weight)
 
     d_value, mine, theirs, grad_wide = call(
         value_body,
@@ -405,7 +455,7 @@
 
     results = call(
         input_body,
-        chunks + [shape((1, D), F32)],
+        [shape((PAIR, D), BF)] * CHIPS + [shape((1, D), F32)],
         scratch=[
             pltpu.VMEM((D, TRIPLE), BF),
             pltpu.VMEM((ROWS, WIDE), F32),
@@ -414,14 +464,13 @@
             pltpu.VMEM((ROWS, D), F32),
             pltpu.SemaphoreType.DMA((2, 3)),
         ],
-        in_specs=[VMEM] * 6 + [HBM],
+        in_specs=[VMEM] * (CHIPS + 5) + [HBM],
         mib=40,
         flops=6 * 10**9,
         data=20 * 10**6,
         name="input",
-    )(x, qkv, soft, grad_wide, d_value, gain, qkv_weight)
-    returned = [results[0]] + [swap_seq(results[k], k) for k in range(1, SLOTS)]
-    gain_term = results[SLOTS]
+    )(*x, qkv, soft, grad_wide, d_value, gain, qkv_weight)
+    returned, gain_term = results[:CHIPS], results[CHIPS]
     gains = [gain_term] + [swap_plane(gain_term, j) for j in range(1, 4)]
 
     sums = call(second_body, shape((16, 24, HALF), BF), mib=16, data=5 * 10**6, name="second")(
@@ -438,7 +487,7 @@
         data=10**5,
         name="last",
     )(mine, swap_seq(theirs, 1))
-    input_grad = call(join_body, shape((ROWS, D), BF), mib=8, data=10**6, name="join")(*returned)
+    input_grad = gather(returned)
     return input_grad.reshape(block_input.shape), weight_grad, gain_grad.reshape(D)
 
 

time: 96.1 us -> 85.1 us (0.89)
  blocking collectives: 17.9 us -> 0 us
  waiting for transfers between devices: 7.61 us -> 19.3 us
  starting transfers between devices: 41.8 us -> 35.9 us
  local copies, waits for them, and re-layouts: 1.12 us -> 2.22 us
    all_to_all x1 -> x0, blocking collectives: 17.9 us -> none  [exchange(): lax.all_to_all(blocks, 'seq', split_axis=0, concat_axis=0, tiled=True)]
    ppermute x17 -> x15, waiting for transfers between devices: 5.5 us -> 11.8 us  [swap_seq(): return lax.ppermute(value, 'seq', [(i, i ^ k) for i in range(SLOTS)])]
    ppermute x17 -> x15, starting transfers between devices: 26.3 us -> 20.2 us  [swap_seq(): return lax.ppermute(value, 'seq', [(i, i ^ k) for i in range(SLOTS)])]
    all_to_all x1, waiting for transfers between devices: 0.01 us -> 5.48 us  [exchange_plane(): lax.all_to_all(blocks, ('dp', 'seq'), split_axis=0, concat_axis=0, tiled=...]
    unnamed x6, local copies, waits for them, and re-layouts: 1.11 us -> 2.22 us
    pallas_call x5 -> x8, Pallas kernels: 11.8 us -> 11.7 us  [the longest x1 10 us: shards(): call(input_body, [shape((PAIR, D), BF)] * CHIPS + [shape((1, D), F32)], s...]
  transfers between devices with their start and end apart: 24 -> 22, of which waited for: 4 -> 8; matrix products, arithmetic and copies ran while one was open for 0% -> 0% of each run, Pallas kernels for 23% -> 27%
where the time goes in v2:
time: 85.1 us; the launch traced here: 84.8 us
  starting transfers between devices  35.9 us (42%)
  Pallas kernels  25.3 us (30%)
  waiting for transfers between devices  19.3 us (23%)
  local copies, waits for them, and re-layouts  2.22 us (3%)
  between operations  1.43 us (2%)
    ppermute x15, starting transfers between devices, swap_seq(): return lax.ppermute(value, 'seq', [(i, i ^ k) for i in range(SLOTS)])  20.2 us
    ppermute x15, waiting for transfers between devices, swap_seq(): return lax.ppermute(value, 'seq', [(i, i ^ k) for i in range(SLOTS)])  11.8 us
    ppermute x6, starting transfers between devices, swap_plane(): return lax.ppermute(value, ('dp', 'seq'), pairs)  10.5 us
    pallas_call x1, Pallas kernels, shards(): call(input_body, [shape((PAIR, D), BF)] * CHIPS + [shape((1, D), F32)], s...  10 us
    pallas_call x1, Pallas kernels, shards(): call(project_body, [shape((ROWS, PADDED), BF), shape((HEADS, ROWS, ROWS),...  8.84 us
    all_to_all x1, waiting for transfers between devices, exchange_plane(): lax.all_to_all(blocks, ('dp', 'seq'), split_axis=0, concat_axis=0, tiled=...  5.48 us
    all_to_all x1, starting transfers between devices, exchange_plane(): lax.all_to_all(blocks, ('dp', 'seq'), split_axis=0, concat_axis=0, tiled=...  5.24 us
    unnamed x6, local copies, waits for them, and re-layouts  2.22 us
  transfers between devices with their start and end apart: 22, of which 8 were waited for; matrix products, arithmetic and copies ran while one was open for 0% of the time, Pallas kernels for 27%

profile of v2, /device:TPU:1, one launch (start us, length us, event | category | flops | bytes accessed | tf_op | source)
XLA Modules:
  0.0 84.8 jit_solution(6836041212689963656)
XLA Ops:
  2.5 1.5 %collective-permute-start = (bf16[4,32,1536]{2,1,0:T(8,128)(2,1)S(1)}, bf16[4,32,1536]{2,1,0:T(8,128)(2,1)S(1)}, u32[]{:S(2)}, u32[]{:S(2)}) collective-permute-start(bf16[4,32,1536]{2,1,0:T(8,128)(2,1)S(1)} %get-tuple-element.42), channel_id=1, source_target_pairs={{0,1},{1,0},{2,3},{3,2},{4,5},{5,4},{6,7},{7,6},{8,9},{9,8},{10,11... | collective-permute-start | bytes 1179656 | tf_op jit(solution)/shard_map/ppermute | solution.py:328
  5.4 1.4 %collective-permute-start.1 = (bf16[64,1536]{1,0:T(8,128)(2,1)S(1)}, bf16[64,1536]{1,0:T(8,128)(2,1)S(1)}, u32[]{:S(2)}, u32[]{:S(2)}) collective-permute-start(bf16[64,1536]{1,0:T(8,128)(2,1)S(1)} %get-tuple-element.44), channel_id=1, source_target_pairs={{0,2},{1,3},{2,0},{3,1},{4,6},{5,7},{6,4},{7,5},{8,10},{9,11},{10,... | collective-permute-start | bytes 589832 | tf_op jit(solution)/shard_map/ppermute | solution.py:328
  6.8 2.5 %collective-permute-start.2 = (bf16[64,1536]{1,0:T(8,128)(2,1)S(1)}, bf16[64,1536]{1,0:T(8,128)(2,1)S(1)}, u32[]{:S(2)}, u32[]{:S(2)}) collective-permute-start(bf16[64,1536]{1,0:T(8,128)(2,1)S(1)} %get-tuple-element.45), channel_id=1, source_target_pairs={{0,4},{1,5},{2,6},{3,7},{4,0},{5,1},{6,2},{7,3},{8,12},{9,13},{10,... | collective-permute-start | bytes 589832 | tf_op jit(solution)/shard_map/ppermute | solution.py:328
  9.3 2.2 %collective-permute-done.1.refs_1_.refs_0_ = bf16[64,1536]{1,0:T(8,128)(2,1)S(1)} collective-permute-done((bf16[64,1536]{1,0:T(8,128)(2,1)S(1)}, bf16[64,1536]{1,0:T(8,128)(2,1)S(1)}, u32[]{:S(2)}, u32[]{:S(2)}) %collective-permute-start.1) | collective-permute-done | bytes 196640 | tf_op jit(solution)/shard_map/ppermute | solution.py:328
  11.6 1.4 %collective-permute-start.5 = (bf16[64,1408]{1,0:T(8,128)(2,1)S(1)}, bf16[64,1408]{1,0:T(8,128)(2,1)S(1)}, u32[]{:S(2)}, u32[]{:S(2)}) collective-permute-start(bf16[64,1408]{1,0:T(8,128)(2,1)S(1)} %get-tuple-element.55), channel_id=1, source_target_pairs={{0,2},{1,3},{2,0},{3,1},{4,6},{5,7},{6,4},{7,5},{8,10},{9,11},{10,... | collective-permute-start | bytes 540680 | tf_op jit(solution)/shard_map/ppermute | solution.py:328
  13.0 2.5 %collective-permute-start.6 = (bf16[64,1408]{1,0:T(8,128)(2,1)S(1)}, bf16[64,1408]{1,0:T(8,128)(2,1)S(1)}, u32[]{:S(2)}, u32[]{:S(2)}) collective-permute-start(bf16[64,1408]{1,0:T(8,128)(2,1)S(1)} %get-tuple-element.56), channel_id=1, source_target_pairs={{0,4},{1,5},{2,6},{3,7},{4,0},{5,1},{6,2},{7,3},{8,12},{9,13},{10,... | collective-permute-start | bytes 540680 | tf_op jit(solution)/shard_map/ppermute | solution.py:328
  15.5 2.5 %collective-permute-done.2.refs_2_ = bf16[64,1536]{1,0:T(8,128)(2,1)S(1)} collective-permute-done((bf16[64,1536]{1,0:T(8,128)(2,1)S(1)}, bf16[64,1536]{1,0:T(8,128)(2,1)S(1)}, u32[]{:S(2)}, u32[]{:S(2)}) %collective-permute-start.2) | collective-permute-done | bytes 196640 | tf_op jit(solution)/shard_map/ppermute | solution.py:328
  18.1 2.4 %collective-permute-done.3.refs_3_ = bf16[64,1536]{1,0:T(8,128)(2,1)S(1)} collective-permute-done((bf16[64,1536]{1,0:T(8,128)(2,1)S(1)}, bf16[64,1536]{1,0:T(8,128)(2,1)S(1)}, u32[]{:S(2)}, u32[]{:S(2)}) %collective-permute-start.3) | collective-permute-done | bytes 196640 | tf_op jit(solution)/shard_map/ppermute | solution.py:328
  21.6 3.4 %collective-permute-start.12 = (bf16[1408,256]{1,0:T(8,128)(2,1)S(1)}, bf16[1408,256]{1,0:T(8,128)(2,1)S(1)}, u32[]{:S(2)}, u32[]{:S(2)}) collective-permute-start(bf16[1408,256]{1,0:T(8,128)(2,1)S(1)} %get-tuple-element.67), channel_id=1, source_target_pairs={{0,1},{1,0},{2,3},{3,2},{4,5},{5,4},{6,7},{7,6},{8,9},{9,8},{10,11... | collective-permute-start | bytes 2162696 | tf_op jit(solution)/shard_map/ppermute | solution.py:328
  25.0 8.8 %project.1 = (bf16[256,4352]{1,0:T(8,128)(2,1)S(1)}, f32[16,256,256]{2,1,0:T(8,128)S(1)}, bf16[16,256,256]{2,1,0:T(8,128)(2,1)S(1)}) custom-call(f32[256,128]{1,0:T(8,128)S(1)} %get-tuple-element.47.clip_ref, bf16[256,1408]{1,0:T(8,128)(2,1)S(1)} %get-tuple-element.48.normed_ref, bf16[1408,4224]{1,0:T(8,128)(2,1)} %refs_9_.1), custom_call_target="tpu_custom_call" | custom-call | flops 5000000000 | bytes 40000000 | tf_op jit(solution)/shard_map/project/pallas_call | solution.py:412
  35.0 1.7 %collective-permute-done.13.dv_other_ref = bf16[256,768]{1,0:T(8,128)(2,1)S(1)} collective-permute-done((bf16[256,768]{1,0:T(8,128)(2,1)S(1)}, bf16[256,768]{1,0:T(8,128)(2,1)S(1)}, u32[]{:S(2)}, u32[]{:S(2)}) %collective-permute-start.13) | collective-permute-done | bytes 393248 | tf_op jit(solution)/shard_map/ppermute | solution.py:328
  36.8 1.3 %weight.1 = (f32[352,768]{1,0:T(8,128)S(1)}, bf16[352,768]{1,0:T(8,128)(2,1)S(1)}, bf16[352,768]{1,0:T(8,128)(2,1)S(1)}, bf16[352,768]{1,0:T(8,128)(2,1)S(1)}) custom-call(bf16[1408,256]{1,0:T(8,128)(2,1)S(1)} %get-tuple-element.66.nt_ref, bf16[1408,256]{1,0:T(8,128)(2,1)S(1)} %collective-permute-done.12.nt_other_ref, ...), custom_call_target="tpu_custom_call" | custom-call | flops 1100000000 | bytes 6000000 | tf_op jit(solution)/shard_map/weight/pallas_call | solution.py:446
  38.0 1.7 %collective-permute-start.14 = (bf16[352,768]{1,0:T(8,128)(2,1)S(1)}, bf16[352,768]{1,0:T(8,128)(2,1)S(1)}, u32[]{:S(2)}, u32[]{:S(2)}) collective-permute-start(bf16[352,768]{1,0:T(8,128)(2,1)S(1)} %get-tuple-element.71), channel_id=1, source_target_pairs={{0,32},{1,9},{2,34},{3,11},{4,36},{5,13},{6,38},{7,15},{8,40},{9,1... | collective-permute-start | bytes 1622024 | tf_op jit(solution)/shard_map/ppermute | solution.py:336
  39.8 3.3 %collective-permute-start.15 = (bf16[352,768]{1,0:T(8,128)(2,1)S(1)}, bf16[352,768]{1,0:T(8,128)(2,1)S(1)}, u32[]{:S(2)}, u32[]{:S(2)}) collective-permute-start(bf16[352,768]{1,0:T(8,128)(2,1)S(1)} %get-tuple-element.72), channel_id=1, source_target_pairs={{0,64},{1,17},{2,66},{3,19},{4,68},{5,21},{6,70},{7,23},{8,72},{9,... | collective-permute-start | bytes 1622024 | tf_op jit(solution)/shard_map/ppermute | solution.py:336
  43.1 10.0 %input.1 = (bf16[64,1408]{1,0:T(8,128)(2,1)S(1)}, bf16[64,1408]{1,0:T(8,128)(2,1)S(1)}, bf16[64,1408]{1,0:T(8,128)(2,1)S(1)}, bf16[64,1408]{1,0:T(8,128)(2,1)S(1)}, f32[1,1408]{1,0:T(1,128)S(1)}) custom-call(bf16[64,1536]{1,0:T(8,128)(2,1)S(1)} %get-tuple-element.43.refs_0_, bf16[64,1536]{1,0:T(8,128)(2,1)S(1)} %collective-permute-done.1.refs_1_.refs_0_, ...), custom_call_target="tpu_custom_call" | custom-call | flops 6000000000 | bytes 20000000 | tf_op jit(solution)/shard_map/input/pallas_call | solution.py:456
  53.2 3.8 %collective-permute-start.18 = (f32[1,1408]{1,0:T(1,128)S(1)}, f32[1,1408]{1,0:T(1,128)S(1)}, u32[]{:S(2)}, u32[]{:S(2)}) collective-permute-start(f32[1,1408]{1,0:T(1,128)S(1)} %get-tuple-element.74.refs_4_), channel_id=1, source_target_pairs={{0,64},{1,17},{2,66},{3,19},{4,68},{5,21},{6,70},{7,23},{8,72},{9,... | collective-permute-start | bytes 16904 | tf_op jit(solution)/shard_map/ppermute | solution.py:336
  57.1 1.6 %collective-permute-start.19 = (f32[1,1408]{1,0:T(1,128)S(1)}, f32[1,1408]{1,0:T(1,128)S(1)}, u32[]{:S(2)}, u32[]{:S(2)}) collective-permute-start(f32[1,1408]{1,0:T(1,128)S(1)} %get-tuple-element.74.refs_4_), channel_id=1, source_target_pairs={{0,96},{1,25},{2,98},{3,27},{4,100},{5,29},{6,102},{7,31},{8,104},... | collective-permute-start | bytes 16904 | tf_op jit(solution)/shard_map/ppermute | solution.py:336
  58.6 2.1 %collective-permute-done.19.refs_7_ = f32[1,1408]{1,0:T(1,128)S(1)} collective-permute-done((f32[1,1408]{1,0:T(1,128)S(1)}, f32[1,1408]{1,0:T(1,128)S(1)}, u32[]{:S(2)}, u32[]{:S(2)}) %collective-permute-start.19) | collective-permute-done | bytes 5664 | tf_op jit(solution)/shard_map/ppermute | solution.py:336
  60.7 1.8 %collective-permute-start.10 = (bf16[64,1408]{1,0:T(8,128)(2,1)S(1)}, bf16[64,1408]{1,0:T(8,128)(2,1)S(1)}, u32[]{:S(2)}, u32[]{:S(2)}) collective-permute-start(bf16[64,1408]{1,0:T(8,128)(2,1)S(1)} %get-tuple-element.63), channel_id=1, source_target_pairs={{0,6},{1,7},{2,4},{3,5},{4,2},{5,3},{6,0},{7,1},{8,14},{9,15},{10,... | collective-permute-start | bytes 540680 | tf_op jit(solution)/shard_map/ppermute | solution.py:328
  63.6 5.2 %all-to-all-start = ((bf16[16,24,768]{2,1,0:T(8,128)(2,1)}), bf16[16,24,768]{2,1,0:T(8,128)(2,1)S(1)}, u32[]{:S(2)}, u32[]{:S(2)}) async-start(bf16[16,24,768]{2,1,0:T(8,128)(2,1)} %second.1), calls=%async_computation | async-start | bytes 1179648 | tf_op jit(solution)/shard_map/all_to_all | solution.py:345
  68.9 2.9 %collective-permute-done.10.refs_3_ = bf16[64,1408]{1,0:T(8,128)(2,1)S(1)} collective-permute-done((bf16[64,1408]{1,0:T(8,128)(2,1)S(1)}, bf16[64,1408]{1,0:T(8,128)(2,1)S(1)}, u32[]{:S(2)}, u32[]{:S(2)}) %collective-permute-start.10) | collective-permute-done | bytes 180256 | tf_op jit(solution)/shard_map/ppermute | solution.py:328
  71.8 1.2 %collective-permute-start.11 = (bf16[4,32,1408]{2,1,0:T(8,128)(2,1)S(1)}, bf16[4,32,1408]{2,1,0:T(8,128)(2,1)S(1)}, u32[]{:S(2)}, u32[]{:S(2)}) collective-permute-start(bf16[4,32,1408]{2,1,0:T(8,128)(2,1)S(1)} %get-tuple-element.65), channel_id=1, source_target_pairs={{0,1},{1,0},{2,3},{3,2},{4,5},{5,4},{6,7},{7,6},{8,9},{9,8},{10,11... | collective-permute-start | bytes 1081352 | tf_op jit(solution)/shard_map/ppermute | solution.py:328
  73.0 5.5 %all-to-all-done.parts_ref = bf16[16,24,768]{2,1,0:T(8,128)(2,1)S(1)} async-done(((bf16[16,24,768]{2,1,0:T(8,128)(2,1)}), bf16[16,24,768]{2,1,0:T(8,128)(2,1)S(1)}, u32[]{:S(2)}, u32[]{:S(2)}) %all-to-all-start) | async-done | bytes 589856 | tf_op jit(solution)/shard_map/all_to_all | solution.py:345
  78.6 4.1 %collective-permute-start.20 = (f32[16,768]{1,0:T(8,128)S(1)}, f32[16,768]{1,0:T(8,128)S(1)}, u32[]{:S(2)}, u32[]{:S(2)}) collective-permute-start(f32[16,768]{1,0:T(8,128)S(1)} %get-tuple-element.76), channel_id=1, source_target_pairs={{0,1},{1,0},{2,3},{3,2},{4,5},{5,4},{6,7},{7,6},{8,9},{9,8},{10,11... | collective-permute-start | bytes 147464 | tf_op jit(solution)/shard_map/ppermute | solution.py:328
  (43 shorter events, 8.7 us)
Async XLA Ops:
  1.3 1.1 %copy-start = (bf16[1,1,256,1408]{3,2,1,0:T(8,128)(2,1)S(1)}, bf16[1,1,256,1408]{3,2,1,0:T(8,128)(2,1)}, u32[]{:S(2)}) copy-start(bf16[1,1,256,1408]{3,2,1,0:T(8,128)(2,1)} %param.5) | copy-start | bytes 2162692
  2.4 6.9 %copy-start.2 = (f32[1408]{0:T(1024)S(1)}, f32[1408]{0:T(1024)}, u32[]{:S(2)}) copy-start(f32[1408]{0:T(1024)} %param.6) | copy-start | bytes 16900
  2.5 2.9 %collective-permute-start = (bf16[4,32,1536]{2,1,0:T(8,128)(2,1)S(1)}, bf16[4,32,1536]{2,1,0:T(8,128)(2,1)S(1)}, u32[]{:S(2)}, u32[]{:S(2)}) collective-permute-start(bf16[4,32,1536]{2,1,0:T(8,128)(2,1)S(1)} %get-tuple-element.42), channel_id=1, source_target_pairs={{0,1},{1,0},{2,3},{3,2},{4,5},{5,4},{6,7},{7,6},{8,9},{9,8},{10,11... | collective-permute-start | bytes 1179656 | tf_op jit(solution)/shard_map/ppermute | solution.py:328
  5.1 4.2 %collective-permute-start.4 = (bf16[4,32,1408]{2,1,0:T(8,128)(2,1)S(1)}, bf16[4,32,1408]{2,1,0:T(8,128)(2,1)S(1)}, u32[]{:S(2)}, u32[]{:S(2)}) collective-permute-start(bf16[4,32,1408]{2,1,0:T(8,128)(2,1)S(1)} %get-tuple-element.53), channel_id=1, source_target_pairs={{0,1},{1,0},{2,3},{3,2},{4,5},{5,4},{6,7},{7,6},{8,9},{9,8},{10,11... | collective-permute-start | bytes 1081352 | tf_op jit(solution)/shard_map/ppermute | solution.py:328
  5.4 6.2 %collective-permute-start.1 = (bf16[64,1536]{1,0:T(8,128)(2,1)S(1)}, bf16[64,1536]{1,0:T(8,128)(2,1)S(1)}, u32[]{:S(2)}, u32[]{:S(2)}) collective-permute-start(bf16[64,1536]{1,0:T(8,128)(2,1)S(1)} %get-tuple-element.44), channel_id=1, source_target_pairs={{0,2},{1,3},{2,0},{3,1},{4,6},{5,7},{6,4},{7,5},{8,10},{9,11},{10,... | collective-permute-start | bytes 589832 | tf_op jit(solution)/shard_map/ppermute | solution.py:328
  6.8 11.3 %collective-permute-start.2 = (bf16[64,1536]{1,0:T(8,128)(2,1)S(1)}, bf16[64,1536]{1,0:T(8,128)(2,1)S(1)}, u32[]{:S(2)}, u32[]{:S(2)}) collective-permute-start(bf16[64,1536]{1,0:T(8,128)(2,1)S(1)} %get-tuple-element.45), channel_id=1, source_target_pairs={{0,4},{1,5},{2,6},{3,7},{4,0},{5,1},{6,2},{7,3},{8,12},{9,13},{10,... | collective-permute-start | bytes 589832 | tf_op jit(solution)/shard_map/ppermute | solution.py:328
  9.2 11.2 %collective-permute-start.3 = (bf16[64,1536]{1,0:T(8,128)(2,1)S(1)}, bf16[64,1536]{1,0:T(8,128)(2,1)S(1)}, u32[]{:S(2)}, u32[]{:S(2)}) collective-permute-start(bf16[64,1536]{1,0:T(8,128)(2,1)S(1)} %get-tuple-element.46), channel_id=1, source_target_pairs={{0,6},{1,7},{2,4},{3,5},{4,2},{5,3},{6,0},{7,1},{8,14},{9,15},{10,... | collective-permute-start | bytes 589832 | tf_op jit(solution)/shard_map/ppermute | solution.py:328
  11.6 22.3 %collective-permute-start.5 = (bf16[64,1408]{1,0:T(8,128)(2,1)S(1)}, bf16[64,1408]{1,0:T(8,128)(2,1)S(1)}, u32[]{:S(2)}, u32[]{:S(2)}) collective-permute-start(bf16[64,1408]{1,0:T(8,128)(2,1)S(1)} %get-tuple-element.55), channel_id=1, source_target_pairs={{0,2},{1,3},{2,0},{3,1},{4,6},{5,7},{6,4},{7,5},{8,10},{9,11},{10,... | collective-permute-start | bytes 540680 | tf_op jit(solution)/shard_map/ppermute | solution.py:328
  13.0 20.9 %collective-permute-start.6 = (bf16[64,1408]{1,0:T(8,128)(2,1)S(1)}, bf16[64,1408]{1,0:T(8,128)(2,1)S(1)}, u32[]{:S(2)}, u32[]{:S(2)}) collective-permute-start(bf16[64,1408]{1,0:T(8,128)(2,1)S(1)} %get-tuple-element.56), channel_id=1, source_target_pairs={{0,4},{1,5},{2,6},{3,7},{4,0},{5,1},{6,2},{7,3},{8,12},{9,13},{10,... | collective-permute-start | bytes 540680 | tf_op jit(solution)/shard_map/ppermute | solution.py:328
  15.4 18.4 %collective-permute-start.7 = (bf16[64,1408]{1,0:T(8,128)(2,1)S(1)}, bf16[64,1408]{1,0:T(8,128)(2,1)S(1)}, u32[]{:S(2)}, u32[]{:S(2)}) collective-permute-start(bf16[64,1408]{1,0:T(8,128)(2,1)S(1)} %get-tuple-element.57), channel_id=1, source_target_pairs={{0,6},{1,7},{2,4},{3,5},{4,2},{5,3},{6,0},{7,1},{8,14},{9,15},{10,... | collective-permute-start | bytes 540680 | tf_op jit(solution)/shard_map/ppermute | solution.py:328
  21.6 15.2 %collective-permute-start.12 = (bf16[1408,256]{1,0:T(8,128)(2,1)S(1)}, bf16[1408,256]{1,0:T(8,128)(2,1)S(1)}, u32[]{:S(2)}, u32[]{:S(2)}) collective-permute-start(bf16[1408,256]{1,0:T(8,128)(2,1)S(1)} %get-tuple-element.67), channel_id=1, source_target_pairs={{0,1},{1,0},{2,3},{3,2},{4,5},{5,4},{6,7},{7,6},{8,9},{9,8},{10,11... | collective-permute-start | bytes 2162696 | tf_op jit(solution)/shard_map/ppermute | solution.py:328
  34.8 2.0 %collective-permute-start.13 = (bf16[256,768]{1,0:T(8,128)(2,1)S(1)}, bf16[256,768]{1,0:T(8,128)(2,1)S(1)}, u32[]{:S(2)}, u32[]{:S(2)}) collective-permute-start(bf16[256,768]{1,0:T(8,128)(2,1)S(1)} %get-tuple-element.69), channel_id=1, source_target_pairs={{0,1},{1,0},{2,3},{3,2},{4,5},{5,4},{6,7},{7,6},{8,9},{9,8},{10,11... | collective-permute-start | bytes 1179656 | tf_op jit(solution)/shard_map/ppermute | solution.py:328
  38.0 22.7 %collective-permute-start.14 = (bf16[352,768]{1,0:T(8,128)(2,1)S(1)}, bf16[352,768]{1,0:T(8,128)(2,1)S(1)}, u32[]{:S(2)}, u32[]{:S(2)}) collective-permute-start(bf16[352,768]{1,0:T(8,128)(2,1)S(1)} %get-tuple-element.71), channel_id=1, source_target_pairs={{0,32},{1,9},{2,34},{3,11},{4,36},{5,13},{6,38},{7,15},{8,40},{9,1... | collective-permute-start | bytes 1622024 | tf_op jit(solution)/shard_map/ppermute | solution.py:336
  39.8 22.8 %collective-permute-start.15 = (bf16[352,768]{1,0:T(8,128)(2,1)S(1)}, bf16[352,768]{1,0:T(8,128)(2,1)S(1)}, u32[]{:S(2)}, u32[]{:S(2)}) collective-permute-start(bf16[352,768]{1,0:T(8,128)(2,1)S(1)} %get-tuple-element.72), channel_id=1, source_target_pairs={{0,64},{1,17},{2,66},{3,19},{4,68},{5,21},{6,70},{7,23},{8,72},{9,... | collective-permute-start | bytes 1622024 | tf_op jit(solution)/shard_map/ppermute | solution.py:336
  43.1 19.5 %collective-permute-start.16 = (bf16[352,768]{1,0:T(8,128)(2,1)S(1)}, bf16[352,768]{1,0:T(8,128)(2,1)S(1)}, u32[]{:S(2)}, u32[]{:S(2)}) collective-permute-start(bf16[352,768]{1,0:T(8,128)(2,1)S(1)} %get-tuple-element.73), channel_id=1, source_target_pairs={{0,96},{1,25},{2,98},{3,27},{4,100},{5,29},{6,102},{7,31},{8,104},... | collective-permute-start | bytes 1622024 | tf_op jit(solution)/shard_map/ppermute | solution.py:336
  53.1 3.9 %collective-permute-start.17 = (f32[1,1408]{1,0:T(1,128)S(1)}, f32[1,1408]{1,0:T(1,128)S(1)}, u32[]{:S(2)}, u32[]{:S(2)}) collective-permute-start(f32[1,1408]{1,0:T(1,128)S(1)} %get-tuple-element.74.refs_4_), channel_id=1, source_target_pairs={{0,32},{1,9},{2,34},{3,11},{4,36},{5,13},{6,38},{7,15},{8,40},{9,1... | collective-permute-start | bytes 16904 | tf_op jit(solution)/shard_map/ppermute | solution.py:336
  53.2 5.4 %collective-permute-start.18 = (f32[1,1408]{1,0:T(1,128)S(1)}, f32[1,1408]{1,0:T(1,128)S(1)}, u32[]{:S(2)}, u32[]{:S(2)}) collective-permute-start(f32[1,1408]{1,0:T(1,128)S(1)} %get-tuple-element.74.refs_4_), channel_id=1, source_target_pairs={{0,64},{1,17},{2,66},{3,19},{4,68},{5,21},{6,70},{7,23},{8,72},{9,... | collective-permute-start | bytes 16904 | tf_op jit(solution)/shard_map/ppermute | solution.py:336
  57.1 3.7 %collective-permute-start.19 = (f32[1,1408]{1,0:T(1,128)S(1)}, f32[1,1408]{1,0:T(1,128)S(1)}, u32[]{:S(2)}, u32[]{:S(2)}) collective-permute-start(f32[1,1408]{1,0:T(1,128)S(1)} %get-tuple-element.74.refs_4_), channel_id=1, source_target_pairs={{0,96},{1,25},{2,98},{3,27},{4,100},{5,29},{6,102},{7,31},{8,104},... | collective-permute-start | bytes 16904 | tf_op jit(solution)/shard_map/ppermute | solution.py:336
  58.6 10.3 %collective-permute-start.8 = (bf16[64,1408]{1,0:T(8,128)(2,1)S(1)}, bf16[64,1408]{1,0:T(8,128)(2,1)S(1)}, u32[]{:S(2)}, u32[]{:S(2)}) collective-permute-start(bf16[64,1408]{1,0:T(8,128)(2,1)S(1)} %get-tuple-element.61), channel_id=1, source_target_pairs={{0,2},{1,3},{2,0},{3,1},{4,6},{5,7},{6,4},{7,5},{8,10},{9,11},{10,... | collective-permute-start | bytes 540680 | tf_op jit(solution)/shard_map/ppermute | solution.py:328
  60.7 8.2 %collective-permute-start.9 = (bf16[64,1408]{1,0:T(8,128)(2,1)S(1)}, bf16[64,1408]{1,0:T(8,128)(2,1)S(1)}, u32[]{:S(2)}, u32[]{:S(2)}) collective-permute-start(bf16[64,1408]{1,0:T(8,128)(2,1)S(1)} %get-tuple-element.62), channel_id=1, source_target_pairs={{0,4},{1,5},{2,6},{3,7},{4,0},{5,1},{6,2},{7,3},{8,12},{9,13},{10,... | collective-permute-start | bytes 540680 | tf_op jit(solution)/shard_map/ppermute | solution.py:328
  60.7 11.0 %collective-permute-start.10 = (bf16[64,1408]{1,0:T(8,128)(2,1)S(1)}, bf16[64,1408]{1,0:T(8,128)(2,1)S(1)}, u32[]{:S(2)}, u32[]{:S(2)}) collective-permute-start(bf16[64,1408]{1,0:T(8,128)(2,1)S(1)} %get-tuple-element.63), channel_id=1, source_target_pairs={{0,6},{1,7},{2,4},{3,5},{4,2},{5,3},{6,0},{7,1},{8,14},{9,15},{10,... | collective-permute-start | bytes 540680 | tf_op jit(solution)/shard_map/ppermute | solution.py:328
  63.6 14.8 %all-to-all-start = ((bf16[16,24,768]{2,1,0:T(8,128)(2,1)}), bf16[16,24,768]{2,1,0:T(8,128)(2,1)S(1)}, u32[]{:S(2)}, u32[]{:S(2)}) async-start(bf16[16,24,768]{2,1,0:T(8,128)(2,1)} %second.1), calls=%async_computation | async-start | bytes 1179648 | tf_op jit(solution)/shard_map/all_to_all | solution.py:345
  71.8 10.8 %collective-permute-start.11 = (bf16[4,32,1408]{2,1,0:T(8,128)(2,1)S(1)}, bf16[4,32,1408]{2,1,0:T(8,128)(2,1)S(1)}, u32[]{:S(2)}, u32[]{:S(2)}) collective-permute-start(bf16[4,32,1408]{2,1,0:T(8,128)(2,1)S(1)} %get-tuple-element.65), channel_id=1, source_target_pairs={{0,1},{1,0},{2,3},{3,2},{4,5},{5,4},{6,7},{7,6},{8,9},{9,8},{10,11... | collective-permute-start | bytes 1081352 | tf_op jit(solution)/shard_map/ppermute | solution.py:328
  78.6 5.0 %collective-permute-start.20 = (f32[16,768]{1,0:T(8,128)S(1)}, f32[16,768]{1,0:T(8,128)S(1)}, u32[]{:S(2)}, u32[]{:S(2)}) collective-permute-start(f32[16,768]{1,0:T(8,128)S(1)} %get-tuple-element.76), channel_id=1, source_target_pairs={{0,1},{1,0},{2,3},{3,2},{4,5},{5,4},{6,7},{7,6},{8,9},{9,8},{10,11... | collective-permute-start | bytes 147464 | tf_op jit(solution)/shard_map/ppermute | solution.py:328
  (1 other events, 1.1 us)

commit v3 on v2

--- a/solution.py
+++ b/solution.py
@@ -112,8 +112,14 @@
         out_ref[part_rows(chip ^ j, 1 - core), :] = other_ref[j]
 
 
+def load_body(w_hbm, w_ref, sem):
+    copy = pltpu.make_async_copy(w_hbm, w_ref, sem)
+    copy.start()
+    copy.wait()
+
+
 def norm_body(*refs):
-    xs, (gain_ref, normed_ref, clip_ref) = refs[:CHIPS], refs[CHIPS:]
+    xs, (gain_ref, _, normed_ref, clip_ref) = refs[:CHIPS], refs[CHIPS:]
     for j in range(CHIPS):
         rows = pl.ds(j * PAIR, PAIR)
         normalized, _ = normalize(xs[j][:, pl.ds(0, D)])
@@ -138,22 +144,14 @@
     theirs_ref[...] = other_ref[...].astype(BF)
 
 
-def project_body(clip_ref, normed_ref, w_hbm, qkv_ref, soft_ref, prob_ref, wbuf, bias_ref, sems):
+def project_body(clip_ref, normed_ref, wbuf, qkv_ref, soft_ref, prob_ref, bias_ref):
     first = [(0, 512), (512, 1152), (1664, 1152)]
     rest = [(2816, 384), (3200, 384), (3584, 384), (3968, 256)]
 
-    def fetch(i, start, count):
+    def project(start, count):
         cols = pl.ds(start, count)
-        return pltpu.make_async_copy(w_hbm.at[:, cols], wbuf.at[:, cols], sems.at[i])
-
-    def project(i, start, count):
-        cols = pl.ds(start, count)
-        fetch(i, start, count).wait()
         out = jnp.dot(normed_ref[...], wbuf[:, cols], preferred_element_type=F32)
         qkv_ref[:, cols] = out.astype(BF)
-
-    for i, (start, count) in enumerate(first + rest):
-        fetch(i, start, count).start()
 
     row = lax.broadcasted_iota(jnp.int32, (ROWS, ROWS), 0)
     col = lax.broadcasted_iota(jnp.int32, (ROWS, ROWS), 1)
@@ -163,8 +161,8 @@
     bias_ref[...] = jnp.where(kept, 0.0, MASKED).astype(F32)
     qkv_ref[:, pl.ds(TRIPLE, 128)] = jnp.zeros((ROWS, 128), BF)
 
-    for i, (start, count) in enumerate(first):
-        project(i, start, count)
+    for start, count in first:
+        project(start, count)
 
     def attend(head):
         start, lanes = head_window(head)
@@ -181,7 +179,7 @@
     for head in range(HEADS):
         attend(head)
         if head % 4 == 3:
-            project(len(first) + head // 4, *rest[head // 4])
+            project(*rest[head // 4])
 
 
 def value_body(prob_ref, *refs):
@@ -252,27 +250,20 @@
         gain = (first + second)[11:13]
         out_ref[:, pl.ds(0, HALF)] = first[:11]
         out_ref[:, pl.ds(HALF, D - HALF)] = second[:11, 2 * HALF - D :]
-        gain_ref[:, pl.ds(0, HALF)] = gain[0:1]
-        gain_ref[:, pl.ds(HALF, D - HALF)] = gain[1:2, : D - HALF]
+        gain_ref[pl.ds(0, HALF)] = gain[0]
+        gain_ref[pl.ds(HALF, D - HALF)] = gain[1, : D - HALF]
 
     return body
 
 
 def input_body(*refs):
     xs, refs = refs[:CHIPS], refs[CHIPS:]
-    qkv_ref, soft_ref, grad_ref, dv_ref, gain_ref, w_hbm = refs[:6]
+    qkv_ref, soft_ref, grad_ref, dv_ref, gain_ref, wbuf = refs[:6]
     outs, gain_out = refs[6 : 6 + CHIPS], refs[6 + CHIPS]
-    wbuf, dq_ref, dk_ref, g_ref, dn_ref, sems = refs[7 + CHIPS :]
+    dq_ref, dk_ref, g_ref, dn_ref = refs[7 + CHIPS :]
     tiles = [(0, 512), (512, 512), (1024, 384)]
     parts = [pl.ds(2 * D, D), pl.ds(0, 2 * D)]
 
-    def fetch(part, i):
-        at = pl.ds(*tiles[i]), parts[part]
-        return pltpu.make_async_copy(w_hbm.at[at], wbuf.at[at], sems.at[part, i])
-
-    for part in range(2):
-        for i in range(len(tiles)):
-            fetch(part, i).start()
     dq_ref[...] = jnp.zeros_like(dq_ref)
     dk_ref[...] = jnp.zeros_like(dk_ref)
     across = (((1,), (1,)), ((), ()))
@@ -295,17 +286,14 @@
     for head in range(HEADS):
         one(head)
         if head % 4 == 3 and head < 15:
-            i = head // 4
-            fetch(0, i).wait()
-            rows = pl.ds(*tiles[i])
+            rows = pl.ds(*tiles[head // 4])
             dn_ref[:, rows] = lax.dot_general(
                 dv_ref[...], wbuf[rows, parts[0]], across, preferred_element_type=F32
             )
     g_ref[:, pl.ds(0, D)] = dq_ref[:, pl.ds(0, D)].astype(BF)
     g_ref[:, pl.ds(D, D)] = dk_ref[:, pl.ds(0, D)].astype(BF)
-    for i in range(len(tiles)):
-        fetch(1, i).wait()
-        rows = pl.ds(*tiles[i])
+    for tile in tiles:
+        rows = pl.ds(*tile)
         dn_ref[:, rows] += lax.dot_general(
             g_ref[...], wbuf[rows, parts[1]], across, preferred_element_type=F32
         )
@@ -397,9 +385,23 @@
     x = spread(block_input.reshape(ROWS, D), frame_clip)
     grads = spread(out_grad.reshape(ROWS, D), after=x[1:2])
 
+    weight = call(
+        load_body,
+        shape((D, TRIPLE), BF),
+        scratch=[pltpu.SemaphoreType.DMA(())],
+        in_specs=[HBM],
+        mib=2,
+        data=24 * 10**6,
+        name="load",
+    )(qkv_weight)
     normed, clips = call(
-        norm_body, [shape((ROWS, D), BF), shape((ROWS, 128), F32)], mib=8, data=10**6, name="norm"
-    )(*x, gain)
+        norm_body,
+        [shape((ROWS, D), BF), shape((ROWS, 128), F32)],
+        in_specs=[VMEM] * (CHIPS + 1) + [pl.BlockSpec(memory_space=pl.ANY)],
+        mib=8,
+        data=10**6,
+        name="norm",
+    )(*x, gain, weight)
     nt, nt_sent = call(
         turn_body,
         [shape((D, ROWS), BF)] * 2,
@@ -417,16 +419,13 @@
             shape((HEADS, ROWS, ROWS), BF),
         ],
         scratch=[
-            pltpu.VMEM((D, TRIPLE), BF),
             pltpu.VMEM((ROWS, ROWS), F32),
-            pltpu.SemaphoreType.DMA((7,)),
         ],
-        in_specs=[VMEM, VMEM, HBM],
-        mib=40,
+        mib=16,
         flops=5 * 10**9,
         data=40 * 10**6,
         name="project",
-    )(clips, normed, qkv_weight)
+    )(clips, normed, weight)
 
     d_value, mine, theirs, grad_wide = call(
         value_body,
@@ -457,19 +456,16 @@
         input_body,
         [shape((PAIR, D), BF)] * CHIPS + [shape((1, D), F32)],
         scratch=[
-            pltpu.VMEM((D, TRIPLE), BF),
             pltpu.VMEM((ROWS, WIDE), F32),
             pltpu.VMEM((ROWS, WIDE), F32),
             pltpu.VMEM((ROWS, 2 * D), BF),
             pltpu.VMEM((ROWS, D), F32),
-            pltpu.SemaphoreType.DMA((2, 3)),
         ],
-        in_specs=[VMEM] * (CHIPS + 5) + [HBM],
-        mib=40,
+        mib=16,
         flops=6 * 10**9,
         data=20 * 10**6,
         name="input",
-    )(*x, qkv, soft, grad_wide, d_value, gain, qkv_weight)
+    )(*x, qkv, soft, grad_wide, d_value, gain, weight)
     returned, gain_term = results[:CHIPS], results[CHIPS]
     gains = [gain_term] + [swap_plane(gain_term, j) for j in range(1, 4)]
 
@@ -482,13 +478,13 @@
     )
     weight_grad, gain_grad = call(
         last_body(factor),
-        [shape((11, D), F32), shape((1, D), F32)],
+        [shape((11, D), F32), shape((D,), F32)],
         mib=8,
         data=10**5,
         name="last",
     )(mine, swap_seq(theirs, 1))
     input_grad = gather(returned)
-    return input_grad.reshape(block_input.shape), weight_grad, gain_grad.reshape(D)
+    return input_grad.reshape(block_input.shape), weight_grad, gain_grad
 
 
 def solution(mesh):

time: 85.1 us -> 79.4 us (0.933)
  waiting for transfers between devices: 19.3 us -> 13.9 us
  local copies, waits for them, and re-layouts: 2.22 us -> 7.29 us
  Pallas kernels: 25.3 us -> 20.9 us
    ppermute x15, waiting for transfers between devices: 11.8 us -> 6.5 us  [swap_seq(): return lax.ppermute(value, 'seq', [(i, i ^ k) for i in range(SLOTS)])]
    unnamed x6, local copies, waits for them, and re-layouts: 2.22 us -> 6.59 us
    pallas_call x1, Pallas kernels: 8.84 us -> 5.56 us  [shards(): call(project_body, [shape((ROWS, PADDED), BF), shape((HEADS, ROWS, ROWS),...]
    pallas_call x1, Pallas kernels: 10 us -> 7.98 us  [shards(): call(input_body, [shape((PAIR, D), BF)] * CHIPS + [shape((1, D), F32)], s...]
    pallas_call x2 -> x3, Pallas kernels: 1.13 us -> 2.07 us  [the longest x1 0.94 us: shards(): call(load_body, shape((D, TRIPLE), BF), scratch=[pltpu.SemaphoreType.DMA(...]
  transfers between devices with their start and end apart: 22 -> 22, of which waited for: 8 -> 7; matrix products, arithmetic and copies ran while one was open for 0% -> 1% of each run, Pallas kernels for 27% -> 24%
where the time goes in v3:
time: 79.4 us; the launch traced here: 79 us
  starting transfers between devices  35.4 us (45%)
  Pallas kernels  20.9 us (26%)
  waiting for transfers between devices  13.9 us (18%)
  local copies, waits for them, and re-layouts  7.29 us (9%)
  between operations  1.45 us (2%)
    ppermute x15, starting transfers between devices, swap_seq(): return lax.ppermute(value, 'seq', [(i, i ^ k) for i in range(SLOTS)])  19.7 us
    ppermute x6, starting transfers between devices, swap_plane(): return lax.ppermute(value, ('dp', 'seq'), pairs)  10.5 us
    pallas_call x1, Pallas kernels, shards(): call(input_body, [shape((PAIR, D), BF)] * CHIPS + [shape((1, D), F32)], s...  7.98 us
    unnamed x6, local copies, waits for them, and re-layouts  6.59 us
    ppermute x15, waiting for transfers between devices, swap_seq(): return lax.ppermute(value, 'seq', [(i, i ^ k) for i in range(SLOTS)])  6.5 us
    pallas_call x1, Pallas kernels, shards(): call(project_body, [shape((ROWS, PADDED), BF), shape((HEADS, ROWS, ROWS),...  5.56 us
    all_to_all x1, starting transfers between devices, exchange_plane(): lax.all_to_all(blocks, ('dp', 'seq'), split_axis=0, concat_axis=0, tiled=...  5.23 us
    all_to_all x1, waiting for transfers between devices, exchange_plane(): lax.all_to_all(blocks, ('dp', 'seq'), split_axis=0, concat_axis=0, tiled=...  5.02 us
  transfers between devices with their start and end apart: 22, of which 7 were waited for; matrix products, arithmetic and copies ran while one was open for 1% of the time, Pallas kernels for 24%

profile of v3, /device:TPU:1, one launch (start us, length us, event | category | flops | bytes accessed | tf_op | source)
XLA Modules:
  0.0 79.0 jit_solution(14937381876486326962)
XLA Ops:
  1.3 1.1 %copy-done.1 = bf16[1,1,256,1408]{3,2,1,0:T(8,128)(2,1)S(1)} copy-done((bf16[1,1,256,1408]{3,2,1,0:T(8,128)(2,1)S(1)}, bf16[1,1,256,1408]{3,2,1,0:T(8,128)(2,1)}, u32[]{:S(2)}) %copy-start.1) | copy-done | bytes 720920
  2.5 1.5 %collective-permute-start = (bf16[4,32,1536]{2,1,0:T(8,128)(2,1)S(1)}, bf16[4,32,1536]{2,1,0:T(8,128)(2,1)S(1)}, u32[]{:S(2)}, u32[]{:S(2)}) collective-permute-start(bf16[4,32,1536]{2,1,0:T(8,128)(2,1)S(1)} %get-tuple-element.42), channel_id=1, source_target_pairs={{0,1},{1,0},{2,3},{3,2},{4,5},{5,4},{6,7},{7,6},{8,9},{9,8},{10,11... | collective-permute-start | bytes 1179656 | tf_op jit(solution)/shard_map/ppermute | solution.py:316
  4.0 1.1 %copy-done.2 = bf16[1,1,256,1408]{3,2,1,0:T(8,128)(2,1)S(1)} copy-done((bf16[1,1,256,1408]{3,2,1,0:T(8,128)(2,1)S(1)}, bf16[1,1,256,1408]{3,2,1,0:T(8,128)(2,1)}, u32[]{:S(2)}) %copy-start.2) | copy-done | bytes 720920
  5.4 1.4 %collective-permute-start.1 = (bf16[64,1536]{1,0:T(8,128)(2,1)S(1)}, bf16[64,1536]{1,0:T(8,128)(2,1)S(1)}, u32[]{:S(2)}, u32[]{:S(2)}) collective-permute-start(bf16[64,1536]{1,0:T(8,128)(2,1)S(1)} %get-tuple-element.44), channel_id=1, source_target_pairs={{0,2},{1,3},{2,0},{3,1},{4,6},{5,7},{6,4},{7,5},{8,10},{9,11},{10,... | collective-permute-start | bytes 589832 | tf_op jit(solution)/shard_map/ppermute | solution.py:316
  6.8 2.5 %collective-permute-start.2 = (bf16[64,1536]{1,0:T(8,128)(2,1)S(1)}, bf16[64,1536]{1,0:T(8,128)(2,1)S(1)}, u32[]{:S(2)}, u32[]{:S(2)}) collective-permute-start(bf16[64,1536]{1,0:T(8,128)(2,1)S(1)} %get-tuple-element.45), channel_id=1, source_target_pairs={{0,4},{1,5},{2,6},{3,7},{4,0},{5,1},{6,2},{7,3},{8,12},{9,13},{10,... | collective-permute-start | bytes 589832 | tf_op jit(solution)/shard_map/ppermute | solution.py:316
  10.0 4.4 %copy-done = bf16[1408,4224]{1,0:T(8,128)(2,1)S(1)} copy-done((bf16[1408,4224]{1,0:T(8,128)(2,1)S(1)}, bf16[1408,4224]{1,0:T(8,128)(2,1)}, u32[]{:S(2)}) %copy-start) | copy-done | bytes 11894808
  15.6 3.7 %collective-permute-start.6 = (bf16[64,1408]{1,0:T(8,128)(2,1)S(1)}, bf16[64,1408]{1,0:T(8,128)(2,1)S(1)}, u32[]{:S(2)}, u32[]{:S(2)}) collective-permute-start(bf16[64,1408]{1,0:T(8,128)(2,1)S(1)} %get-tuple-element.56), channel_id=1, source_target_pairs={{0,4},{1,5},{2,6},{3,7},{4,0},{5,1},{6,2},{7,3},{8,12},{9,13},{10,... | collective-permute-start | bytes 540680 | tf_op jit(solution)/shard_map/ppermute | solution.py:316
  21.6 1.6 %collective-permute-start.12 = (bf16[1408,256]{1,0:T(8,128)(2,1)S(1)}, bf16[1408,256]{1,0:T(8,128)(2,1)S(1)}, u32[]{:S(2)}, u32[]{:S(2)}) collective-permute-start(bf16[1408,256]{1,0:T(8,128)(2,1)S(1)} %get-tuple-element.67), channel_id=1, source_target_pairs={{0,1},{1,0},{2,3},{3,2},{4,5},{5,4},{6,7},{7,6},{8,9},{9,8},{10,11... | collective-permute-start | bytes 2162696 | tf_op jit(solution)/shard_map/ppermute | solution.py:316
  23.2 5.6 %project.1 = (bf16[256,4352]{1,0:T(8,128)(2,1)S(1)}, f32[16,256,256]{2,1,0:T(8,128)S(1)}, bf16[16,256,256]{2,1,0:T(8,128)(2,1)S(1)}) custom-call(f32[256,128]{1,0:T(8,128)S(1)} %get-tuple-element.47.clip_ref, bf16[256,1408]{1,0:T(8,128)(2,1)S(1)} %get-tuple-element.48.normed_ref, bf16[1408,4224]{1,0:T(8,128)(2,1)S(1)} %load.1.refs_5_.wbuf.refs_9_), custom_call_target="tpu_custom_call" | custom-call | flops 5000000000 | bytes 40000000 | tf_op jit(solution)/shard_map/project/pallas_call | solution.py:414
  30.3 1.7 %collective-permute-start.13 = (bf16[256,768]{1,0:T(8,128)(2,1)S(1)}, bf16[256,768]{1,0:T(8,128)(2,1)S(1)}, u32[]{:S(2)}, u32[]{:S(2)}) collective-permute-start(bf16[256,768]{1,0:T(8,128)(2,1)S(1)} %get-tuple-element.69), channel_id=1, source_target_pairs={{0,1},{1,0},{2,3},{3,2},{4,5},{5,4},{6,7},{7,6},{8,9},{9,8},{10,11... | collective-permute-start | bytes 1179656 | tf_op jit(solution)/shard_map/ppermute | solution.py:316
  32.0 1.3 %collective-permute-done.13.dv_other_ref = bf16[256,768]{1,0:T(8,128)(2,1)S(1)} collective-permute-done((bf16[256,768]{1,0:T(8,128)(2,1)S(1)}, bf16[256,768]{1,0:T(8,128)(2,1)S(1)}, u32[]{:S(2)}, u32[]{:S(2)}) %collective-permute-start.13) | collective-permute-done | bytes 393248 | tf_op jit(solution)/shard_map/ppermute | solution.py:316
  33.4 1.3 %weight.1 = (f32[352,768]{1,0:T(8,128)S(1)}, bf16[352,768]{1,0:T(8,128)(2,1)S(1)}, bf16[352,768]{1,0:T(8,128)(2,1)S(1)}, bf16[352,768]{1,0:T(8,128)(2,1)S(1)}) custom-call(bf16[1408,256]{1,0:T(8,128)(2,1)S(1)} %get-tuple-element.66.nt_ref, bf16[1408,256]{1,0:T(8,128)(2,1)S(1)} %collective-permute-done.12.nt_other_ref, ...), custom_call_target="tpu_custom_call" | custom-call | flops 1100000000 | bytes 6000000 | tf_op jit(solution)/shard_map/weight/pallas_call | solution.py:445
  34.7 1.7 %collective-permute-start.14 = (bf16[352,768]{1,0:T(8,128)(2,1)S(1)}, bf16[352,768]{1,0:T(8,128)(2,1)S(1)}, u32[]{:S(2)}, u32[]{:S(2)}) collective-permute-start(bf16[352,768]{1,0:T(8,128)(2,1)S(1)} %get-tuple-element.71), channel_id=1, source_target_pairs={{0,32},{1,9},{2,34},{3,11},{4,36},{5,13},{6,38},{7,15},{8,40},{9,1... | collective-permute-start | bytes 1622024 | tf_op jit(solution)/shard_map/ppermute | solution.py:324
  36.4 3.3 %collective-permute-start.15 = (bf16[352,768]{1,0:T(8,128)(2,1)S(1)}, bf16[352,768]{1,0:T(8,128)(2,1)S(1)}, u32[]{:S(2)}, u32[]{:S(2)}) collective-permute-start(bf16[352,768]{1,0:T(8,128)(2,1)S(1)} %get-tuple-element.72), channel_id=1, source_target_pairs={{0,64},{1,17},{2,66},{3,19},{4,68},{5,21},{6,70},{7,23},{8,72},{9,... | collective-permute-start | bytes 1622024 | tf_op jit(solution)/shard_map/ppermute | solution.py:324
  39.7 8.0 %input.1 = (bf16[64,1408]{1,0:T(8,128)(2,1)S(1)}, bf16[64,1408]{1,0:T(8,128)(2,1)S(1)}, bf16[64,1408]{1,0:T(8,128)(2,1)S(1)}, bf16[64,1408]{1,0:T(8,128)(2,1)S(1)}, f32[1,1408]{1,0:T(1,128)S(1)}) custom-call(bf16[64,1536]{1,0:T(8,128)(2,1)S(1)} %get-tuple-element.43.refs_0_, bf16[64,1536]{1,0:T(8,128)(2,1)S(1)} %collective-permute-done.1.refs_1_.refs_0_, ...), custom_call_target="tpu_custom_call" | custom-call | flops 6000000000 | bytes 20000000 | tf_op jit(solution)/shard_map/input/pallas_call | solution.py:455
  47.8 3.8 %collective-permute-start.18 = (f32[1,1408]{1,0:T(1,128)S(1)}, f32[1,1408]{1,0:T(1,128)S(1)}, u32[]{:S(2)}, u32[]{:S(2)}) collective-permute-start(f32[1,1408]{1,0:T(1,128)S(1)} %get-tuple-element.74.refs_4_), channel_id=1, source_target_pairs={{0,64},{1,17},{2,66},{3,19},{4,68},{5,21},{6,70},{7,23},{8,72},{9,... | collective-permute-start | bytes 16904 | tf_op jit(solution)/shard_map/ppermute | solution.py:324
  51.6 1.6 %collective-permute-start.19 = (f32[1,1408]{1,0:T(1,128)S(1)}, f32[1,1408]{1,0:T(1,128)S(1)}, u32[]{:S(2)}, u32[]{:S(2)}) collective-permute-start(f32[1,1408]{1,0:T(1,128)S(1)} %get-tuple-element.74.refs_4_), channel_id=1, source_target_pairs={{0,96},{1,25},{2,98},{3,27},{4,100},{5,29},{6,102},{7,31},{8,104},... | collective-permute-start | bytes 16904 | tf_op jit(solution)/shard_map/ppermute | solution.py:324
  53.2 2.4 %collective-permute-done.19.refs_7_ = f32[1,1408]{1,0:T(1,128)S(1)} collective-permute-done((f32[1,1408]{1,0:T(1,128)S(1)}, f32[1,1408]{1,0:T(1,128)S(1)}, u32[]{:S(2)}, u32[]{:S(2)}) %collective-permute-start.19) | collective-permute-done | bytes 5664 | tf_op jit(solution)/shard_map/ppermute | solution.py:324
  55.6 1.5 %collective-permute-start.10 = (bf16[64,1408]{1,0:T(8,128)(2,1)S(1)}, bf16[64,1408]{1,0:T(8,128)(2,1)S(1)}, u32[]{:S(2)}, u32[]{:S(2)}) collective-permute-start(bf16[64,1408]{1,0:T(8,128)(2,1)S(1)} %get-tuple-element.63), channel_id=1, source_target_pairs={{0,6},{1,7},{2,4},{3,5},{4,2},{5,3},{6,0},{7,1},{8,14},{9,15},{10,... | collective-permute-start | bytes 540680 | tf_op jit(solution)/shard_map/ppermute | solution.py:316
  57.1 1.1 %second.1 = bf16[16,24,768]{2,1,0:T(8,128)(2,1)} custom-call(f32[352,768]{1,0:T(8,128)S(1)} %get-tuple-element.70.refs_0_, bf16[352,768]{1,0:T(8,128)(2,1)S(1)} %collective-permute-done.14.refs_1_, bf16[352,768]{1,0:T(8,128)(2,1)S(1)} %collective-permute-done.15.refs_2_, bf16[352,768]{1,0:T(8,128)(2,1)S(1)} %collective-permute-done.16.refs_3_, ...), custom_call_target="tpu_custom_call" | custom-call | bytes 5000000 | tf_op jit(solution)/shard_map/second/pallas_call | solution.py:472
  58.2 5.2 %all-to-all-start = ((bf16[16,24,768]{2,1,0:T(8,128)(2,1)}), bf16[16,24,768]{2,1,0:T(8,128)(2,1)S(1)}, u32[]{:S(2)}, u32[]{:S(2)}) async-start(bf16[16,24,768]{2,1,0:T(8,128)(2,1)} %second.1), calls=%async_computation | async-start | bytes 1179648 | tf_op jit(solution)/shard_map/all_to_all | solution.py:333
  63.5 3.3 %collective-permute-done.10.refs_3_ = bf16[64,1408]{1,0:T(8,128)(2,1)S(1)} collective-permute-done((bf16[64,1408]{1,0:T(8,128)(2,1)S(1)}, bf16[64,1408]{1,0:T(8,128)(2,1)S(1)}, u32[]{:S(2)}, u32[]{:S(2)}) %collective-permute-start.10) | collective-permute-done | bytes 180256 | tf_op jit(solution)/shard_map/ppermute | solution.py:316
  67.8 5.0 %all-to-all-done.parts_ref = bf16[16,24,768]{2,1,0:T(8,128)(2,1)S(1)} async-done(((bf16[16,24,768]{2,1,0:T(8,128)(2,1)}), bf16[16,24,768]{2,1,0:T(8,128)(2,1)S(1)}, u32[]{:S(2)}, u32[]{:S(2)}) %all-to-all-start) | async-done | bytes 589856 | tf_op jit(solution)/shard_map/all_to_all | solution.py:333
  72.9 4.5 %collective-permute-start.20 = (f32[16,768]{1,0:T(8,128)S(1)}, f32[16,768]{1,0:T(8,128)S(1)}, u32[]{:S(2)}, u32[]{:S(2)}) collective-permute-start(f32[16,768]{1,0:T(8,128)S(1)} %get-tuple-element.76), channel_id=1, source_target_pairs={{0,1},{1,0},{2,3},{3,2},{4,5},{5,4},{6,7},{7,6},{8,9},{9,8},{10,11... | collective-permute-start | bytes 147464 | tf_op jit(solution)/shard_map/ppermute | solution.py:316
  (43 shorter events, 9.0 us)
Async XLA Ops:
  1.3 1.1 %copy-start.1 = (bf16[1,1,256,1408]{3,2,1,0:T(8,128)(2,1)S(1)}, bf16[1,1,256,1408]{3,2,1,0:T(8,128)(2,1)}, u32[]{:S(2)}) copy-start(bf16[1,1,256,1408]{3,2,1,0:T(8,128)(2,1)} %param.5) | copy-start | bytes 2162692
  2.5 2.9 %collective-permute-start = (bf16[4,32,1536]{2,1,0:T(8,128)(2,1)S(1)}, bf16[4,32,1536]{2,1,0:T(8,128)(2,1)S(1)}, u32[]{:S(2)}, u32[]{:S(2)}) collective-permute-start(bf16[4,32,1536]{2,1,0:T(8,128)(2,1)S(1)} %get-tuple-element.42), channel_id=1, source_target_pairs={{0,1},{1,0},{2,3},{3,2},{4,5},{5,4},{6,7},{7,6},{8,9},{9,8},{10,11... | collective-permute-start | bytes 1179656 | tf_op jit(solution)/shard_map/ppermute | solution.py:316
  5.1 10.2 %collective-permute-start.4 = (bf16[4,32,1408]{2,1,0:T(8,128)(2,1)S(1)}, bf16[4,32,1408]{2,1,0:T(8,128)(2,1)S(1)}, u32[]{:S(2)}, u32[]{:S(2)}) collective-permute-start(bf16[4,32,1408]{2,1,0:T(8,128)(2,1)S(1)} %get-tuple-element.53), channel_id=1, source_target_pairs={{0,1},{1,0},{2,3},{3,2},{4,5},{5,4},{6,7},{7,6},{8,9},{9,8},{10,11... | collective-permute-start | bytes 1081352 | tf_op jit(solution)/shard_map/ppermute | solution.py:316
  5.4 10.0 %collective-permute-start.1 = (bf16[64,1536]{1,0:T(8,128)(2,1)S(1)}, bf16[64,1536]{1,0:T(8,128)(2,1)S(1)}, u32[]{:S(2)}, u32[]{:S(2)}) collective-permute-start(bf16[64,1536]{1,0:T(8,128)(2,1)S(1)} %get-tuple-element.44), channel_id=1, source_target_pairs={{0,2},{1,3},{2,0},{3,1},{4,6},{5,7},{6,4},{7,5},{8,10},{9,11},{10,... | collective-permute-start | bytes 589832 | tf_op jit(solution)/shard_map/ppermute | solution.py:316
  6.8 12.6 %collective-permute-start.2 = (bf16[64,1536]{1,0:T(8,128)(2,1)S(1)}, bf16[64,1536]{1,0:T(8,128)(2,1)S(1)}, u32[]{:S(2)}, u32[]{:S(2)}) collective-permute-start(bf16[64,1536]{1,0:T(8,128)(2,1)S(1)} %get-tuple-element.45), channel_id=1, source_target_pairs={{0,4},{1,5},{2,6},{3,7},{4,0},{5,1},{6,2},{7,3},{8,12},{9,13},{10,... | collective-permute-start | bytes 589832 | tf_op jit(solution)/shard_map/ppermute | solution.py:316
  9.2 11.2 %collective-permute-start.3 = (bf16[64,1536]{1,0:T(8,128)(2,1)S(1)}, bf16[64,1536]{1,0:T(8,128)(2,1)S(1)}, u32[]{:S(2)}, u32[]{:S(2)}) collective-permute-start(bf16[64,1536]{1,0:T(8,128)(2,1)S(1)} %get-tuple-element.46), channel_id=1, source_target_pairs={{0,6},{1,7},{2,4},{3,5},{4,2},{5,3},{6,0},{7,1},{8,14},{9,15},{10,... | collective-permute-start | bytes 589832 | tf_op jit(solution)/shard_map/ppermute | solution.py:316
  10.0 4.4 %copy-start = (bf16[1408,4224]{1,0:T(8,128)(2,1)S(1)}, bf16[1408,4224]{1,0:T(8,128)(2,1)}, u32[]{:S(2)}) copy-start(bf16[1408,4224]{1,0:T(8,128)(2,1)} %w_hbm.1) | copy-start | bytes 35684356
  15.4 13.3 %collective-permute-start.5 = (bf16[64,1408]{1,0:T(8,128)(2,1)S(1)}, bf16[64,1408]{1,0:T(8,128)(2,1)S(1)}, u32[]{:S(2)}, u32[]{:S(2)}) collective-permute-start(bf16[64,1408]{1,0:T(8,128)(2,1)S(1)} %get-tuple-element.55), channel_id=1, source_target_pairs={{0,2},{1,3},{2,0},{3,1},{4,6},{5,7},{6,4},{7,5},{8,10},{9,11},{10,... | collective-permute-start | bytes 540680 | tf_op jit(solution)/shard_map/ppermute | solution.py:316
  15.6 13.1 %collective-permute-start.6 = (bf16[64,1408]{1,0:T(8,128)(2,1)S(1)}, bf16[64,1408]{1,0:T(8,128)(2,1)S(1)}, u32[]{:S(2)}, u32[]{:S(2)}) collective-permute-start(bf16[64,1408]{1,0:T(8,128)(2,1)S(1)} %get-tuple-element.56), channel_id=1, source_target_pairs={{0,4},{1,5},{2,6},{3,7},{4,0},{5,1},{6,2},{7,3},{8,12},{9,13},{10,... | collective-permute-start | bytes 540680 | tf_op jit(solution)/shard_map/ppermute | solution.py:316
  19.3 10.1 %collective-permute-start.7 = (bf16[64,1408]{1,0:T(8,128)(2,1)S(1)}, bf16[64,1408]{1,0:T(8,128)(2,1)S(1)}, u32[]{:S(2)}, u32[]{:S(2)}) collective-permute-start(bf16[64,1408]{1,0:T(8,128)(2,1)S(1)} %get-tuple-element.57), channel_id=1, source_target_pairs={{0,6},{1,7},{2,4},{3,5},{4,2},{5,3},{6,0},{7,1},{8,14},{9,15},{10,... | collective-permute-start | bytes 540680 | tf_op jit(solution)/shard_map/ppermute | solution.py:316
  21.6 11.8 %collective-permute-start.12 = (bf16[1408,256]{1,0:T(8,128)(2,1)S(1)}, bf16[1408,256]{1,0:T(8,128)(2,1)S(1)}, u32[]{:S(2)}, u32[]{:S(2)}) collective-permute-start(bf16[1408,256]{1,0:T(8,128)(2,1)S(1)} %get-tuple-element.67), channel_id=1, source_target_pairs={{0,1},{1,0},{2,3},{3,2},{4,5},{5,4},{6,7},{7,6},{8,9},{9,8},{10,11... | collective-permute-start | bytes 2162696 | tf_op jit(solution)/shard_map/ppermute | solution.py:316
  30.3 3.0 %collective-permute-start.13 = (bf16[256,768]{1,0:T(8,128)(2,1)S(1)}, bf16[256,768]{1,0:T(8,128)(2,1)S(1)}, u32[]{:S(2)}, u32[]{:S(2)}) collective-permute-start(bf16[256,768]{1,0:T(8,128)(2,1)S(1)} %get-tuple-element.69), channel_id=1, source_target_pairs={{0,1},{1,0},{2,3},{3,2},{4,5},{5,4},{6,7},{7,6},{8,9},{9,8},{10,11... | collective-permute-start | bytes 1179656 | tf_op jit(solution)/shard_map/ppermute | solution.py:316
  34.7 20.9 %collective-permute-start.14 = (bf16[352,768]{1,0:T(8,128)(2,1)S(1)}, bf16[352,768]{1,0:T(8,128)(2,1)S(1)}, u32[]{:S(2)}, u32[]{:S(2)}) collective-permute-start(bf16[352,768]{1,0:T(8,128)(2,1)S(1)} %get-tuple-element.71), channel_id=1, source_target_pairs={{0,32},{1,9},{2,34},{3,11},{4,36},{5,13},{6,38},{7,15},{8,40},{9,1... | collective-permute-start | bytes 1622024 | tf_op jit(solution)/shard_map/ppermute | solution.py:324
  36.4 20.7 %collective-permute-start.15 = (bf16[352,768]{1,0:T(8,128)(2,1)S(1)}, bf16[352,768]{1,0:T(8,128)(2,1)S(1)}, u32[]{:S(2)}, u32[]{:S(2)}) collective-permute-start(bf16[352,768]{1,0:T(8,128)(2,1)S(1)} %get-tuple-element.72), channel_id=1, source_target_pairs={{0,64},{1,17},{2,66},{3,19},{4,68},{5,21},{6,70},{7,23},{8,72},{9,... | collective-permute-start | bytes 1622024 | tf_op jit(solution)/shard_map/ppermute | solution.py:324
  39.7 17.4 %collective-permute-start.16 = (bf16[352,768]{1,0:T(8,128)(2,1)S(1)}, bf16[352,768]{1,0:T(8,128)(2,1)S(1)}, u32[]{:S(2)}, u32[]{:S(2)}) collective-permute-start(bf16[352,768]{1,0:T(8,128)(2,1)S(1)} %get-tuple-element.73), channel_id=1, source_target_pairs={{0,96},{1,25},{2,98},{3,27},{4,100},{5,29},{6,102},{7,31},{8,104},... | collective-permute-start | bytes 1622024 | tf_op jit(solution)/shard_map/ppermute | solution.py:324
  47.7 3.9 %collective-permute-start.17 = (f32[1,1408]{1,0:T(1,128)S(1)}, f32[1,1408]{1,0:T(1,128)S(1)}, u32[]{:S(2)}, u32[]{:S(2)}) collective-permute-start(f32[1,1408]{1,0:T(1,128)S(1)} %get-tuple-element.74.refs_4_), channel_id=1, source_target_pairs={{0,32},{1,9},{2,34},{3,11},{4,36},{5,13},{6,38},{7,15},{8,40},{9,1... | collective-permute-start | bytes 16904 | tf_op jit(solution)/shard_map/ppermute | solution.py:324
  47.8 5.4 %collective-permute-start.18 = (f32[1,1408]{1,0:T(1,128)S(1)}, f32[1,1408]{1,0:T(1,128)S(1)}, u32[]{:S(2)}, u32[]{:S(2)}) collective-permute-start(f32[1,1408]{1,0:T(1,128)S(1)} %get-tuple-element.74.refs_4_), channel_id=1, source_target_pairs={{0,64},{1,17},{2,66},{3,19},{4,68},{5,21},{6,70},{7,23},{8,72},{9,... | collective-permute-start | bytes 16904 | tf_op jit(solution)/shard_map/ppermute | solution.py:324
  51.6 4.0 %collective-permute-start.19 = (f32[1,1408]{1,0:T(1,128)S(1)}, f32[1,1408]{1,0:T(1,128)S(1)}, u32[]{:S(2)}, u32[]{:S(2)}) collective-permute-start(f32[1,1408]{1,0:T(1,128)S(1)} %get-tuple-element.74.refs_4_), channel_id=1, source_target_pairs={{0,96},{1,25},{2,98},{3,27},{4,100},{5,29},{6,102},{7,31},{8,104},... | collective-permute-start | bytes 16904 | tf_op jit(solution)/shard_map/ppermute | solution.py:324
  53.2 10.2 %collective-permute-start.8 = (bf16[64,1408]{1,0:T(8,128)(2,1)S(1)}, bf16[64,1408]{1,0:T(8,128)(2,1)S(1)}, u32[]{:S(2)}, u32[]{:S(2)}) collective-permute-start(bf16[64,1408]{1,0:T(8,128)(2,1)S(1)} %get-tuple-element.61), channel_id=1, source_target_pairs={{0,2},{1,3},{2,0},{3,1},{4,6},{5,7},{6,4},{7,5},{8,10},{9,11},{10,... | collective-permute-start | bytes 540680 | tf_op jit(solution)/shard_map/ppermute | solution.py:316
  55.6 7.9 %collective-permute-start.9 = (bf16[64,1408]{1,0:T(8,128)(2,1)S(1)}, bf16[64,1408]{1,0:T(8,128)(2,1)S(1)}, u32[]{:S(2)}, u32[]{:S(2)}) collective-permute-start(bf16[64,1408]{1,0:T(8,128)(2,1)S(1)} %get-tuple-element.62), channel_id=1, source_target_pairs={{0,4},{1,5},{2,6},{3,7},{4,0},{5,1},{6,2},{7,3},{8,12},{9,13},{10,... | collective-permute-start | bytes 540680 | tf_op jit(solution)/shard_map/ppermute | solution.py:316
  55.6 11.2 %collective-permute-start.10 = (bf16[64,1408]{1,0:T(8,128)(2,1)S(1)}, bf16[64,1408]{1,0:T(8,128)(2,1)S(1)}, u32[]{:S(2)}, u32[]{:S(2)}) collective-permute-start(bf16[64,1408]{1,0:T(8,128)(2,1)S(1)} %get-tuple-element.63), channel_id=1, source_target_pairs={{0,6},{1,7},{2,4},{3,5},{4,2},{5,3},{6,0},{7,1},{8,14},{9,15},{10,... | collective-permute-start | bytes 540680 | tf_op jit(solution)/shard_map/ppermute | solution.py:316
  58.2 14.6 %all-to-all-start = ((bf16[16,24,768]{2,1,0:T(8,128)(2,1)}), bf16[16,24,768]{2,1,0:T(8,128)(2,1)S(1)}, u32[]{:S(2)}, u32[]{:S(2)}) async-start(bf16[16,24,768]{2,1,0:T(8,128)(2,1)} %second.1), calls=%async_computation | async-start | bytes 1179648 | tf_op jit(solution)/shard_map/all_to_all | solution.py:333
  66.8 10.6 %collective-permute-start.11 = (bf16[4,32,1408]{2,1,0:T(8,128)(2,1)S(1)}, bf16[4,32,1408]{2,1,0:T(8,128)(2,1)S(1)}, u32[]{:S(2)}, u32[]{:S(2)}) collective-permute-start(bf16[4,32,1408]{2,1,0:T(8,128)(2,1)S(1)} %get-tuple-element.65), channel_id=1, source_target_pairs={{0,1},{1,0},{2,3},{3,2},{4,5},{5,4},{6,7},{7,6},{8,9},{9,8},{10,11... | collective-permute-start | bytes 1081352 | tf_op jit(solution)/shard_map/ppermute | solution.py:316
  72.9 5.4 %collective-permute-start.20 = (f32[16,768]{1,0:T(8,128)S(1)}, f32[16,768]{1,0:T(8,128)S(1)}, u32[]{:S(2)}, u32[]{:S(2)}) collective-permute-start(f32[16,768]{1,0:T(8,128)S(1)} %get-tuple-element.76), channel_id=1, source_target_pairs={{0,1},{1,0},{2,3},{3,2},{4,5},{5,4},{6,7},{7,6},{8,9},{9,8},{10,11... | collective-permute-start | bytes 147464 | tf_op jit(solution)/shard_map/ppermute | solution.py:316
  (1 other events, 1.1 us)

commit v4 on v3

--- a/solution.py
+++ b/solution.py
@@ -1,3 +1,5 @@
+import itertools
+
 import jax
 import jax.numpy as jnp
 from jax import lax
@@ -17,6 +19,9 @@
 SLOTS = 8
 CHIPS = 4
 PAIR = 2 * CHUNK
+HALVES = 2
+STEP = 16
+SPAN = 128
 TILE = 256
 BLOCK = 88
 HALF = 768
@@ -118,13 +123,22 @@
     copy.wait()
 
 
+def in_half(j, f, half):
+    return pl.ds(half * SPAN + (2 * j + f) * STEP, STEP)
+
+
 def norm_body(*refs):
     xs, (gain_ref, _, normed_ref, clip_ref) = refs[:CHIPS], refs[CHIPS:]
     for j in range(CHIPS):
-        rows = pl.ds(j * PAIR, PAIR)
         normalized, _ = normalize(xs[j][:, pl.ds(0, D)])
-        normed_ref[rows, :] = (normalized * gain_ref[...]).astype(BF)
-        clip_ref[rows, :] = xs[j][:, pl.ds(D, 128)].astype(F32)
+        normed = (normalized * gain_ref[...]).astype(BF)
+        clip = xs[j][:, pl.ds(D, 128)].astype(F32)
+        for f in range(2):
+            for half in range(HALVES):
+                first = f * CHUNK + half * STEP
+                normed_ref[in_half(j, f, half), :] = normed[first : first + STEP]
+            rows = pl.ds((2 * j + f) * STEP, STEP)
+            clip_ref[rows, :] = clip[f * CHUNK : f * CHUNK + STEP]
 
 
 def turn_body(normed_ref, mine_ref, theirs_ref, wide_ref, other_ref):
@@ -153,11 +167,10 @@
         out = jnp.dot(normed_ref[...], wbuf[:, cols], preferred_element_type=F32)
         qkv_ref[:, cols] = out.astype(BF)
 
-    row = lax.broadcasted_iota(jnp.int32, (ROWS, ROWS), 0)
-    col = lax.broadcasted_iota(jnp.int32, (ROWS, ROWS), 1)
+    row = lax.broadcasted_iota(jnp.int32, (SPAN, SPAN), 0)
+    col = lax.broadcasted_iota(jnp.int32, (SPAN, SPAN), 1)
     clip = clip_ref[...]
-    clip = jnp.concatenate([clip, clip], axis=1)
-    kept = (clip == jnp.transpose(clip)) & (row % CHUNK == col % CHUNK)
+    kept = (clip == jnp.transpose(clip)) & (row % STEP == col % STEP)
     bias_ref[...] = jnp.where(kept, 0.0, MASKED).astype(F32)
     qkv_ref[:, pl.ds(TRIPLE, 128)] = jnp.zeros((ROWS, 128), BF)
 
@@ -166,14 +179,18 @@
 
     def attend(head):
         start, lanes = head_window(head)
-        query = qkv_ref[:, pl.ds(start, WIN)]
-        key = keep(lanes, qkv_ref[:, pl.ds(D + start, WIN)])
-        scores = lax.dot_general(key, query, (((1,), (1,)), ((), ())), preferred_element_type=F32)
-        scores = scores * SCALING + bias_ref[...]
-        powers = jnp.exp(scores - jnp.max(scores, axis=0, keepdims=True))
-        softmaxed = powers / jnp.sum(powers, axis=0, keepdims=True)
-        soft_ref[head] = softmaxed
-        prob_ref[head] = softmaxed.astype(BF)
+        for half in range(HALVES):
+            rows = pl.ds(half * SPAN, SPAN)
+            query = qkv_ref[rows, pl.ds(start, WIN)]
+            key = keep(lanes, qkv_ref[rows, pl.ds(D + start, WIN)])
+            scores = lax.dot_general(
+                key, query, (((1,), (1,)), ((), ())), preferred_element_type=F32
+            )
+            scores = scores * SCALING + bias_ref[...]
+            powers = jnp.exp(scores - jnp.max(scores, axis=0, keepdims=True))
+            softmaxed = powers / jnp.sum(powers, axis=0, keepdims=True)
+            soft_ref[head, half] = softmaxed
+            prob_ref[head, half] = softmaxed.astype(BF)
 
     qkv_ref[:, pl.ds(2 * D, 128)] = jnp.zeros((ROWS, 128), BF)
     for head in range(HEADS):
@@ -186,14 +203,19 @@
     chunks = refs[:CHIPS]
     dv_ref, mine_ref, theirs_ref, grad_ref, acc_ref = refs[CHIPS:]
     for j in range(CHIPS):
-        grad_ref[pl.ds(j * PAIR, PAIR), pl.ds(0, D)] = chunks[j][...]
+        for f in range(2):
+            for half in range(HALVES):
+                rows = pl.ds(f * CHUNK + half * STEP, STEP)
+                grad_ref[in_half(j, f, half), pl.ds(0, D)] = chunks[j][rows, :]
     grad_ref[:, pl.ds(D, 128)] = jnp.zeros((ROWS, 128), BF)
     acc_ref[...] = jnp.zeros_like(acc_ref)
 
     def one(head):
         first, lanes = head_window(head)
-        grad = keep(lanes, grad_ref[:, pl.ds(first, WIN)])
-        acc_ref[:, pl.ds(first, WIN)] += jnp.dot(prob_ref[head], grad, preferred_element_type=F32)
+        for half in range(HALVES):
+            at = pl.ds(half * SPAN, SPAN), pl.ds(first, WIN)
+            grad = keep(lanes, grad_ref[at])
+            acc_ref[at] += jnp.dot(prob_ref[head, half], grad, preferred_element_type=F32)
 
     for head in range(HEADS):
         one(head)
@@ -215,7 +237,7 @@
 
 
 def second_body(*refs):
-    parts, gains, out_ref = refs[:4], refs[4:8], refs[8]
+    parts, gains, out_ref = refs[:4], refs[4:6], refs[6]
     gain = gains[0][...]
     for g in gains[1:]:
         gain = gain + g[...]
@@ -262,7 +284,7 @@
     outs, gain_out = refs[6 : 6 + CHIPS], refs[6 + CHIPS]
     dq_ref, dk_ref, g_ref, dn_ref = refs[7 + CHIPS :]
     tiles = [(0, 512), (512, 512), (1024, 384)]
-    parts = [pl.ds(2 * D, D), pl.ds(0, 2 * D)]
+    sides = [pl.ds(2 * D, D), pl.ds(0, 2 * D)]
 
     dq_ref[...] = jnp.zeros_like(dq_ref)
     dk_ref[...] = jnp.zeros_like(dk_ref)
@@ -270,16 +292,27 @@
 
     def one(head):
         first, lanes = head_window(head)
-        query = keep(lanes, qkv_ref[:, pl.ds(first, WIN)])
+        lane = pl.ds(first, WIN)
+        query = keep(lanes, qkv_ref[:, lane])
         key = keep(lanes, qkv_ref[:, pl.ds(D + first, WIN)])
         value = keep(lanes, qkv_ref[:, pl.ds(2 * D + first, WIN)])
-        grad = grad_ref[:, pl.ds(first, WIN)]
-        d_probs = lax.dot_general(value, grad, across, preferred_element_type=F32)
-        softmaxed = soft_ref[head]
-        row_dot = jnp.sum(softmaxed * d_probs, axis=0, keepdims=True)
-        d_scores = (softmaxed * (d_probs - row_dot) * SCALING).astype(BF)
-        dk_ref[:, pl.ds(first, WIN)] += jnp.dot(d_scores, query, preferred_element_type=F32)
-        dq_ref[:, pl.ds(first, WIN)] += lax.dot_general(
+        parts = []
+        for half in range(HALVES):
+            d_probs = lax.dot_general(
+                value[half * SPAN : (half + 1) * SPAN],
+                grad_ref[pl.ds(half * SPAN, SPAN), lane],
+                across,
+                preferred_element_type=F32,
+            )
+            softmaxed = soft_ref[head, half]
+            row_dot = jnp.sum(softmaxed * d_probs, axis=0, keepdims=True)
+            parts.append((softmaxed * (d_probs - row_dot) * SCALING).astype(BF))
+        none = jnp.zeros((SPAN, SPAN), BF)
+        d_scores = jnp.concatenate(
+            [jnp.concatenate([parts[0], none], 1), jnp.concatenate([none, parts[1]], 1)], 0
+        )
+        dk_ref[:, lane] += jnp.dot(d_scores, query, preferred_element_type=F32)
+        dq_ref[:, lane] += lax.dot_general(
             d_scores, key, (((0,), (0,)), ((), ())), preferred_element_type=F32
         )
 
@@ -288,27 +321,27 @@
         if head % 4 == 3 and head < 15:
             rows = pl.ds(*tiles[head // 4])
             dn_ref[:, rows] = lax.dot_general(
-                dv_ref[...], wbuf[rows, parts[0]], across, preferred_element_type=F32
+                dv_ref[...], wbuf[rows, sides[0]], across, preferred_element_type=F32
             )
     g_ref[:, pl.ds(0, D)] = dq_ref[:, pl.ds(0, D)].astype(BF)
     g_ref[:, pl.ds(D, D)] = dk_ref[:, pl.ds(0, D)].astype(BF)
     for tile in tiles:
         rows = pl.ds(*tile)
         dn_ref[:, rows] += lax.dot_general(
-            g_ref[...], wbuf[rows, parts[1]], across, preferred_element_type=F32
+            g_ref[...], wbuf[rows, sides[1]], across, preferred_element_type=F32
         )
     gain = gain_ref[...]
     gain_sum = jnp.zeros((1, D), F32)
-    for k in range(SLOTS):
-        rows = pl.ds(k % 2 * CHUNK, CHUNK)
-        normalized, inv_std = normalize(xs[k // 2][rows, pl.ds(0, D)])
-        d_normed = dn_ref[pl.ds(k * CHUNK, CHUNK), :]
+    for j, f, half in itertools.product(range(CHIPS), range(2), range(HALVES)):
+        rows = pl.ds(f * CHUNK + half * STEP, STEP)
+        normalized, inv_std = normalize(xs[j][rows, pl.ds(0, D)])
+        d_normed = dn_ref[in_half(j, f, half), :]
         gain_sum = gain_sum + jnp.sum(d_normed * normalized, axis=0, keepdims=True)
         d_hat = d_normed * gain
         first_mean = jnp.mean(d_hat, axis=-1, keepdims=True)
         second_mean = jnp.mean(d_hat * normalized, axis=-1, keepdims=True)
         out = inv_std * (d_hat - first_mean - normalized * second_mean)
-        outs[k // 2][rows, :] = out.astype(BF)
+        outs[j][rows, :] = out.astype(BF)
     gain_out[...] = gain_sum
 
 
@@ -336,7 +369,8 @@
 
 
 def swap_chips(chunks):
-    return [chunks[0]] + [swap_seq(chunks[j], 2 * j) for j in range(1, CHIPS)]
+    moved = {j: swap_seq(chunks[j], 2 * j) for j in (1, 3, 2)}
+    return [chunks[0]] + [moved[j] for j in range(1, CHIPS)]
 
 
 def spread(rows, *clip, after=()):
@@ -396,7 +430,7 @@
     )(qkv_weight)
     normed, clips = call(
         norm_body,
-        [shape((ROWS, D), BF), shape((ROWS, 128), F32)],
+        [shape((ROWS, D), BF), shape((SPAN, 128), F32)],
         in_specs=[VMEM] * (CHIPS + 1) + [pl.BlockSpec(memory_space=pl.ANY)],
         mib=8,
         data=10**6,
@@ -415,11 +449,11 @@
         project_body,
         [
             shape((ROWS, PADDED), BF),
-            shape((HEADS, ROWS, ROWS), F32),
-            shape((HEADS, ROWS, ROWS), BF),
+            shape((HEADS, HALVES, SPAN, SPAN), F32),
+            shape((HEADS, HALVES, SPAN, SPAN), BF),
         ],
         scratch=[
-            pltpu.VMEM((ROWS, ROWS), F32),
+            pltpu.VMEM((SPAN, SPAN), F32),
         ],
         mib=16,
         flops=5 * 10**9,
@@ -467,7 +501,8 @@
         name="input",
     )(*x, qkv, soft, grad_wide, d_value, gain, weight)
     returned, gain_term = results[:CHIPS], results[CHIPS]
-    gains = [gain_term] + [swap_plane(gain_term, j) for j in range(1, 4)]
+    gain_term = gain_term + swap_plane(gain_term, 1)
+    gains = [gain_term, swap_plane(gain_term, 3)]
 
     sums = call(second_body, shape((16, 24, HALF), BF), mib=16, data=5 * 10**6, name="second")(
         *terms, *gains

time: 79.4 us -> 78 us (0.982)
  waiting for transfers between devices: 13.9 us -> 15.3 us
  starting transfers between devices: 35.4 us -> 34.1 us
    ppermute x6 -> x5, starting transfers between devices: 10.5 us -> 7.86 us  [swap_plane(): return lax.ppermute(value, ('dp', 'seq'), pairs)]
    ppermute x15, starting transfers between devices: 19.7 us -> 21.7 us  [swap_seq(): return lax.ppermute(value, 'seq', [(i, i ^ k) for i in range(SLOTS)])]
    ppermute x6 -> x5, waiting for transfers between devices: 2.4 us -> 4.44 us  [swap_plane(): return lax.ppermute(value, ('dp', 'seq'), pairs)]
    all_to_all x1, waiting for transfers between devices: 5.02 us -> 4.15 us  [exchange_plane(): lax.all_to_all(blocks, ('dp', 'seq'), split_axis=0, concat_axis=0, tiled=...]
    unnamed x6 -> x8, local copies, waits for them, and re-layouts: 6.59 us -> 6.59 us
  transfers between devices with their start and end apart: 22 -> 21, of which waited for: 7 -> 8; matrix products, arithmetic and copies ran while one was open for 1% -> 0% of each run, Pallas kernels for 24% -> 24%
where the time goes in v4:
time: 78 us; the launch traced here: 77.7 us
  starting transfers between devices  34.1 us (44%)
  Pallas kernels  20.3 us (26%)
  waiting for transfers between devices  15.3 us (20%)
  local copies, waits for them, and re-layouts  6.6 us (8%)
  between operations  1.46 us (2%)
    ppermute x15, starting transfers between devices, swap_seq(): return lax.ppermute(value, 'seq', [(i, i ^ k) for i in range(SLOTS)])  21.7 us
    pallas_call x1, Pallas kernels, shards(): call(input_body, [shape((PAIR, D), BF)] * CHIPS + [shape((1, D), F32)], s...  8.27 us
    ppermute x5, starting transfers between devices, swap_plane(): return lax.ppermute(value, ('dp', 'seq'), pairs)  7.86 us
    ppermute x15, waiting for transfers between devices, swap_seq(): return lax.ppermute(value, 'seq', [(i, i ^ k) for i in range(SLOTS)])  6.7 us
    unnamed x8, local copies, waits for them, and re-layouts  6.59 us
    pallas_call x1, Pallas kernels, shards(): call(project_body, [shape((ROWS, PADDED), BF), shape((HEADS, HALVES, SPAN...  4.77 us
    all_to_all x1, starting transfers between devices, exchange_plane(): lax.all_to_all(blocks, ('dp', 'seq'), split_axis=0, concat_axis=0, tiled=...  4.51 us
    ppermute x5, waiting for transfers between devices, swap_plane(): return lax.ppermute(value, ('dp', 'seq'), pairs)  4.44 us
  transfers between devices with their start and end apart: 21, of which 8 were waited for; matrix products, arithmetic and copies ran while one was open for 0% of the time, Pallas kernels for 24%

profile of v4, /device:TPU:1, one launch (start us, length us, event | category | flops | bytes accessed | tf_op | source)
XLA Modules:
  0.0 77.7 jit_solution(3449747173023554030)
XLA Ops:
  2.5 1.5 %collective-permute-start = (bf16[4,32,1536]{2,1,0:T(8,128)(2,1)S(1)}, bf16[4,32,1536]{2,1,0:T(8,128)(2,1)S(1)}, u32[]{:S(2)}, u32[]{:S(2)}) collective-permute-start(bf16[4,32,1536]{2,1,0:T(8,128)(2,1)S(1)} %get-tuple-element.42), channel_id=1, source_target_pairs={{0,1},{1,0},{2,3},{3,2},{4,5},{5,4},{6,7},{7,6},{8,9},{9,8},{10,11... | collective-permute-start | bytes 1179656 | tf_op jit(solution)/shard_map/ppermute | solution.py:349
  5.4 1.4 %collective-permute-start.1 = (bf16[64,1536]{1,0:T(8,128)(2,1)S(1)}, bf16[64,1536]{1,0:T(8,128)(2,1)S(1)}, u32[]{:S(2)}, u32[]{:S(2)}) collective-permute-start(bf16[64,1536]{1,0:T(8,128)(2,1)S(1)} %get-tuple-element.44), channel_id=1, source_target_pairs={{0,2},{1,3},{2,0},{3,1},{4,6},{5,7},{6,4},{7,5},{8,10},{9,11},{10,... | collective-permute-start | bytes 589832 | tf_op jit(solution)/shard_map/ppermute | solution.py:349
  6.8 2.5 %collective-permute-start.2 = (bf16[64,1536]{1,0:T(8,128)(2,1)S(1)}, bf16[64,1536]{1,0:T(8,128)(2,1)S(1)}, u32[]{:S(2)}, u32[]{:S(2)}) collective-permute-start(bf16[64,1536]{1,0:T(8,128)(2,1)S(1)} %get-tuple-element.45), channel_id=1, source_target_pairs={{0,4},{1,5},{2,6},{3,7},{4,0},{5,1},{6,2},{7,3},{8,12},{9,13},{10,... | collective-permute-start | bytes 589832 | tf_op jit(solution)/shard_map/ppermute | solution.py:349
  9.3 4.4 %copy-done = bf16[1408,4224]{1,0:T(8,128)(2,1)S(1)} copy-done((bf16[1408,4224]{1,0:T(8,128)(2,1)S(1)}, bf16[1408,4224]{1,0:T(8,128)(2,1)}, u32[]{:S(2)}) %copy-start) | copy-done | bytes 11894808
  14.9 3.7 %collective-permute-start.6 = (bf16[64,1408]{1,0:T(8,128)(2,1)S(1)}, bf16[64,1408]{1,0:T(8,128)(2,1)S(1)}, u32[]{:S(2)}, u32[]{:S(2)}) collective-permute-start(bf16[64,1408]{1,0:T(8,128)(2,1)S(1)} %get-tuple-element.56), channel_id=1, source_target_pairs={{0,4},{1,5},{2,6},{3,7},{4,0},{5,1},{6,2},{7,3},{8,12},{9,13},{10,... | collective-permute-start | bytes 540680 | tf_op jit(solution)/shard_map/ppermute | solution.py:349
  18.7 1.7 %collective-permute-done.3.refs_3_ = bf16[64,1536]{1,0:T(8,128)(2,1)S(1)} collective-permute-done((bf16[64,1536]{1,0:T(8,128)(2,1)S(1)}, bf16[64,1536]{1,0:T(8,128)(2,1)S(1)}, u32[]{:S(2)}, u32[]{:S(2)}) %collective-permute-start.3) | collective-permute-done | bytes 196640 | tf_op jit(solution)/shard_map/ppermute | solution.py:349
  21.6 1.6 %collective-permute-start.12 = (bf16[1408,256]{1,0:T(8,128)(2,1)S(1)}, bf16[1408,256]{1,0:T(8,128)(2,1)S(1)}, u32[]{:S(2)}, u32[]{:S(2)}) collective-permute-start(bf16[1408,256]{1,0:T(8,128)(2,1)S(1)} %get-tuple-element.67), channel_id=1, source_target_pairs={{0,1},{1,0},{2,3},{3,2},{4,5},{5,4},{6,7},{7,6},{8,9},{9,8},{10,11... | collective-permute-start | bytes 2162696 | tf_op jit(solution)/shard_map/ppermute | solution.py:349
  23.2 4.8 %project.1 = (bf16[256,4352]{1,0:T(8,128)(2,1)S(1)}, f32[16,2,128,128]{3,2,1,0:T(8,128)S(1)}, bf16[16,2,128,128]{3,2,1,0:T(8,128)(2,1)S(1)}) custom-call(f32[128,128]{1,0:T(8,128)S(1)} %get-tuple-element.47.clip_ref, bf16[256,1408]{1,0:T(8,128)(2,1)S(1)} %get-tuple-element.48.normed_ref, bf16[1408,4224]{1,0:T(8,128)(2,1)S(1)} %load.1.refs_5_.wbuf.refs_9_), custom_call_target="tpu_custom_call" | custom-call | flops 5000000000 | bytes 40000000 | tf_op jit(solution)/shard_map/project/pallas_call | solution.py:448
  29.5 1.7 %collective-permute-start.13 = (bf16[256,768]{1,0:T(8,128)(2,1)S(1)}, bf16[256,768]{1,0:T(8,128)(2,1)S(1)}, u32[]{:S(2)}, u32[]{:S(2)}) collective-permute-start(bf16[256,768]{1,0:T(8,128)(2,1)S(1)} %get-tuple-element.69), channel_id=1, source_target_pairs={{0,1},{1,0},{2,3},{3,2},{4,5},{5,4},{6,7},{7,6},{8,9},{9,8},{10,11... | collective-permute-start | bytes 1179656 | tf_op jit(solution)/shard_map/ppermute | solution.py:349
  31.2 1.3 %collective-permute-done.13.dv_other_ref = bf16[256,768]{1,0:T(8,128)(2,1)S(1)} collective-permute-done((bf16[256,768]{1,0:T(8,128)(2,1)S(1)}, bf16[256,768]{1,0:T(8,128)(2,1)S(1)}, u32[]{:S(2)}, u32[]{:S(2)}) %collective-permute-start.13) | collective-permute-done | bytes 393248 | tf_op jit(solution)/shard_map/ppermute | solution.py:349
  32.6 1.3 %weight.1 = (f32[352,768]{1,0:T(8,128)S(1)}, bf16[352,768]{1,0:T(8,128)(2,1)S(1)}, bf16[352,768]{1,0:T(8,128)(2,1)S(1)}, bf16[352,768]{1,0:T(8,128)(2,1)S(1)}) custom-call(bf16[1408,256]{1,0:T(8,128)(2,1)S(1)} %get-tuple-element.66.nt_ref, bf16[1408,256]{1,0:T(8,128)(2,1)S(1)} %collective-permute-done.12.nt_other_ref, ...), custom_call_target="tpu_custom_call" | custom-call | flops 1100000000 | bytes 6000000 | tf_op jit(solution)/shard_map/weight/pallas_call | solution.py:479
  33.9 1.7 %collective-permute-start.14 = (bf16[352,768]{1,0:T(8,128)(2,1)S(1)}, bf16[352,768]{1,0:T(8,128)(2,1)S(1)}, u32[]{:S(2)}, u32[]{:S(2)}) collective-permute-start(bf16[352,768]{1,0:T(8,128)(2,1)S(1)} %get-tuple-element.71), channel_id=1, source_target_pairs={{0,32},{1,9},{2,34},{3,11},{4,36},{5,13},{6,38},{7,15},{8,40},{9,1... | collective-permute-start | bytes 1622024 | tf_op jit(solution)/shard_map/ppermute | solution.py:357
  35.6 3.3 %collective-permute-start.15 = (bf16[352,768]{1,0:T(8,128)(2,1)S(1)}, bf16[352,768]{1,0:T(8,128)(2,1)S(1)}, u32[]{:S(2)}, u32[]{:S(2)}) collective-permute-start(bf16[352,768]{1,0:T(8,128)(2,1)S(1)} %get-tuple-element.72), channel_id=1, source_target_pairs={{0,64},{1,17},{2,66},{3,19},{4,68},{5,21},{6,70},{7,23},{8,72},{9,... | collective-permute-start | bytes 1622024 | tf_op jit(solution)/shard_map/ppermute | solution.py:357
  38.9 8.3 %input.1 = (bf16[64,1408]{1,0:T(8,128)(2,1)S(1)}, bf16[64,1408]{1,0:T(8,128)(2,1)S(1)}, bf16[64,1408]{1,0:T(8,128)(2,1)S(1)}, bf16[64,1408]{1,0:T(8,128)(2,1)S(1)}, f32[1,1408]{1,0:T(1,128)S(1)}) custom-call(bf16[64,1536]{1,0:T(8,128)(2,1)S(1)} %get-tuple-element.43.refs_0_, bf16[64,1536]{1,0:T(8,128)(2,1)S(1)} %collective-permute-done.1.refs_1_.refs_0_, ...), custom_call_target="tpu_custom_call" | custom-call | flops 6000000000 | bytes 20000000 | tf_op jit(solution)/shard_map/input/pallas_call | solution.py:489
  47.2 2.8 %collective-permute-done.17 = f32[1,1408]{1,0:T(1,128)S(1)} collective-permute-done((f32[1,1408]{1,0:T(1,128)S(1)}, f32[1,1408]{1,0:T(1,128)S(1)}, u32[]{:S(2)}, u32[]{:S(2)}) %collective-permute-start.17) | collective-permute-done | bytes 5664 | tf_op jit(solution)/shard_map/ppermute | solution.py:357
  50.0 2.8 %collective-permute-start.18 = (f32[1,1408]{1,0:T(1,128)S(1)}, f32[1,1408]{1,0:T(1,128)S(1)}, u32[]{:S(2)}, u32[]{:S(2)}) collective-permute-start(f32[1,1408]{1,0:T(1,128)S(1)} %add.3.refs_4_), channel_id=1, source_target_pairs={{0,96},{1,25},{2,98},{3,27},{4,100},{5,29},{6,102},{7,31},{8,104},... | collective-permute-start | bytes 16904 | tf_op jit(solution)/shard_map/ppermute | solution.py:357
  52.8 1.7 %collective-permute-done.18.refs_5_ = f32[1,1408]{1,0:T(1,128)S(1)} collective-permute-done((f32[1,1408]{1,0:T(1,128)S(1)}, f32[1,1408]{1,0:T(1,128)S(1)}, u32[]{:S(2)}, u32[]{:S(2)}) %collective-permute-start.18) | collective-permute-done | bytes 5664 | tf_op jit(solution)/shard_map/ppermute | solution.py:357
  54.5 2.2 %collective-permute-start.10 = (bf16[64,1408]{1,0:T(8,128)(2,1)S(1)}, bf16[64,1408]{1,0:T(8,128)(2,1)S(1)}, u32[]{:S(2)}, u32[]{:S(2)}) collective-permute-start(bf16[64,1408]{1,0:T(8,128)(2,1)S(1)} %get-tuple-element.63), channel_id=1, source_target_pairs={{0,6},{1,7},{2,4},{3,5},{4,2},{5,3},{6,0},{7,1},{8,14},{9,15},{10,... | collective-permute-start | bytes 540680 | tf_op jit(solution)/shard_map/ppermute | solution.py:349
  56.6 1.1 %second.1 = bf16[16,24,768]{2,1,0:T(8,128)(2,1)} custom-call(f32[352,768]{1,0:T(8,128)S(1)} %get-tuple-element.70.refs_0_, bf16[352,768]{1,0:T(8,128)(2,1)S(1)} %collective-permute-done.14.refs_1_, bf16[352,768]{1,0:T(8,128)(2,1)S(1)} %collective-permute-done.15.refs_2_, bf16[352,768]{1,0:T(8,128)(2,1)S(1)} %collective-permute-done.16.refs_3_, ...), custom_call_target="tpu_custom_call" | custom-call | bytes 5000000 | tf_op jit(solution)/shard_map/second/pallas_call | solution.py:507
  57.8 4.5 %all-to-all-start = ((bf16[16,24,768]{2,1,0:T(8,128)(2,1)}), bf16[16,24,768]{2,1,0:T(8,128)(2,1)S(1)}, u32[]{:S(2)}, u32[]{:S(2)}) async-start(bf16[16,24,768]{2,1,0:T(8,128)(2,1)} %second.1), calls=%async_computation | async-start | bytes 1179648 | tf_op jit(solution)/shard_map/all_to_all | solution.py:366
  62.3 2.7 %collective-permute-done.10.refs_3_ = bf16[64,1408]{1,0:T(8,128)(2,1)S(1)} collective-permute-done((bf16[64,1408]{1,0:T(8,128)(2,1)S(1)}, bf16[64,1408]{1,0:T(8,128)(2,1)S(1)}, u32[]{:S(2)}, u32[]{:S(2)}) %collective-permute-start.10) | collective-permute-done | bytes 180256 | tf_op jit(solution)/shard_map/ppermute | solution.py:349
  65.1 2.4 %collective-permute-start.11 = (bf16[4,32,1408]{2,1,0:T(8,128)(2,1)S(1)}, bf16[4,32,1408]{2,1,0:T(8,128)(2,1)S(1)}, u32[]{:S(2)}, u32[]{:S(2)}) collective-permute-start(bf16[4,32,1408]{2,1,0:T(8,128)(2,1)S(1)} %get-tuple-element.65), channel_id=1, source_target_pairs={{0,1},{1,0},{2,3},{3,2},{4,5},{5,4},{6,7},{7,6},{8,9},{9,8},{10,11... | collective-permute-start | bytes 1081352 | tf_op jit(solution)/shard_map/ppermute | solution.py:349
  67.5 4.1 %all-to-all-done.parts_ref = bf16[16,24,768]{2,1,0:T(8,128)(2,1)S(1)} async-done(((bf16[16,24,768]{2,1,0:T(8,128)(2,1)}), bf16[16,24,768]{2,1,0:T(8,128)(2,1)S(1)}, u32[]{:S(2)}, u32[]{:S(2)}) %all-to-all-start) | async-done | bytes 589856 | tf_op jit(solution)/shard_map/all_to_all | solution.py:366
  71.7 4.4 %collective-permute-start.19 = (f32[16,768]{1,0:T(8,128)S(1)}, f32[16,768]{1,0:T(8,128)S(1)}, u32[]{:S(2)}, u32[]{:S(2)}) collective-permute-start(f32[16,768]{1,0:T(8,128)S(1)} %get-tuple-element.76), channel_id=1, source_target_pairs={{0,1},{1,0},{2,3},{3,2},{4,5},{5,4},{6,7},{7,6},{8,9},{9,8},{10,11... | collective-permute-start | bytes 147464 | tf_op jit(solution)/shard_map/ppermute | solution.py:349
  (44 shorter events, 8.5 us)
Async XLA Ops:
  1.3 1.1 %copy-start.1 = (bf16[1,1,256,1408]{3,2,1,0:T(8,128)(2,1)S(1)}, bf16[1,1,256,1408]{3,2,1,0:T(8,128)(2,1)}, u32[]{:S(2)}) copy-start(bf16[1,1,256,1408]{3,2,1,0:T(8,128)(2,1)} %param.5) | copy-start | bytes 2162692
  2.4 6.9 %copy-start.3 = (f32[1408]{0:T(1024)S(1)}, f32[1408]{0:T(1024)}, u32[]{:S(2)}) copy-start(f32[1408]{0:T(1024)} %param.6) | copy-start | bytes 16900
  2.5 2.9 %collective-permute-start = (bf16[4,32,1536]{2,1,0:T(8,128)(2,1)S(1)}, bf16[4,32,1536]{2,1,0:T(8,128)(2,1)S(1)}, u32[]{:S(2)}, u32[]{:S(2)}) collective-permute-start(bf16[4,32,1536]{2,1,0:T(8,128)(2,1)S(1)} %get-tuple-element.42), channel_id=1, source_target_pairs={{0,1},{1,0},{2,3},{3,2},{4,5},{5,4},{6,7},{7,6},{8,9},{9,8},{10,11... | collective-permute-start | bytes 1179656 | tf_op jit(solution)/shard_map/ppermute | solution.py:349
  5.1 9.5 %collective-permute-start.4 = (bf16[4,32,1408]{2,1,0:T(8,128)(2,1)S(1)}, bf16[4,32,1408]{2,1,0:T(8,128)(2,1)S(1)}, u32[]{:S(2)}, u32[]{:S(2)}) collective-permute-start(bf16[4,32,1408]{2,1,0:T(8,128)(2,1)S(1)} %get-tuple-element.53), channel_id=1, source_target_pairs={{0,1},{1,0},{2,3},{3,2},{4,5},{5,4},{6,7},{7,6},{8,9},{9,8},{10,11... | collective-permute-start | bytes 1081352 | tf_op jit(solution)/shard_map/ppermute | solution.py:349
  5.4 9.3 %collective-permute-start.1 = (bf16[64,1536]{1,0:T(8,128)(2,1)S(1)}, bf16[64,1536]{1,0:T(8,128)(2,1)S(1)}, u32[]{:S(2)}, u32[]{:S(2)}) collective-permute-start(bf16[64,1536]{1,0:T(8,128)(2,1)S(1)} %get-tuple-element.44), channel_id=1, source_target_pairs={{0,2},{1,3},{2,0},{3,1},{4,6},{5,7},{6,4},{7,5},{8,10},{9,11},{10,... | collective-permute-start | bytes 589832 | tf_op jit(solution)/shard_map/ppermute | solution.py:349
  6.8 11.9 %collective-permute-start.2 = (bf16[64,1536]{1,0:T(8,128)(2,1)S(1)}, bf16[64,1536]{1,0:T(8,128)(2,1)S(1)}, u32[]{:S(2)}, u32[]{:S(2)}) collective-permute-start(bf16[64,1536]{1,0:T(8,128)(2,1)S(1)} %get-tuple-element.45), channel_id=1, source_target_pairs={{0,4},{1,5},{2,6},{3,7},{4,0},{5,1},{6,2},{7,3},{8,12},{9,13},{10,... | collective-permute-start | bytes 589832 | tf_op jit(solution)/shard_map/ppermute | solution.py:349
  9.2 11.2 %collective-permute-start.3 = (bf16[64,1536]{1,0:T(8,128)(2,1)S(1)}, bf16[64,1536]{1,0:T(8,128)(2,1)S(1)}, u32[]{:S(2)}, u32[]{:S(2)}) collective-permute-start(bf16[64,1536]{1,0:T(8,128)(2,1)S(1)} %get-tuple-element.46), channel_id=1, source_target_pairs={{0,6},{1,7},{2,4},{3,5},{4,2},{5,3},{6,0},{7,1},{8,14},{9,15},{10,... | collective-permute-start | bytes 589832 | tf_op jit(solution)/shard_map/ppermute | solution.py:349
  9.3 4.4 %copy-start = (bf16[1408,4224]{1,0:T(8,128)(2,1)S(1)}, bf16[1408,4224]{1,0:T(8,128)(2,1)}, u32[]{:S(2)}) copy-start(bf16[1408,4224]{1,0:T(8,128)(2,1)} %w_hbm.1) | copy-start | bytes 35684356
  14.8 13.2 %collective-permute-start.5 = (bf16[64,1408]{1,0:T(8,128)(2,1)S(1)}, bf16[64,1408]{1,0:T(8,128)(2,1)S(1)}, u32[]{:S(2)}, u32[]{:S(2)}) collective-permute-start(bf16[64,1408]{1,0:T(8,128)(2,1)S(1)} %get-tuple-element.55), channel_id=1, source_target_pairs={{0,2},{1,3},{2,0},{3,1},{4,6},{5,7},{6,4},{7,5},{8,10},{9,11},{10,... | collective-permute-start | bytes 540680 | tf_op jit(solution)/shard_map/ppermute | solution.py:349
  14.9 13.0 %collective-permute-start.6 = (bf16[64,1408]{1,0:T(8,128)(2,1)S(1)}, bf16[64,1408]{1,0:T(8,128)(2,1)S(1)}, u32[]{:S(2)}, u32[]{:S(2)}) collective-permute-start(bf16[64,1408]{1,0:T(8,128)(2,1)S(1)} %get-tuple-element.56), channel_id=1, source_target_pairs={{0,4},{1,5},{2,6},{3,7},{4,0},{5,1},{6,2},{7,3},{8,12},{9,13},{10,... | collective-permute-start | bytes 540680 | tf_op jit(solution)/shard_map/ppermute | solution.py:349
  18.6 10.1 %collective-permute-start.7 = (bf16[64,1408]{1,0:T(8,128)(2,1)S(1)}, bf16[64,1408]{1,0:T(8,128)(2,1)S(1)}, u32[]{:S(2)}, u32[]{:S(2)}) collective-permute-start(bf16[64,1408]{1,0:T(8,128)(2,1)S(1)} %get-tuple-element.57), channel_id=1, source_target_pairs={{0,6},{1,7},{2,4},{3,5},{4,2},{5,3},{6,0},{7,1},{8,14},{9,15},{10,... | collective-permute-start | bytes 540680 | tf_op jit(solution)/shard_map/ppermute | solution.py:349
  21.6 11.0 %collective-permute-start.12 = (bf16[1408,256]{1,0:T(8,128)(2,1)S(1)}, bf16[1408,256]{1,0:T(8,128)(2,1)S(1)}, u32[]{:S(2)}, u32[]{:S(2)}) collective-permute-start(bf16[1408,256]{1,0:T(8,128)(2,1)S(1)} %get-tuple-element.67), channel_id=1, source_target_pairs={{0,1},{1,0},{2,3},{3,2},{4,5},{5,4},{6,7},{7,6},{8,9},{9,8},{10,11... | collective-permute-start | bytes 2162696 | tf_op jit(solution)/shard_map/ppermute | solution.py:349
  29.5 3.0 %collective-permute-start.13 = (bf16[256,768]{1,0:T(8,128)(2,1)S(1)}, bf16[256,768]{1,0:T(8,128)(2,1)S(1)}, u32[]{:S(2)}, u32[]{:S(2)}) collective-permute-start(bf16[256,768]{1,0:T(8,128)(2,1)S(1)} %get-tuple-element.69), channel_id=1, source_target_pairs={{0,1},{1,0},{2,3},{3,2},{4,5},{5,4},{6,7},{7,6},{8,9},{9,8},{10,11... | collective-permute-start | bytes 1179656 | tf_op jit(solution)/shard_map/ppermute | solution.py:349
  33.9 20.6 %collective-permute-start.14 = (bf16[352,768]{1,0:T(8,128)(2,1)S(1)}, bf16[352,768]{1,0:T(8,128)(2,1)S(1)}, u32[]{:S(2)}, u32[]{:S(2)}) collective-permute-start(bf16[352,768]{1,0:T(8,128)(2,1)S(1)} %get-tuple-element.71), channel_id=1, source_target_pairs={{0,32},{1,9},{2,34},{3,11},{4,36},{5,13},{6,38},{7,15},{8,40},{9,1... | collective-permute-start | bytes 1622024 | tf_op jit(solution)/shard_map/ppermute | solution.py:357
  35.6 21.1 %collective-permute-start.15 = (bf16[352,768]{1,0:T(8,128)(2,1)S(1)}, bf16[352,768]{1,0:T(8,128)(2,1)S(1)}, u32[]{:S(2)}, u32[]{:S(2)}) collective-permute-start(bf16[352,768]{1,0:T(8,128)(2,1)S(1)} %get-tuple-element.72), channel_id=1, source_target_pairs={{0,64},{1,17},{2,66},{3,19},{4,68},{5,21},{6,70},{7,23},{8,72},{9,... | collective-permute-start | bytes 1622024 | tf_op jit(solution)/shard_map/ppermute | solution.py:357
  38.9 17.8 %collective-permute-start.16 = (bf16[352,768]{1,0:T(8,128)(2,1)S(1)}, bf16[352,768]{1,0:T(8,128)(2,1)S(1)}, u32[]{:S(2)}, u32[]{:S(2)}) collective-permute-start(bf16[352,768]{1,0:T(8,128)(2,1)S(1)} %get-tuple-element.73), channel_id=1, source_target_pairs={{0,96},{1,25},{2,98},{3,27},{4,100},{5,29},{6,102},{7,31},{8,104},... | collective-permute-start | bytes 1622024 | tf_op jit(solution)/shard_map/ppermute | solution.py:357
  47.2 2.8 %collective-permute-start.17 = (f32[1,1408]{1,0:T(1,128)S(1)}, f32[1,1408]{1,0:T(1,128)S(1)}, u32[]{:S(2)}, u32[]{:S(2)}) collective-permute-start(f32[1,1408]{1,0:T(1,128)S(1)} %get-tuple-element.74), channel_id=1, source_target_pairs={{0,32},{1,9},{2,34},{3,11},{4,36},{5,13},{6,38},{7,15},{8,40},{9,1... | collective-permute-start | bytes 16904 | tf_op jit(solution)/shard_map/ppermute | solution.py:357
  50.0 4.4 %collective-permute-start.18 = (f32[1,1408]{1,0:T(1,128)S(1)}, f32[1,1408]{1,0:T(1,128)S(1)}, u32[]{:S(2)}, u32[]{:S(2)}) collective-permute-start(f32[1,1408]{1,0:T(1,128)S(1)} %add.3.refs_4_), channel_id=1, source_target_pairs={{0,96},{1,25},{2,98},{3,27},{4,100},{5,29},{6,102},{7,31},{8,104},... | collective-permute-start | bytes 16904 | tf_op jit(solution)/shard_map/ppermute | solution.py:357
  52.8 9.5 %collective-permute-start.8 = (bf16[64,1408]{1,0:T(8,128)(2,1)S(1)}, bf16[64,1408]{1,0:T(8,128)(2,1)S(1)}, u32[]{:S(2)}, u32[]{:S(2)}) collective-permute-start(bf16[64,1408]{1,0:T(8,128)(2,1)S(1)} %get-tuple-element.61), channel_id=1, source_target_pairs={{0,2},{1,3},{2,0},{3,1},{4,6},{5,7},{6,4},{7,5},{8,10},{9,11},{10,... | collective-permute-start | bytes 540680 | tf_op jit(solution)/shard_map/ppermute | solution.py:349
  54.4 7.9 %collective-permute-start.9 = (bf16[64,1408]{1,0:T(8,128)(2,1)S(1)}, bf16[64,1408]{1,0:T(8,128)(2,1)S(1)}, u32[]{:S(2)}, u32[]{:S(2)}) collective-permute-start(bf16[64,1408]{1,0:T(8,128)(2,1)S(1)} %get-tuple-element.62), channel_id=1, source_target_pairs={{0,4},{1,5},{2,6},{3,7},{4,0},{5,1},{6,2},{7,3},{8,12},{9,13},{10,... | collective-permute-start | bytes 540680 | tf_op jit(solution)/shard_map/ppermute | solution.py:349
  54.5 10.6 %collective-permute-start.10 = (bf16[64,1408]{1,0:T(8,128)(2,1)S(1)}, bf16[64,1408]{1,0:T(8,128)(2,1)S(1)}, u32[]{:S(2)}, u32[]{:S(2)}) collective-permute-start(bf16[64,1408]{1,0:T(8,128)(2,1)S(1)} %get-tuple-element.63), channel_id=1, source_target_pairs={{0,6},{1,7},{2,4},{3,5},{4,2},{5,3},{6,0},{7,1},{8,14},{9,15},{10,... | collective-permute-start | bytes 540680 | tf_op jit(solution)/shard_map/ppermute | solution.py:349
  57.8 13.9 %all-to-all-start = ((bf16[16,24,768]{2,1,0:T(8,128)(2,1)}), bf16[16,24,768]{2,1,0:T(8,128)(2,1)S(1)}, u32[]{:S(2)}, u32[]{:S(2)}) async-start(bf16[16,24,768]{2,1,0:T(8,128)(2,1)} %second.1), calls=%async_computation | async-start | bytes 1179648 | tf_op jit(solution)/shard_map/all_to_all | solution.py:366
  65.1 11.0 %collective-permute-start.11 = (bf16[4,32,1408]{2,1,0:T(8,128)(2,1)S(1)}, bf16[4,32,1408]{2,1,0:T(8,128)(2,1)S(1)}, u32[]{:S(2)}, u32[]{:S(2)}) collective-permute-start(bf16[4,32,1408]{2,1,0:T(8,128)(2,1)S(1)} %get-tuple-element.65), channel_id=1, source_target_pairs={{0,1},{1,0},{2,3},{3,2},{4,5},{5,4},{6,7},{7,6},{8,9},{9,8},{10,11... | collective-permute-start | bytes 1081352 | tf_op jit(solution)/shard_map/ppermute | solution.py:349
  71.7 5.3 %collective-permute-start.19 = (f32[16,768]{1,0:T(8,128)S(1)}, f32[16,768]{1,0:T(8,128)S(1)}, u32[]{:S(2)}, u32[]{:S(2)}) collective-permute-start(f32[16,768]{1,0:T(8,128)S(1)} %get-tuple-element.76), channel_id=1, source_target_pairs={{0,1},{1,0},{2,3},{3,2},{4,5},{5,4},{6,7},{7,6},{8,9},{9,8},{10,11... | collective-permute-start | bytes 147464 | tf_op jit(solution)/shard_map/ppermute | solution.py:349
  (1 other events, 1.1 us)

commit v5 on v4

--- a/solution.py
+++ b/solution.py
@@ -226,11 +226,17 @@
     theirs_ref[...] = dv_ref[:, pl.ds(pl.multiple_of((1 - core) * lead, 128), HALF)]
 
 
-def weight_body(nt_ref, nt_other_ref, dv_ref, dv_other_ref, *out_refs):
+def own_body(nt_ref, dv_ref, out_ref):
     for tile in range(HALF // TILE):
         cols = pl.ds(tile * TILE, TILE)
-        term = jnp.dot(nt_ref[...], dv_ref[:, cols], preferred_element_type=F32)
-        term += jnp.dot(nt_other_ref[...], dv_other_ref[:, cols], preferred_element_type=F32)
+        out_ref[:, cols] = jnp.dot(nt_ref[...], dv_ref[:, cols], preferred_element_type=F32)
+
+
+def weight_body(own_ref, nt_other_ref, dv_other_ref, *out_refs):
+    for tile in range(HALF // TILE):
+        cols = pl.ds(tile * TILE, TILE)
+        term = jnp.dot(nt_other_ref[...], dv_other_ref[:, cols], preferred_element_type=F32)
+        term += own_ref[:, cols]
         for j in range(4):
             out = out_refs[j]
             out[:, cols] = term[j * 4 * BLOCK : (j + 1) * 4 * BLOCK].astype(out.dtype)
@@ -476,6 +482,9 @@
         name="value",
     )(probs, *grads)
     other = swap_seq(theirs, 1)
+    own = call(
+        own_body, shape((D, HALF), F32), mib=16, flops=5 * 10**8, data=6 * 10**6, name="own"
+    )(nt, mine)
     terms = call(
         weight_body,
         four(4, (4 * BLOCK, HALF)),
@@ -483,7 +492,7 @@
         flops=11 * 10**8,
         data=6 * 10**6,
         name="weight",
-    )(nt, nt_other, mine, other)
+    )(own, nt_other, other)
     terms = [terms[0]] + [swap_plane(terms[j], j) for j in range(1, 4)]
 
     results = call(

time: 78 us -> 78.1 us (level)
    unnamed x8 -> x6, local copies, waits for them, and re-layouts: 6.59 us -> 6.59 us
  transfers between devices with their start and end apart: 21 -> 21, of which waited for: 8 -> 8; matrix products, arithmetic and copies ran while one was open for 0% -> 1% of each run, Pallas kernels for 24% -> 24%
where the time goes in v5:
time: 78.1 us; the launch traced here: 77.7 us
  starting transfers between devices  33.9 us (43%)
  Pallas kernels  20.4 us (26%)
  waiting for transfers between devices  14.7 us (19%)
  local copies, waits for them, and re-layouts  7.29 us (9%)
  between operations  1.45 us (2%)
    ppermute x15, starting transfers between devices, swap_seq(): return lax.ppermute(value, 'seq', [(i, i ^ k) for i in range(SLOTS)])  21.5 us
    pallas_call x1, Pallas kernels, shards(): call(input_body, [shape((PAIR, D), BF)] * CHIPS + [shape((1, D), F32)], s...  8.23 us
    ppermute x5, starting transfers between devices, swap_plane(): return lax.ppermute(value, ('dp', 'seq'), pairs)  7.85 us
    unnamed x6, local copies, waits for them, and re-layouts  6.59 us
    ppermute x15, waiting for transfers between devices, swap_seq(): return lax.ppermute(value, 'seq', [(i, i ^ k) for i in range(SLOTS)])  6.02 us
    pallas_call x1, Pallas kernels, shards(): call(project_body, [shape((ROWS, PADDED), BF), shape((HEADS, HALVES, SPAN...  4.77 us
    all_to_all x1, starting transfers between devices, exchange_plane(): lax.all_to_all(blocks, ('dp', 'seq'), split_axis=0, concat_axis=0, tiled=...  4.56 us
    ppermute x5, waiting for transfers between devices, swap_plane(): return lax.ppermute(value, ('dp', 'seq'), pairs)  4.48 us
  transfers between devices with their start and end apart: 21, of which 8 were waited for; matrix products, arithmetic and copies ran while one was open for 1% of the time, Pallas kernels for 24%

profile of v5, /device:TPU:1, one launch (start us, length us, event | category | flops | bytes accessed | tf_op | source)
XLA Modules:
  0.0 77.7 jit_solution(14564414571564709012)
XLA Ops:
  1.3 1.1 %copy-done.1 = bf16[1,1,256,1408]{3,2,1,0:T(8,128)(2,1)S(1)} copy-done((bf16[1,1,256,1408]{3,2,1,0:T(8,128)(2,1)S(1)}, bf16[1,1,256,1408]{3,2,1,0:T(8,128)(2,1)}, u32[]{:S(2)}) %copy-start.1) | copy-done | bytes 720920
  2.5 1.5 %collective-permute-start = (bf16[4,32,1536]{2,1,0:T(8,128)(2,1)S(1)}, bf16[4,32,1536]{2,1,0:T(8,128)(2,1)S(1)}, u32[]{:S(2)}, u32[]{:S(2)}) collective-permute-start(bf16[4,32,1536]{2,1,0:T(8,128)(2,1)S(1)} %get-tuple-element.42), channel_id=1, source_target_pairs={{0,1},{1,0},{2,3},{3,2},{4,5},{5,4},{6,7},{7,6},{8,9},{9,8},{10,11... | collective-permute-start | bytes 1179656 | tf_op jit(solution)/shard_map/ppermute | solution.py:355
  4.0 1.1 %copy-done.2 = bf16[1,1,256,1408]{3,2,1,0:T(8,128)(2,1)S(1)} copy-done((bf16[1,1,256,1408]{3,2,1,0:T(8,128)(2,1)S(1)}, bf16[1,1,256,1408]{3,2,1,0:T(8,128)(2,1)}, u32[]{:S(2)}) %copy-start.2) | copy-done | bytes 720920
  5.4 1.4 %collective-permute-start.1 = (bf16[64,1536]{1,0:T(8,128)(2,1)S(1)}, bf16[64,1536]{1,0:T(8,128)(2,1)S(1)}, u32[]{:S(2)}, u32[]{:S(2)}) collective-permute-start(bf16[64,1536]{1,0:T(8,128)(2,1)S(1)} %get-tuple-element.44), channel_id=1, source_target_pairs={{0,2},{1,3},{2,0},{3,1},{4,6},{5,7},{6,4},{7,5},{8,10},{9,11},{10,... | collective-permute-start | bytes 589832 | tf_op jit(solution)/shard_map/ppermute | solution.py:355
  6.8 2.5 %collective-permute-start.2 = (bf16[64,1536]{1,0:T(8,128)(2,1)S(1)}, bf16[64,1536]{1,0:T(8,128)(2,1)S(1)}, u32[]{:S(2)}, u32[]{:S(2)}) collective-permute-start(bf16[64,1536]{1,0:T(8,128)(2,1)S(1)} %get-tuple-element.45), channel_id=1, source_target_pairs={{0,4},{1,5},{2,6},{3,7},{4,0},{5,1},{6,2},{7,3},{8,12},{9,13},{10,... | collective-permute-start | bytes 589832 | tf_op jit(solution)/shard_map/ppermute | solution.py:355
  10.0 4.4 %copy-done = bf16[1408,4224]{1,0:T(8,128)(2,1)S(1)} copy-done((bf16[1408,4224]{1,0:T(8,128)(2,1)S(1)}, bf16[1408,4224]{1,0:T(8,128)(2,1)}, u32[]{:S(2)}) %copy-start) | copy-done | bytes 11894808
  15.6 3.7 %collective-permute-start.6 = (bf16[64,1408]{1,0:T(8,128)(2,1)S(1)}, bf16[64,1408]{1,0:T(8,128)(2,1)S(1)}, u32[]{:S(2)}, u32[]{:S(2)}) collective-permute-start(bf16[64,1408]{1,0:T(8,128)(2,1)S(1)} %get-tuple-element.56), channel_id=1, source_target_pairs={{0,4},{1,5},{2,6},{3,7},{4,0},{5,1},{6,2},{7,3},{8,12},{9,13},{10,... | collective-permute-start | bytes 540680 | tf_op jit(solution)/shard_map/ppermute | solution.py:355
  21.6 1.6 %collective-permute-start.12 = (bf16[1408,256]{1,0:T(8,128)(2,1)S(1)}, bf16[1408,256]{1,0:T(8,128)(2,1)S(1)}, u32[]{:S(2)}, u32[]{:S(2)}) collective-permute-start(bf16[1408,256]{1,0:T(8,128)(2,1)S(1)} %get-tuple-element.68), channel_id=1, source_target_pairs={{0,1},{1,0},{2,3},{3,2},{4,5},{5,4},{6,7},{7,6},{8,9},{9,8},{10,11... | collective-permute-start | bytes 2162696 | tf_op jit(solution)/shard_map/ppermute | solution.py:355
  23.2 4.8 %project.1 = (bf16[256,4352]{1,0:T(8,128)(2,1)S(1)}, f32[16,2,128,128]{3,2,1,0:T(8,128)S(1)}, bf16[16,2,128,128]{3,2,1,0:T(8,128)(2,1)S(1)}) custom-call(f32[128,128]{1,0:T(8,128)S(1)} %get-tuple-element.47.clip_ref, bf16[256,1408]{1,0:T(8,128)(2,1)S(1)} %get-tuple-element.48.normed_ref, bf16[1408,4224]{1,0:T(8,128)(2,1)S(1)} %load.1.refs_5_.wbuf.refs_9_), custom_call_target="tpu_custom_call" | custom-call | flops 5000000000 | bytes 40000000 | tf_op jit(solution)/shard_map/project/pallas_call | solution.py:454
  28.0 1.5 %collective-permute-done.7.refs_3_ = bf16[64,1408]{1,0:T(8,128)(2,1)S(1)} collective-permute-done((bf16[64,1408]{1,0:T(8,128)(2,1)S(1)}, bf16[64,1408]{1,0:T(8,128)(2,1)S(1)}, u32[]{:S(2)}, u32[]{:S(2)}) %collective-permute-start.7) | collective-permute-done | bytes 180256 | tf_op jit(solution)/shard_map/ppermute | solution.py:355
  30.2 1.7 %collective-permute-start.13 = (bf16[256,768]{1,0:T(8,128)(2,1)S(1)}, bf16[256,768]{1,0:T(8,128)(2,1)S(1)}, u32[]{:S(2)}, u32[]{:S(2)}) collective-permute-start(bf16[256,768]{1,0:T(8,128)(2,1)S(1)} %get-tuple-element.69), channel_id=1, source_target_pairs={{0,1},{1,0},{2,3},{3,2},{4,5},{5,4},{6,7},{7,6},{8,9},{9,8},{10,11... | collective-permute-start | bytes 1179656 | tf_op jit(solution)/shard_map/ppermute | solution.py:355
  34.0 1.7 %collective-permute-start.14 = (bf16[352,768]{1,0:T(8,128)(2,1)S(1)}, bf16[352,768]{1,0:T(8,128)(2,1)S(1)}, u32[]{:S(2)}, u32[]{:S(2)}) collective-permute-start(bf16[352,768]{1,0:T(8,128)(2,1)S(1)} %get-tuple-element.71), channel_id=1, source_target_pairs={{0,32},{1,9},{2,34},{3,11},{4,36},{5,13},{6,38},{7,15},{8,40},{9,1... | collective-permute-start | bytes 1622024 | tf_op jit(solution)/shard_map/ppermute | solution.py:363
  35.7 3.3 %collective-permute-start.15 = (bf16[352,768]{1,0:T(8,128)(2,1)S(1)}, bf16[352,768]{1,0:T(8,128)(2,1)S(1)}, u32[]{:S(2)}, u32[]{:S(2)}) collective-permute-start(bf16[352,768]{1,0:T(8,128)(2,1)S(1)} %get-tuple-element.72), channel_id=1, source_target_pairs={{0,64},{1,17},{2,66},{3,19},{4,68},{5,21},{6,70},{7,23},{8,72},{9,... | collective-permute-start | bytes 1622024 | tf_op jit(solution)/shard_map/ppermute | solution.py:363
  39.0 8.2 %input.1 = (bf16[64,1408]{1,0:T(8,128)(2,1)S(1)}, bf16[64,1408]{1,0:T(8,128)(2,1)S(1)}, bf16[64,1408]{1,0:T(8,128)(2,1)S(1)}, bf16[64,1408]{1,0:T(8,128)(2,1)S(1)}, f32[1,1408]{1,0:T(1,128)S(1)}) custom-call(bf16[64,1536]{1,0:T(8,128)(2,1)S(1)} %get-tuple-element.43.refs_0_, bf16[64,1536]{1,0:T(8,128)(2,1)S(1)} %collective-permute-done.1.refs_1_.refs_0_, ...), custom_call_target="tpu_custom_call" | custom-call | flops 6000000000 | bytes 20000000 | tf_op jit(solution)/shard_map/input/pallas_call | solution.py:498
  47.3 2.8 %collective-permute-done.17 = f32[1,1408]{1,0:T(1,128)S(1)} collective-permute-done((f32[1,1408]{1,0:T(1,128)S(1)}, f32[1,1408]{1,0:T(1,128)S(1)}, u32[]{:S(2)}, u32[]{:S(2)}) %collective-permute-start.17) | collective-permute-done | bytes 5664 | tf_op jit(solution)/shard_map/ppermute | solution.py:363
  50.1 2.7 %collective-permute-start.18 = (f32[1,1408]{1,0:T(1,128)S(1)}, f32[1,1408]{1,0:T(1,128)S(1)}, u32[]{:S(2)}, u32[]{:S(2)}) collective-permute-start(f32[1,1408]{1,0:T(1,128)S(1)} %add.3.refs_4_), channel_id=1, source_target_pairs={{0,96},{1,25},{2,98},{3,27},{4,100},{5,29},{6,102},{7,31},{8,104},... | collective-permute-start | bytes 16904 | tf_op jit(solution)/shard_map/ppermute | solution.py:363
  52.8 1.7 %collective-permute-done.18.refs_5_ = f32[1,1408]{1,0:T(1,128)S(1)} collective-permute-done((f32[1,1408]{1,0:T(1,128)S(1)}, f32[1,1408]{1,0:T(1,128)S(1)}, u32[]{:S(2)}, u32[]{:S(2)}) %collective-permute-start.18) | collective-permute-done | bytes 5664 | tf_op jit(solution)/shard_map/ppermute | solution.py:363
  54.5 2.1 %collective-permute-start.10 = (bf16[64,1408]{1,0:T(8,128)(2,1)S(1)}, bf16[64,1408]{1,0:T(8,128)(2,1)S(1)}, u32[]{:S(2)}, u32[]{:S(2)}) collective-permute-start(bf16[64,1408]{1,0:T(8,128)(2,1)S(1)} %get-tuple-element.63), channel_id=1, source_target_pairs={{0,6},{1,7},{2,4},{3,5},{4,2},{5,3},{6,0},{7,1},{8,14},{9,15},{10,... | collective-permute-start | bytes 540680 | tf_op jit(solution)/shard_map/ppermute | solution.py:355
  56.7 1.1 %second.1 = bf16[16,24,768]{2,1,0:T(8,128)(2,1)} custom-call(f32[352,768]{1,0:T(8,128)S(1)} %get-tuple-element.70.refs_0_, bf16[352,768]{1,0:T(8,128)(2,1)S(1)} %collective-permute-done.14.refs_1_, bf16[352,768]{1,0:T(8,128)(2,1)S(1)} %collective-permute-done.15.refs_2_, bf16[352,768]{1,0:T(8,128)(2,1)S(1)} %collective-permute-done.16.refs_3_, ...), custom_call_target="tpu_custom_call" | custom-call | bytes 5000000 | tf_op jit(solution)/shard_map/second/pallas_call | solution.py:516
  57.8 4.6 %all-to-all-start = ((bf16[16,24,768]{2,1,0:T(8,128)(2,1)}), bf16[16,24,768]{2,1,0:T(8,128)(2,1)S(1)}, u32[]{:S(2)}, u32[]{:S(2)}) async-start(bf16[16,24,768]{2,1,0:T(8,128)(2,1)} %second.1), calls=%async_computation | async-start | bytes 1179648 | tf_op jit(solution)/shard_map/all_to_all | solution.py:372
  62.4 2.8 %collective-permute-done.10.refs_3_ = bf16[64,1408]{1,0:T(8,128)(2,1)S(1)} collective-permute-done((bf16[64,1408]{1,0:T(8,128)(2,1)S(1)}, bf16[64,1408]{1,0:T(8,128)(2,1)S(1)}, u32[]{:S(2)}, u32[]{:S(2)}) %collective-permute-start.10) | collective-permute-done | bytes 180256 | tf_op jit(solution)/shard_map/ppermute | solution.py:355
  65.2 2.3 %collective-permute-start.11 = (bf16[4,32,1408]{2,1,0:T(8,128)(2,1)S(1)}, bf16[4,32,1408]{2,1,0:T(8,128)(2,1)S(1)}, u32[]{:S(2)}, u32[]{:S(2)}) collective-permute-start(bf16[4,32,1408]{2,1,0:T(8,128)(2,1)S(1)} %get-tuple-element.65), channel_id=1, source_target_pairs={{0,1},{1,0},{2,3},{3,2},{4,5},{5,4},{6,7},{7,6},{8,9},{9,8},{10,11... | collective-permute-start | bytes 1081352 | tf_op jit(solution)/shard_map/ppermute | solution.py:355
  67.5 4.2 %all-to-all-done.parts_ref = bf16[16,24,768]{2,1,0:T(8,128)(2,1)S(1)} async-done(((bf16[16,24,768]{2,1,0:T(8,128)(2,1)}), bf16[16,24,768]{2,1,0:T(8,128)(2,1)S(1)}, u32[]{:S(2)}, u32[]{:S(2)}) %all-to-all-start) | async-done | bytes 589856 | tf_op jit(solution)/shard_map/all_to_all | solution.py:372
  71.8 4.3 %collective-permute-start.19 = (f32[16,768]{1,0:T(8,128)S(1)}, f32[16,768]{1,0:T(8,128)S(1)}, u32[]{:S(2)}, u32[]{:S(2)}) collective-permute-start(f32[16,768]{1,0:T(8,128)S(1)} %get-tuple-element.76), channel_id=1, source_target_pairs={{0,1},{1,0},{2,3},{3,2},{4,5},{5,4},{6,7},{7,6},{8,9},{9,8},{10,11... | collective-permute-start | bytes 147464 | tf_op jit(solution)/shard_map/ppermute | solution.py:355
  (43 shorter events, 9.3 us)
Async XLA Ops:
  1.3 1.1 %copy-start.1 = (bf16[1,1,256,1408]{3,2,1,0:T(8,128)(2,1)S(1)}, bf16[1,1,256,1408]{3,2,1,0:T(8,128)(2,1)}, u32[]{:S(2)}) copy-start(bf16[1,1,256,1408]{3,2,1,0:T(8,128)(2,1)} %param.5) | copy-start | bytes 2162692
  2.5 2.9 %collective-permute-start = (bf16[4,32,1536]{2,1,0:T(8,128)(2,1)S(1)}, bf16[4,32,1536]{2,1,0:T(8,128)(2,1)S(1)}, u32[]{:S(2)}, u32[]{:S(2)}) collective-permute-start(bf16[4,32,1536]{2,1,0:T(8,128)(2,1)S(1)} %get-tuple-element.42), channel_id=1, source_target_pairs={{0,1},{1,0},{2,3},{3,2},{4,5},{5,4},{6,7},{7,6},{8,9},{9,8},{10,11... | collective-permute-start | bytes 1179656 | tf_op jit(solution)/shard_map/ppermute | solution.py:355
  4.0 1.1 %copy-start.2 = (bf16[1,1,256,1408]{3,2,1,0:T(8,128)(2,1)S(1)}, bf16[1,1,256,1408]{3,2,1,0:T(8,128)(2,1)}, u32[]{:S(2)}) copy-start(bf16[1,1,256,1408]{3,2,1,0:T(8,128)(2,1)} %param.9) | copy-start | bytes 2162692
  5.1 10.2 %collective-permute-start.4 = (bf16[4,32,1408]{2,1,0:T(8,128)(2,1)S(1)}, bf16[4,32,1408]{2,1,0:T(8,128)(2,1)S(1)}, u32[]{:S(2)}, u32[]{:S(2)}) collective-permute-start(bf16[4,32,1408]{2,1,0:T(8,128)(2,1)S(1)} %get-tuple-element.53), channel_id=1, source_target_pairs={{0,1},{1,0},{2,3},{3,2},{4,5},{5,4},{6,7},{7,6},{8,9},{9,8},{10,11... | collective-permute-start | bytes 1081352 | tf_op jit(solution)/shard_map/ppermute | solution.py:355
  5.4 10.0 %collective-permute-start.1 = (bf16[64,1536]{1,0:T(8,128)(2,1)S(1)}, bf16[64,1536]{1,0:T(8,128)(2,1)S(1)}, u32[]{:S(2)}, u32[]{:S(2)}) collective-permute-start(bf16[64,1536]{1,0:T(8,128)(2,1)S(1)} %get-tuple-element.44), channel_id=1, source_target_pairs={{0,2},{1,3},{2,0},{3,1},{4,6},{5,7},{6,4},{7,5},{8,10},{9,11},{10,... | collective-permute-start | bytes 589832 | tf_op jit(solution)/shard_map/ppermute | solution.py:355
  6.8 12.6 %collective-permute-start.2 = (bf16[64,1536]{1,0:T(8,128)(2,1)S(1)}, bf16[64,1536]{1,0:T(8,128)(2,1)S(1)}, u32[]{:S(2)}, u32[]{:S(2)}) collective-permute-start(bf16[64,1536]{1,0:T(8,128)(2,1)S(1)} %get-tuple-element.45), channel_id=1, source_target_pairs={{0,4},{1,5},{2,6},{3,7},{4,0},{5,1},{6,2},{7,3},{8,12},{9,13},{10,... | collective-permute-start | bytes 589832 | tf_op jit(solution)/shard_map/ppermute | solution.py:355
  9.2 11.2 %collective-permute-start.3 = (bf16[64,1536]{1,0:T(8,128)(2,1)S(1)}, bf16[64,1536]{1,0:T(8,128)(2,1)S(1)}, u32[]{:S(2)}, u32[]{:S(2)}) collective-permute-start(bf16[64,1536]{1,0:T(8,128)(2,1)S(1)} %get-tuple-element.46), channel_id=1, source_target_pairs={{0,6},{1,7},{2,4},{3,5},{4,2},{5,3},{6,0},{7,1},{8,14},{9,15},{10,... | collective-permute-start | bytes 589832 | tf_op jit(solution)/shard_map/ppermute | solution.py:355
  10.0 4.4 %copy-start = (bf16[1408,4224]{1,0:T(8,128)(2,1)S(1)}, bf16[1408,4224]{1,0:T(8,128)(2,1)}, u32[]{:S(2)}) copy-start(bf16[1408,4224]{1,0:T(8,128)(2,1)} %w_hbm.1) | copy-start | bytes 35684356
  15.4 12.5 %collective-permute-start.5 = (bf16[64,1408]{1,0:T(8,128)(2,1)S(1)}, bf16[64,1408]{1,0:T(8,128)(2,1)S(1)}, u32[]{:S(2)}, u32[]{:S(2)}) collective-permute-start(bf16[64,1408]{1,0:T(8,128)(2,1)S(1)} %get-tuple-element.55), channel_id=1, source_target_pairs={{0,2},{1,3},{2,0},{3,1},{4,6},{5,7},{6,4},{7,5},{8,10},{9,11},{10,... | collective-permute-start | bytes 540680 | tf_op jit(solution)/shard_map/ppermute | solution.py:355
  15.6 12.3 %collective-permute-start.6 = (bf16[64,1408]{1,0:T(8,128)(2,1)S(1)}, bf16[64,1408]{1,0:T(8,128)(2,1)S(1)}, u32[]{:S(2)}, u32[]{:S(2)}) collective-permute-start(bf16[64,1408]{1,0:T(8,128)(2,1)S(1)} %get-tuple-element.56), channel_id=1, source_target_pairs={{0,4},{1,5},{2,6},{3,7},{4,0},{5,1},{6,2},{7,3},{8,12},{9,13},{10,... | collective-permute-start | bytes 540680 | tf_op jit(solution)/shard_map/ppermute | solution.py:355
  19.3 10.1 %collective-permute-start.7 = (bf16[64,1408]{1,0:T(8,128)(2,1)S(1)}, bf16[64,1408]{1,0:T(8,128)(2,1)S(1)}, u32[]{:S(2)}, u32[]{:S(2)}) collective-permute-start(bf16[64,1408]{1,0:T(8,128)(2,1)S(1)} %get-tuple-element.57), channel_id=1, source_target_pairs={{0,6},{1,7},{2,4},{3,5},{4,2},{5,3},{6,0},{7,1},{8,14},{9,15},{10,... | collective-permute-start | bytes 540680 | tf_op jit(solution)/shard_map/ppermute | solution.py:355
  21.6 11.7 %collective-permute-start.12 = (bf16[1408,256]{1,0:T(8,128)(2,1)S(1)}, bf16[1408,256]{1,0:T(8,128)(2,1)S(1)}, u32[]{:S(2)}, u32[]{:S(2)}) collective-permute-start(bf16[1408,256]{1,0:T(8,128)(2,1)S(1)} %get-tuple-element.68), channel_id=1, source_target_pairs={{0,1},{1,0},{2,3},{3,2},{4,5},{5,4},{6,7},{7,6},{8,9},{9,8},{10,11... | collective-permute-start | bytes 2162696 | tf_op jit(solution)/shard_map/ppermute | solution.py:355
  30.2 3.0 %collective-permute-start.13 = (bf16[256,768]{1,0:T(8,128)(2,1)S(1)}, bf16[256,768]{1,0:T(8,128)(2,1)S(1)}, u32[]{:S(2)}, u32[]{:S(2)}) collective-permute-start(bf16[256,768]{1,0:T(8,128)(2,1)S(1)} %get-tuple-element.69), channel_id=1, source_target_pairs={{0,1},{1,0},{2,3},{3,2},{4,5},{5,4},{6,7},{7,6},{8,9},{9,8},{10,11... | collective-permute-start | bytes 1179656 | tf_op jit(solution)/shard_map/ppermute | solution.py:355
  34.0 20.6 %collective-permute-start.14 = (bf16[352,768]{1,0:T(8,128)(2,1)S(1)}, bf16[352,768]{1,0:T(8,128)(2,1)S(1)}, u32[]{:S(2)}, u32[]{:S(2)}) collective-permute-start(bf16[352,768]{1,0:T(8,128)(2,1)S(1)} %get-tuple-element.71), channel_id=1, source_target_pairs={{0,32},{1,9},{2,34},{3,11},{4,36},{5,13},{6,38},{7,15},{8,40},{9,1... | collective-permute-start | bytes 1622024 | tf_op jit(solution)/shard_map/ppermute | solution.py:363
  35.7 21.0 %collective-permute-start.15 = (bf16[352,768]{1,0:T(8,128)(2,1)S(1)}, bf16[352,768]{1,0:T(8,128)(2,1)S(1)}, u32[]{:S(2)}, u32[]{:S(2)}) collective-permute-start(bf16[352,768]{1,0:T(8,128)(2,1)S(1)} %get-tuple-element.72), channel_id=1, source_target_pairs={{0,64},{1,17},{2,66},{3,19},{4,68},{5,21},{6,70},{7,23},{8,72},{9,... | collective-permute-start | bytes 1622024 | tf_op jit(solution)/shard_map/ppermute | solution.py:363
  39.0 17.7 %collective-permute-start.16 = (bf16[352,768]{1,0:T(8,128)(2,1)S(1)}, bf16[352,768]{1,0:T(8,128)(2,1)S(1)}, u32[]{:S(2)}, u32[]{:S(2)}) collective-permute-start(bf16[352,768]{1,0:T(8,128)(2,1)S(1)} %get-tuple-element.73), channel_id=1, source_target_pairs={{0,96},{1,25},{2,98},{3,27},{4,100},{5,29},{6,102},{7,31},{8,104},... | collective-permute-start | bytes 1622024 | tf_op jit(solution)/shard_map/ppermute | solution.py:363
  47.2 2.8 %collective-permute-start.17 = (f32[1,1408]{1,0:T(1,128)S(1)}, f32[1,1408]{1,0:T(1,128)S(1)}, u32[]{:S(2)}, u32[]{:S(2)}) collective-permute-start(f32[1,1408]{1,0:T(1,128)S(1)} %get-tuple-element.74), channel_id=1, source_target_pairs={{0,32},{1,9},{2,34},{3,11},{4,36},{5,13},{6,38},{7,15},{8,40},{9,1... | collective-permute-start | bytes 16904 | tf_op jit(solution)/shard_map/ppermute | solution.py:363
  50.1 4.5 %collective-permute-start.18 = (f32[1,1408]{1,0:T(1,128)S(1)}, f32[1,1408]{1,0:T(1,128)S(1)}, u32[]{:S(2)}, u32[]{:S(2)}) collective-permute-start(f32[1,1408]{1,0:T(1,128)S(1)} %add.3.refs_4_), channel_id=1, source_target_pairs={{0,96},{1,25},{2,98},{3,27},{4,100},{5,29},{6,102},{7,31},{8,104},... | collective-permute-start | bytes 16904 | tf_op jit(solution)/shard_map/ppermute | solution.py:363
  52.8 9.6 %collective-permute-start.8 = (bf16[64,1408]{1,0:T(8,128)(2,1)S(1)}, bf16[64,1408]{1,0:T(8,128)(2,1)S(1)}, u32[]{:S(2)}, u32[]{:S(2)}) collective-permute-start(bf16[64,1408]{1,0:T(8,128)(2,1)S(1)} %get-tuple-element.61), channel_id=1, source_target_pairs={{0,2},{1,3},{2,0},{3,1},{4,6},{5,7},{6,4},{7,5},{8,10},{9,11},{10,... | collective-permute-start | bytes 540680 | tf_op jit(solution)/shard_map/ppermute | solution.py:355
  54.5 7.9 %collective-permute-start.9 = (bf16[64,1408]{1,0:T(8,128)(2,1)S(1)}, bf16[64,1408]{1,0:T(8,128)(2,1)S(1)}, u32[]{:S(2)}, u32[]{:S(2)}) collective-permute-start(bf16[64,1408]{1,0:T(8,128)(2,1)S(1)} %get-tuple-element.62), channel_id=1, source_target_pairs={{0,4},{1,5},{2,6},{3,7},{4,0},{5,1},{6,2},{7,3},{8,12},{9,13},{10,... | collective-permute-start | bytes 540680 | tf_op jit(solution)/shard_map/ppermute | solution.py:355
  54.5 10.6 %collective-permute-start.10 = (bf16[64,1408]{1,0:T(8,128)(2,1)S(1)}, bf16[64,1408]{1,0:T(8,128)(2,1)S(1)}, u32[]{:S(2)}, u32[]{:S(2)}) collective-permute-start(bf16[64,1408]{1,0:T(8,128)(2,1)S(1)} %get-tuple-element.63), channel_id=1, source_target_pairs={{0,6},{1,7},{2,4},{3,5},{4,2},{5,3},{6,0},{7,1},{8,14},{9,15},{10,... | collective-permute-start | bytes 540680 | tf_op jit(solution)/shard_map/ppermute | solution.py:355
  57.8 13.9 %all-to-all-start = ((bf16[16,24,768]{2,1,0:T(8,128)(2,1)}), bf16[16,24,768]{2,1,0:T(8,128)(2,1)S(1)}, u32[]{:S(2)}, u32[]{:S(2)}) async-start(bf16[16,24,768]{2,1,0:T(8,128)(2,1)} %second.1), calls=%async_computation | async-start | bytes 1179648 | tf_op jit(solution)/shard_map/all_to_all | solution.py:372
  65.2 10.9 %collective-permute-start.11 = (bf16[4,32,1408]{2,1,0:T(8,128)(2,1)S(1)}, bf16[4,32,1408]{2,1,0:T(8,128)(2,1)S(1)}, u32[]{:S(2)}, u32[]{:S(2)}) collective-permute-start(bf16[4,32,1408]{2,1,0:T(8,128)(2,1)S(1)} %get-tuple-element.65), channel_id=1, source_target_pairs={{0,1},{1,0},{2,3},{3,2},{4,5},{5,4},{6,7},{7,6},{8,9},{9,8},{10,11... | collective-permute-start | bytes 1081352 | tf_op jit(solution)/shard_map/ppermute | solution.py:355
  71.8 5.3 %collective-permute-start.19 = (f32[16,768]{1,0:T(8,128)S(1)}, f32[16,768]{1,0:T(8,128)S(1)}, u32[]{:S(2)}, u32[]{:S(2)}) collective-permute-start(f32[16,768]{1,0:T(8,128)S(1)} %get-tuple-element.76), channel_id=1, source_target_pairs={{0,1},{1,0},{2,3},{3,2},{4,5},{5,4},{6,7},{7,6},{8,9},{9,8},{10,11... | collective-permute-start | bytes 147464 | tf_op jit(solution)/shard_map/ppermute | solution.py:355

commit v6 on v5

--- a/solution.py
+++ b/solution.py
@@ -22,6 +22,7 @@
 HALVES = 2
 STEP = 16
 SPAN = 128
+EARLY = 768
 TILE = 256
 BLOCK = 88
 HALF = 768
@@ -159,8 +160,9 @@
 
 
 def project_body(clip_ref, normed_ref, wbuf, qkv_ref, soft_ref, prob_ref, bias_ref):
-    first = [(0, 512), (512, 1152), (1664, 1152)]
-    rest = [(2816, 384), (3200, 384), (3584, 384), (3968, 256)]
+    first = [(0, EARLY), (D, EARLY)]
+    rest = {1: (EARLY, D - EARLY), 4: (D + EARLY, D - EARLY)}
+    rest.update({7: (2 * D, 512), 10: (2 * D + 512, 512), 13: (2 * D + 1024, 384)})
 
     def project(start, count):
         cols = pl.ds(start, count)
@@ -173,6 +175,7 @@
     kept = (clip == jnp.transpose(clip)) & (row % STEP == col % STEP)
     bias_ref[...] = jnp.where(kept, 0.0, MASKED).astype(F32)
     qkv_ref[:, pl.ds(TRIPLE, 128)] = jnp.zeros((ROWS, 128), BF)
+    qkv_ref[:, pl.ds(2 * D, 128)] = jnp.zeros((ROWS, 128), BF)
 
     for start, count in first:
         project(start, count)
@@ -192,11 +195,10 @@
             soft_ref[head, half] = softmaxed
             prob_ref[head, half] = softmaxed.astype(BF)
 
-    qkv_ref[:, pl.ds(2 * D, 128)] = jnp.zeros((ROWS, 128), BF)
     for head in range(HEADS):
         attend(head)
-        if head % 4 == 3:
-            project(*rest[head // 4])
+        if head in rest:
+            project(*rest[head])
 
 
 def value_body(prob_ref, *refs):
@@ -423,7 +425,7 @@
     gain = norm_gain.reshape(1, D)
 
     x = spread(block_input.reshape(ROWS, D), frame_clip)
-    grads = spread(out_grad.reshape(ROWS, D), after=x[1:2])
+    grads = spread(out_grad.reshape(ROWS, D))
 
     weight = call(
         load_body,

time: 78.1 us -> 78.1 us (level)
  no operation moved by 1% of the time
where the time goes in v6:
time: 78.1 us; the launch traced here: 77.8 us
  starting transfers between devices  33.9 us (43%)
  Pallas kernels  20.2 us (26%)
  waiting for transfers between devices  14.9 us (19%)
  local copies, waits for them, and re-layouts  7.29 us (9%)
  between operations  1.44 us (2%)
    ppermute x15, starting transfers between devices, swap_seq(): return lax.ppermute(value, 'seq', [(i, i ^ k) for i in range(SLOTS)])  21.5 us
    pallas_call x1, Pallas kernels, shards(): call(input_body, [shape((PAIR, D), BF)] * CHIPS + [shape((1, D), F32)], s...  8.23 us
    ppermute x5, starting transfers between devices, swap_plane(): return lax.ppermute(value, ('dp', 'seq'), pairs)  7.86 us
    unnamed x6, local copies, waits for them, and re-layouts  6.59 us
    ppermute x15, waiting for transfers between devices, swap_seq(): return lax.ppermute(value, 'seq', [(i, i ^ k) for i in range(SLOTS)])  6.19 us
    pallas_call x1, Pallas kernels, shards(): call(project_body, [shape((ROWS, PADDED), BF), shape((HEADS, HALVES, SPAN...  4.61 us
    all_to_all x1, starting transfers between devices, exchange_plane(): lax.all_to_all(blocks, ('dp', 'seq'), split_axis=0, concat_axis=0, tiled=...  4.55 us
    ppermute x5, waiting for transfers between devices, swap_plane(): return lax.ppermute(value, ('dp', 'seq'), pairs)  4.48 us
  transfers between devices with their start and end apart: 21, of which 8 were waited for; matrix products, arithmetic and copies ran while one was open for 1% of the time, Pallas kernels for 24%

profile of v6, /device:TPU:1, one launch (start us, length us, event | category | flops | bytes accessed | tf_op | source)
XLA Modules:
  0.0 77.8 jit_solution(183065051333916771)
XLA Ops:
  1.3 1.1 %copy-done.1 = bf16[1,1,256,1408]{3,2,1,0:T(8,128)(2,1)S(1)} copy-done((bf16[1,1,256,1408]{3,2,1,0:T(8,128)(2,1)S(1)}, bf16[1,1,256,1408]{3,2,1,0:T(8,128)(2,1)}, u32[]{:S(2)}) %copy-start.1) | copy-done | bytes 720920
  2.5 1.5 %collective-permute-start = (bf16[4,32,1536]{2,1,0:T(8,128)(2,1)S(1)}, bf16[4,32,1536]{2,1,0:T(8,128)(2,1)S(1)}, u32[]{:S(2)}, u32[]{:S(2)}) collective-permute-start(bf16[4,32,1536]{2,1,0:T(8,128)(2,1)S(1)} %get-tuple-element.42), channel_id=1, source_target_pairs={{0,1},{1,0},{2,3},{3,2},{4,5},{5,4},{6,7},{7,6},{8,9},{9,8},{10,11... | collective-permute-start | bytes 1179656 | tf_op jit(solution)/shard_map/ppermute | solution.py:357
  4.0 1.1 %copy-done.2 = bf16[1,1,256,1408]{3,2,1,0:T(8,128)(2,1)S(1)} copy-done((bf16[1,1,256,1408]{3,2,1,0:T(8,128)(2,1)S(1)}, bf16[1,1,256,1408]{3,2,1,0:T(8,128)(2,1)}, u32[]{:S(2)}) %copy-start.2) | copy-done | bytes 720920
  5.4 1.4 %collective-permute-start.1 = (bf16[64,1536]{1,0:T(8,128)(2,1)S(1)}, bf16[64,1536]{1,0:T(8,128)(2,1)S(1)}, u32[]{:S(2)}, u32[]{:S(2)}) collective-permute-start(bf16[64,1536]{1,0:T(8,128)(2,1)S(1)} %get-tuple-element.44), channel_id=1, source_target_pairs={{0,2},{1,3},{2,0},{3,1},{4,6},{5,7},{6,4},{7,5},{8,10},{9,11},{10,... | collective-permute-start | bytes 589832 | tf_op jit(solution)/shard_map/ppermute | solution.py:357
  6.8 2.5 %collective-permute-start.2 = (bf16[64,1536]{1,0:T(8,128)(2,1)S(1)}, bf16[64,1536]{1,0:T(8,128)(2,1)S(1)}, u32[]{:S(2)}, u32[]{:S(2)}) collective-permute-start(bf16[64,1536]{1,0:T(8,128)(2,1)S(1)} %get-tuple-element.45), channel_id=1, source_target_pairs={{0,4},{1,5},{2,6},{3,7},{4,0},{5,1},{6,2},{7,3},{8,12},{9,13},{10,... | collective-permute-start | bytes 589832 | tf_op jit(solution)/shard_map/ppermute | solution.py:357
  10.0 4.4 %copy-done = bf16[1408,4224]{1,0:T(8,128)(2,1)S(1)} copy-done((bf16[1408,4224]{1,0:T(8,128)(2,1)S(1)}, bf16[1408,4224]{1,0:T(8,128)(2,1)}, u32[]{:S(2)}) %copy-start) | copy-done | bytes 11894808
  15.6 3.7 %collective-permute-start.6 = (bf16[64,1408]{1,0:T(8,128)(2,1)S(1)}, bf16[64,1408]{1,0:T(8,128)(2,1)S(1)}, u32[]{:S(2)}, u32[]{:S(2)}) collective-permute-start(bf16[64,1408]{1,0:T(8,128)(2,1)S(1)} %get-tuple-element.56), channel_id=1, source_target_pairs={{0,4},{1,5},{2,6},{3,7},{4,0},{5,1},{6,2},{7,3},{8,12},{9,13},{10,... | collective-permute-start | bytes 540680 | tf_op jit(solution)/shard_map/ppermute | solution.py:357
  21.6 1.6 %collective-permute-start.12 = (bf16[1408,256]{1,0:T(8,128)(2,1)S(1)}, bf16[1408,256]{1,0:T(8,128)(2,1)S(1)}, u32[]{:S(2)}, u32[]{:S(2)}) collective-permute-start(bf16[1408,256]{1,0:T(8,128)(2,1)S(1)} %get-tuple-element.68), channel_id=1, source_target_pairs={{0,1},{1,0},{2,3},{3,2},{4,5},{5,4},{6,7},{7,6},{8,9},{9,8},{10,11... | collective-permute-start | bytes 2162696 | tf_op jit(solution)/shard_map/ppermute | solution.py:357
  23.2 4.6 %project.1 = (bf16[256,4352]{1,0:T(8,128)(2,1)S(1)}, f32[16,2,128,128]{3,2,1,0:T(8,128)S(1)}, bf16[16,2,128,128]{3,2,1,0:T(8,128)(2,1)S(1)}) custom-call(f32[128,128]{1,0:T(8,128)S(1)} %get-tuple-element.47.clip_ref, bf16[256,1408]{1,0:T(8,128)(2,1)S(1)} %get-tuple-element.48.normed_ref, bf16[1408,4224]{1,0:T(8,128)(2,1)S(1)} %load.1.refs_5_.wbuf.refs_9_), custom_call_target="tpu_custom_call" | custom-call | flops 5000000000 | bytes 40000000 | tf_op jit(solution)/shard_map/project/pallas_call | solution.py:456
  27.8 1.6 %collective-permute-done.7.refs_3_ = bf16[64,1408]{1,0:T(8,128)(2,1)S(1)} collective-permute-done((bf16[64,1408]{1,0:T(8,128)(2,1)S(1)}, bf16[64,1408]{1,0:T(8,128)(2,1)S(1)}, u32[]{:S(2)}, u32[]{:S(2)}) %collective-permute-start.7) | collective-permute-done | bytes 180256 | tf_op jit(solution)/shard_map/ppermute | solution.py:357
  30.2 1.7 %collective-permute-start.13 = (bf16[256,768]{1,0:T(8,128)(2,1)S(1)}, bf16[256,768]{1,0:T(8,128)(2,1)S(1)}, u32[]{:S(2)}, u32[]{:S(2)}) collective-permute-start(bf16[256,768]{1,0:T(8,128)(2,1)S(1)} %get-tuple-element.69), channel_id=1, source_target_pairs={{0,1},{1,0},{2,3},{3,2},{4,5},{5,4},{6,7},{7,6},{8,9},{9,8},{10,11... | collective-permute-start | bytes 1179656 | tf_op jit(solution)/shard_map/ppermute | solution.py:357
  33.9 1.7 %collective-permute-start.14 = (bf16[352,768]{1,0:T(8,128)(2,1)S(1)}, bf16[352,768]{1,0:T(8,128)(2,1)S(1)}, u32[]{:S(2)}, u32[]{:S(2)}) collective-permute-start(bf16[352,768]{1,0:T(8,128)(2,1)S(1)} %get-tuple-element.71), channel_id=1, source_target_pairs={{0,32},{1,9},{2,34},{3,11},{4,36},{5,13},{6,38},{7,15},{8,40},{9,1... | collective-permute-start | bytes 1622024 | tf_op jit(solution)/shard_map/ppermute | solution.py:365
  35.7 3.3 %collective-permute-start.15 = (bf16[352,768]{1,0:T(8,128)(2,1)S(1)}, bf16[352,768]{1,0:T(8,128)(2,1)S(1)}, u32[]{:S(2)}, u32[]{:S(2)}) collective-permute-start(bf16[352,768]{1,0:T(8,128)(2,1)S(1)} %get-tuple-element.72), channel_id=1, source_target_pairs={{0,64},{1,17},{2,66},{3,19},{4,68},{5,21},{6,70},{7,23},{8,72},{9,... | collective-permute-start | bytes 1622024 | tf_op jit(solution)/shard_map/ppermute | solution.py:365
  39.0 8.2 %input.1 = (bf16[64,1408]{1,0:T(8,128)(2,1)S(1)}, bf16[64,1408]{1,0:T(8,128)(2,1)S(1)}, bf16[64,1408]{1,0:T(8,128)(2,1)S(1)}, bf16[64,1408]{1,0:T(8,128)(2,1)S(1)}, f32[1,1408]{1,0:T(1,128)S(1)}) custom-call(bf16[64,1536]{1,0:T(8,128)(2,1)S(1)} %get-tuple-element.43.refs_0_, bf16[64,1536]{1,0:T(8,128)(2,1)S(1)} %collective-permute-done.1.refs_1_, ...), custom_call_target="tpu_custom_call" | custom-call | flops 6000000000 | bytes 20000000 | tf_op jit(solution)/shard_map/input/pallas_call | solution.py:500
  47.3 2.8 %collective-permute-done.17 = f32[1,1408]{1,0:T(1,128)S(1)} collective-permute-done((f32[1,1408]{1,0:T(1,128)S(1)}, f32[1,1408]{1,0:T(1,128)S(1)}, u32[]{:S(2)}, u32[]{:S(2)}) %collective-permute-start.17) | collective-permute-done | bytes 5664 | tf_op jit(solution)/shard_map/ppermute | solution.py:365
  50.1 2.8 %collective-permute-start.18 = (f32[1,1408]{1,0:T(1,128)S(1)}, f32[1,1408]{1,0:T(1,128)S(1)}, u32[]{:S(2)}, u32[]{:S(2)}) collective-permute-start(f32[1,1408]{1,0:T(1,128)S(1)} %add.3.refs_4_), channel_id=1, source_target_pairs={{0,96},{1,25},{2,98},{3,27},{4,100},{5,29},{6,102},{7,31},{8,104},... | collective-permute-start | bytes 16904 | tf_op jit(solution)/shard_map/ppermute | solution.py:365
  52.8 1.7 %collective-permute-done.18.refs_5_ = f32[1,1408]{1,0:T(1,128)S(1)} collective-permute-done((f32[1,1408]{1,0:T(1,128)S(1)}, f32[1,1408]{1,0:T(1,128)S(1)}, u32[]{:S(2)}, u32[]{:S(2)}) %collective-permute-start.18) | collective-permute-done | bytes 5664 | tf_op jit(solution)/shard_map/ppermute | solution.py:365
  54.5 2.1 %collective-permute-start.10 = (bf16[64,1408]{1,0:T(8,128)(2,1)S(1)}, bf16[64,1408]{1,0:T(8,128)(2,1)S(1)}, u32[]{:S(2)}, u32[]{:S(2)}) collective-permute-start(bf16[64,1408]{1,0:T(8,128)(2,1)S(1)} %get-tuple-element.63), channel_id=1, source_target_pairs={{0,6},{1,7},{2,4},{3,5},{4,2},{5,3},{6,0},{7,1},{8,14},{9,15},{10,... | collective-permute-start | bytes 540680 | tf_op jit(solution)/shard_map/ppermute | solution.py:357
  56.7 1.1 %second.1 = bf16[16,24,768]{2,1,0:T(8,128)(2,1)} custom-call(f32[352,768]{1,0:T(8,128)S(1)} %get-tuple-element.70.refs_0_, bf16[352,768]{1,0:T(8,128)(2,1)S(1)} %collective-permute-done.14.refs_1_, bf16[352,768]{1,0:T(8,128)(2,1)S(1)} %collective-permute-done.15.refs_2_, bf16[352,768]{1,0:T(8,128)(2,1)S(1)} %collective-permute-done.16.refs_3_, ...), custom_call_target="tpu_custom_call" | custom-call | bytes 5000000 | tf_op jit(solution)/shard_map/second/pallas_call | solution.py:518
  57.8 4.6 %all-to-all-start = ((bf16[16,24,768]{2,1,0:T(8,128)(2,1)}), bf16[16,24,768]{2,1,0:T(8,128)(2,1)S(1)}, u32[]{:S(2)}, u32[]{:S(2)}) async-start(bf16[16,24,768]{2,1,0:T(8,128)(2,1)} %second.1), calls=%async_computation | async-start | bytes 1179648 | tf_op jit(solution)/shard_map/all_to_all | solution.py:374
  62.4 2.8 %collective-permute-done.10.refs_3_ = bf16[64,1408]{1,0:T(8,128)(2,1)S(1)} collective-permute-done((bf16[64,1408]{1,0:T(8,128)(2,1)S(1)}, bf16[64,1408]{1,0:T(8,128)(2,1)S(1)}, u32[]{:S(2)}, u32[]{:S(2)}) %collective-permute-start.10) | collective-permute-done | bytes 180256 | tf_op jit(solution)/shard_map/ppermute | solution.py:357
  65.2 2.3 %collective-permute-start.11 = (bf16[4,32,1408]{2,1,0:T(8,128)(2,1)S(1)}, bf16[4,32,1408]{2,1,0:T(8,128)(2,1)S(1)}, u32[]{:S(2)}, u32[]{:S(2)}) collective-permute-start(bf16[4,32,1408]{2,1,0:T(8,128)(2,1)S(1)} %get-tuple-element.65), channel_id=1, source_target_pairs={{0,1},{1,0},{2,3},{3,2},{4,5},{5,4},{6,7},{7,6},{8,9},{9,8},{10,11... | collective-permute-start | bytes 1081352 | tf_op jit(solution)/shard_map/ppermute | solution.py:357
  67.5 4.2 %all-to-all-done.parts_ref = bf16[16,24,768]{2,1,0:T(8,128)(2,1)S(1)} async-done(((bf16[16,24,768]{2,1,0:T(8,128)(2,1)}), bf16[16,24,768]{2,1,0:T(8,128)(2,1)S(1)}, u32[]{:S(2)}, u32[]{:S(2)}) %all-to-all-start) | async-done | bytes 589856 | tf_op jit(solution)/shard_map/all_to_all | solution.py:374
  71.8 4.4 %collective-permute-start.19 = (f32[16,768]{1,0:T(8,128)S(1)}, f32[16,768]{1,0:T(8,128)S(1)}, u32[]{:S(2)}, u32[]{:S(2)}) collective-permute-start(f32[16,768]{1,0:T(8,128)S(1)} %get-tuple-element.76), channel_id=1, source_target_pairs={{0,1},{1,0},{2,3},{3,2},{4,5},{5,4},{6,7},{7,6},{8,9},{9,8},{10,11... | collective-permute-start | bytes 147464 | tf_op jit(solution)/shard_map/ppermute | solution.py:357
  (43 shorter events, 9.3 us)
Async XLA Ops:
  1.3 1.1 %copy-start.1 = (bf16[1,1,256,1408]{3,2,1,0:T(8,128)(2,1)S(1)}, bf16[1,1,256,1408]{3,2,1,0:T(8,128)(2,1)}, u32[]{:S(2)}) copy-start(bf16[1,1,256,1408]{3,2,1,0:T(8,128)(2,1)} %param.5) | copy-start | bytes 2162692
  2.5 2.9 %collective-permute-start = (bf16[4,32,1536]{2,1,0:T(8,128)(2,1)S(1)}, bf16[4,32,1536]{2,1,0:T(8,128)(2,1)S(1)}, u32[]{:S(2)}, u32[]{:S(2)}) collective-permute-start(bf16[4,32,1536]{2,1,0:T(8,128)(2,1)S(1)} %get-tuple-element.42), channel_id=1, source_target_pairs={{0,1},{1,0},{2,3},{3,2},{4,5},{5,4},{6,7},{7,6},{8,9},{9,8},{10,11... | collective-permute-start | bytes 1179656 | tf_op jit(solution)/shard_map/ppermute | solution.py:357
  4.0 1.1 %copy-start.2 = (bf16[1,1,256,1408]{3,2,1,0:T(8,128)(2,1)S(1)}, bf16[1,1,256,1408]{3,2,1,0:T(8,128)(2,1)}, u32[]{:S(2)}) copy-start(bf16[1,1,256,1408]{3,2,1,0:T(8,128)(2,1)} %param.9) | copy-start | bytes 2162692
  5.1 10.2 %collective-permute-start.4 = (bf16[4,32,1408]{2,1,0:T(8,128)(2,1)S(1)}, bf16[4,32,1408]{2,1,0:T(8,128)(2,1)S(1)}, u32[]{:S(2)}, u32[]{:S(2)}) collective-permute-start(bf16[4,32,1408]{2,1,0:T(8,128)(2,1)S(1)} %get-tuple-element.53), channel_id=1, source_target_pairs={{0,1},{1,0},{2,3},{3,2},{4,5},{5,4},{6,7},{7,6},{8,9},{9,8},{10,11... | collective-permute-start | bytes 1081352 | tf_op jit(solution)/shard_map/ppermute | solution.py:357
  5.4 13.9 %collective-permute-start.1 = (bf16[64,1536]{1,0:T(8,128)(2,1)S(1)}, bf16[64,1536]{1,0:T(8,128)(2,1)S(1)}, u32[]{:S(2)}, u32[]{:S(2)}) collective-permute-start(bf16[64,1536]{1,0:T(8,128)(2,1)S(1)} %get-tuple-element.44), channel_id=1, source_target_pairs={{0,2},{1,3},{2,0},{3,1},{4,6},{5,7},{6,4},{7,5},{8,10},{9,11},{10,... | collective-permute-start | bytes 589832 | tf_op jit(solution)/shard_map/ppermute | solution.py:357
  6.8 12.6 %collective-permute-start.2 = (bf16[64,1536]{1,0:T(8,128)(2,1)S(1)}, bf16[64,1536]{1,0:T(8,128)(2,1)S(1)}, u32[]{:S(2)}, u32[]{:S(2)}) collective-permute-start(bf16[64,1536]{1,0:T(8,128)(2,1)S(1)} %get-tuple-element.45), channel_id=1, source_target_pairs={{0,4},{1,5},{2,6},{3,7},{4,0},{5,1},{6,2},{7,3},{8,12},{9,13},{10,... | collective-permute-start | bytes 589832 | tf_op jit(solution)/shard_map/ppermute | solution.py:357
  9.2 11.2 %collective-permute-start.3 = (bf16[64,1536]{1,0:T(8,128)(2,1)S(1)}, bf16[64,1536]{1,0:T(8,128)(2,1)S(1)}, u32[]{:S(2)}, u32[]{:S(2)}) collective-permute-start(bf16[64,1536]{1,0:T(8,128)(2,1)S(1)} %get-tuple-element.46), channel_id=1, source_target_pairs={{0,6},{1,7},{2,4},{3,5},{4,2},{5,3},{6,0},{7,1},{8,14},{9,15},{10,... | collective-permute-start | bytes 589832 | tf_op jit(solution)/shard_map/ppermute | solution.py:357
  10.0 4.4 %copy-start = (bf16[1408,4224]{1,0:T(8,128)(2,1)S(1)}, bf16[1408,4224]{1,0:T(8,128)(2,1)}, u32[]{:S(2)}) copy-start(bf16[1408,4224]{1,0:T(8,128)(2,1)} %w_hbm.1) | copy-start | bytes 35684356
  15.4 12.3 %collective-permute-start.5 = (bf16[64,1408]{1,0:T(8,128)(2,1)S(1)}, bf16[64,1408]{1,0:T(8,128)(2,1)S(1)}, u32[]{:S(2)}, u32[]{:S(2)}) collective-permute-start(bf16[64,1408]{1,0:T(8,128)(2,1)S(1)} %get-tuple-element.55), channel_id=1, source_target_pairs={{0,2},{1,3},{2,0},{3,1},{4,6},{5,7},{6,4},{7,5},{8,10},{9,11},{10,... | collective-permute-start | bytes 540680 | tf_op jit(solution)/shard_map/ppermute | solution.py:357
  15.6 12.2 %collective-permute-start.6 = (bf16[64,1408]{1,0:T(8,128)(2,1)S(1)}, bf16[64,1408]{1,0:T(8,128)(2,1)S(1)}, u32[]{:S(2)}, u32[]{:S(2)}) collective-permute-start(bf16[64,1408]{1,0:T(8,128)(2,1)S(1)} %get-tuple-element.56), channel_id=1, source_target_pairs={{0,4},{1,5},{2,6},{3,7},{4,0},{5,1},{6,2},{7,3},{8,12},{9,13},{10,... | collective-permute-start | bytes 540680 | tf_op jit(solution)/shard_map/ppermute | solution.py:357
  19.3 10.1 %collective-permute-start.7 = (bf16[64,1408]{1,0:T(8,128)(2,1)S(1)}, bf16[64,1408]{1,0:T(8,128)(2,1)S(1)}, u32[]{:S(2)}, u32[]{:S(2)}) collective-permute-start(bf16[64,1408]{1,0:T(8,128)(2,1)S(1)} %get-tuple-element.57), channel_id=1, source_target_pairs={{0,6},{1,7},{2,4},{3,5},{4,2},{5,3},{6,0},{7,1},{8,14},{9,15},{10,... | collective-permute-start | bytes 540680 | tf_op jit(solution)/shard_map/ppermute | solution.py:357
  21.6 11.7 %collective-permute-start.12 = (bf16[1408,256]{1,0:T(8,128)(2,1)S(1)}, bf16[1408,256]{1,0:T(8,128)(2,1)S(1)}, u32[]{:S(2)}, u32[]{:S(2)}) collective-permute-start(bf16[1408,256]{1,0:T(8,128)(2,1)S(1)} %get-tuple-element.68), channel_id=1, source_target_pairs={{0,1},{1,0},{2,3},{3,2},{4,5},{5,4},{6,7},{7,6},{8,9},{9,8},{10,11... | collective-permute-start | bytes 2162696 | tf_op jit(solution)/shard_map/ppermute | solution.py:357
  30.2 3.0 %collective-permute-start.13 = (bf16[256,768]{1,0:T(8,128)(2,1)S(1)}, bf16[256,768]{1,0:T(8,128)(2,1)S(1)}, u32[]{:S(2)}, u32[]{:S(2)}) collective-permute-start(bf16[256,768]{1,0:T(8,128)(2,1)S(1)} %get-tuple-element.69), channel_id=1, source_target_pairs={{0,1},{1,0},{2,3},{3,2},{4,5},{5,4},{6,7},{7,6},{8,9},{9,8},{10,11... | collective-permute-start | bytes 1179656 | tf_op jit(solution)/shard_map/ppermute | solution.py:357
  33.9 20.6 %collective-permute-start.14 = (bf16[352,768]{1,0:T(8,128)(2,1)S(1)}, bf16[352,768]{1,0:T(8,128)(2,1)S(1)}, u32[]{:S(2)}, u32[]{:S(2)}) collective-permute-start(bf16[352,768]{1,0:T(8,128)(2,1)S(1)} %get-tuple-element.71), channel_id=1, source_target_pairs={{0,32},{1,9},{2,34},{3,11},{4,36},{5,13},{6,38},{7,15},{8,40},{9,1... | collective-permute-start | bytes 1622024 | tf_op jit(solution)/shard_map/ppermute | solution.py:365
  35.7 21.0 %collective-permute-start.15 = (bf16[352,768]{1,0:T(8,128)(2,1)S(1)}, bf16[352,768]{1,0:T(8,128)(2,1)S(1)}, u32[]{:S(2)}, u32[]{:S(2)}) collective-permute-start(bf16[352,768]{1,0:T(8,128)(2,1)S(1)} %get-tuple-element.72), channel_id=1, source_target_pairs={{0,64},{1,17},{2,66},{3,19},{4,68},{5,21},{6,70},{7,23},{8,72},{9,... | collective-permute-start | bytes 1622024 | tf_op jit(solution)/shard_map/ppermute | solution.py:365
  39.0 17.7 %collective-permute-start.16 = (bf16[352,768]{1,0:T(8,128)(2,1)S(1)}, bf16[352,768]{1,0:T(8,128)(2,1)S(1)}, u32[]{:S(2)}, u32[]{:S(2)}) collective-permute-start(bf16[352,768]{1,0:T(8,128)(2,1)S(1)} %get-tuple-element.73), channel_id=1, source_target_pairs={{0,96},{1,25},{2,98},{3,27},{4,100},{5,29},{6,102},{7,31},{8,104},... | collective-permute-start | bytes 1622024 | tf_op jit(solution)/shard_map/ppermute | solution.py:365
  47.2 2.8 %collective-permute-start.17 = (f32[1,1408]{1,0:T(1,128)S(1)}, f32[1,1408]{1,0:T(1,128)S(1)}, u32[]{:S(2)}, u32[]{:S(2)}) collective-permute-start(f32[1,1408]{1,0:T(1,128)S(1)} %get-tuple-element.74), channel_id=1, source_target_pairs={{0,32},{1,9},{2,34},{3,11},{4,36},{5,13},{6,38},{7,15},{8,40},{9,1... | collective-permute-start | bytes 16904 | tf_op jit(solution)/shard_map/ppermute | solution.py:365
  50.1 4.5 %collective-permute-start.18 = (f32[1,1408]{1,0:T(1,128)S(1)}, f32[1,1408]{1,0:T(1,128)S(1)}, u32[]{:S(2)}, u32[]{:S(2)}) collective-permute-start(f32[1,1408]{1,0:T(1,128)S(1)} %add.3.refs_4_), channel_id=1, source_target_pairs={{0,96},{1,25},{2,98},{3,27},{4,100},{5,29},{6,102},{7,31},{8,104},... | collective-permute-start | bytes 16904 | tf_op jit(solution)/shard_map/ppermute | solution.py:365
  52.8 9.6 %collective-permute-start.8 = (bf16[64,1408]{1,0:T(8,128)(2,1)S(1)}, bf16[64,1408]{1,0:T(8,128)(2,1)S(1)}, u32[]{:S(2)}, u32[]{:S(2)}) collective-permute-start(bf16[64,1408]{1,0:T(8,128)(2,1)S(1)} %get-tuple-element.61), channel_id=1, source_target_pairs={{0,2},{1,3},{2,0},{3,1},{4,6},{5,7},{6,4},{7,5},{8,10},{9,11},{10,... | collective-permute-start | bytes 540680 | tf_op jit(solution)/shard_map/ppermute | solution.py:357
  54.5 7.9 %collective-permute-start.9 = (bf16[64,1408]{1,0:T(8,128)(2,1)S(1)}, bf16[64,1408]{1,0:T(8,128)(2,1)S(1)}, u32[]{:S(2)}, u32[]{:S(2)}) collective-permute-start(bf16[64,1408]{1,0:T(8,128)(2,1)S(1)} %get-tuple-element.62), channel_id=1, source_target_pairs={{0,4},{1,5},{2,6},{3,7},{4,0},{5,1},{6,2},{7,3},{8,12},{9,13},{10,... | collective-permute-start | bytes 540680 | tf_op jit(solution)/shard_map/ppermute | solution.py:357
  54.5 10.6 %collective-permute-start.10 = (bf16[64,1408]{1,0:T(8,128)(2,1)S(1)}, bf16[64,1408]{1,0:T(8,128)(2,1)S(1)}, u32[]{:S(2)}, u32[]{:S(2)}) collective-permute-start(bf16[64,1408]{1,0:T(8,128)(2,1)S(1)} %get-tuple-element.63), channel_id=1, source_target_pairs={{0,6},{1,7},{2,4},{3,5},{4,2},{5,3},{6,0},{7,1},{8,14},{9,15},{10,... | collective-permute-start | bytes 540680 | tf_op jit(solution)/shard_map/ppermute | solution.py:357
  57.8 13.9 %all-to-all-start = ((bf16[16,24,768]{2,1,0:T(8,128)(2,1)}), bf16[16,24,768]{2,1,0:T(8,128)(2,1)S(1)}, u32[]{:S(2)}, u32[]{:S(2)}) async-start(bf16[16,24,768]{2,1,0:T(8,128)(2,1)} %second.1), calls=%async_computation | async-start | bytes 1179648 | tf_op jit(solution)/shard_map/all_to_all | solution.py:374
  65.2 10.9 %collective-permute-start.11 = (bf16[4,32,1408]{2,1,0:T(8,128)(2,1)S(1)}, bf16[4,32,1408]{2,1,0:T(8,128)(2,1)S(1)}, u32[]{:S(2)}, u32[]{:S(2)}) collective-permute-start(bf16[4,32,1408]{2,1,0:T(8,128)(2,1)S(1)} %get-tuple-element.65), channel_id=1, source_target_pairs={{0,1},{1,0},{2,3},{3,2},{4,5},{5,4},{6,7},{7,6},{8,9},{9,8},{10,11... | collective-permute-start | bytes 1081352 | tf_op jit(solution)/shard_map/ppermute | solution.py:357
  71.8 5.3 %collective-permute-start.19 = (f32[16,768]{1,0:T(8,128)S(1)}, f32[16,768]{1,0:T(8,128)S(1)}, u32[]{:S(2)}, u32[]{:S(2)}) collective-permute-start(f32[16,768]{1,0:T(8,128)S(1)} %get-tuple-element.76), channel_id=1, source_target_pairs={{0,1},{1,0},{2,3},{3,2},{4,5},{5,4},{6,7},{7,6},{8,9},{9,8},{10,11... | collective-permute-start | bytes 147464 | tf_op jit(solution)/shard_map/ppermute | solution.py:357
